TPU v7x, 32 devices: a whole 2x2x4 slice. The times are simulated.
32 devices in a mesh: seq: 4 (over y, x), dp: 8 (over z, core).
Axes of the slice: x: 2, y: 2, z: 4, core: 2. Of those that a mesh axis runs over, the one named last changes fastest.
Arguments:
- frames_in: bfloat16 [8, 4, 8, 320, 128], P('dp', 'seq'), may hold values from -6 to 6
- spatial_kernel: bfloat16 [9, 320, 320], P(None, 'seq'), may hold values from -0.109375 to 0.109375
- temporal_kernel: bfloat16 [3, 320, 320], P(None, 'seq'), may hold values from -0.1875 to 0.1875
- out_cotangent: bfloat16 [8, 4, 8, 320, 128], P('dp', 'seq'), may hold values from -6 to 6
Outputs:
- block_out: bfloat16 [8, 4, 8, 320, 128], P('dp', 'seq')
- input_grad: bfloat16 [8, 4, 8, 320, 128], P('dp', 'seq')
- spatial_grad: float32 [9, 320, 320], P(None, 'seq')
- temporal_grad: float32 [3, 320, 320], P(None, 'seq')
All inputs are finite; a program needn't handle non-finite values.
Results may differ from a plain program's by a relative error of at most 0.0055.
Values may be sent and summed in bfloat16 or wider, within the bound.
No kernel may reach another device: no remote copies, remote signals or barrier semaphores. Data moves between devices by JAX's collectives and lax.ppermute only.
A program may use at most 128 MiB of HBM per device.

v0:
```python
import math

import jax
import jax.numpy as jnp
from jax import lax
from jax.sharding import PartitionSpec as P


def pad_frames(values):
    return jnp.pad(values, ((0, 0), (1, 1), (0, 0), (0, 0), (0, 0)))


def pad_pixels(values):
    return jnp.pad(values, ((0, 0), (0, 0), (1, 1), (0, 0), (1, 1)))


def spatial_forward(frames, kernel):
    row_count = frames.shape[2]
    col_count = frames.shape[4]
    padded = pad_pixels(frames)
    running = jnp.zeros(frames.shape[:3] + (kernel.shape[1], col_count), jnp.float32)
    for offset_row in range(3):
        for offset_col in range(3):
            window = padded[
                :, :, offset_row : offset_row + row_count, :, offset_col : offset_col + col_count
            ]
            running = running + jnp.einsum(
                "oc,bfhcw->bfhow",
                kernel[3 * offset_row + offset_col],
                window,
                preferred_element_type=jnp.float32,
            )
    return running


def spatial_backward(pre_grad, kernel):
    row_count = pre_grad.shape[2]
    col_count = pre_grad.shape[4]
    padded = pad_pixels(pre_grad)
    running = jnp.zeros(pre_grad.shape[:3] + (kernel.shape[2], col_count), jnp.float32)
    for offset_row in range(3):
        for offset_col in range(3):
            window = padded[
                :,
                :,
                2 - offset_row : 2 - offset_row + row_count,
                :,
                2 - offset_col : 2 - offset_col + col_count,
            ]
            running = running + jnp.einsum(
                "oc,bfhow->bfhcw",
                kernel[3 * offset_row + offset_col],
                window,
                preferred_element_type=jnp.float32,
            )
    return running


def spatial_weight_grad(frames, pre_grad):
    row_count = frames.shape[2]
    col_count = frames.shape[4]
    padded = pad_pixels(frames)
    pieces = []
    for offset_row in range(3):
        for offset_col in range(3):
            window = padded[
                :, :, offset_row : offset_row + row_count, :, offset_col : offset_col + col_count
            ]
            pieces.append(
                jnp.einsum("bfhow,bfhcw->oc", pre_grad, window, preferred_element_type=jnp.float32)
            )
    return jnp.stack(pieces)


def temporal_forward(padded_act, kernel):
    frame_count = padded_act.shape[1] - 2
    running = jnp.zeros(
        padded_act.shape[:1]
        + (frame_count,)
        + padded_act.shape[2:3]
        + (kernel.shape[1], padded_act.shape[4]),
        jnp.float32,
    )
    for offset in range(3):
        running = running + jnp.einsum(
            "oc,bfhcw->bfhow",
            kernel[offset],
            padded_act[:, offset : offset + frame_count],
            preferred_element_type=jnp.float32,
        )
    return running


def temporal_backward(padded_cot, kernel):
    frame_count = padded_cot.shape[1] - 2
    running = jnp.zeros(
        padded_cot.shape[:1]
        + (frame_count,)
        + padded_cot.shape[2:3]
        + (kernel.shape[2], padded_cot.shape[4]),
        jnp.float32,
    )
    for offset in range(3):
        running = running + jnp.einsum(
            "oc,bfhow->bfhcw",
            kernel[offset],
            padded_cot[:, 2 - offset : 2 - offset + frame_count],
            preferred_element_type=jnp.float32,
        )
    return running


def temporal_weight_grad(cotangent, padded_act):
    frame_count = cotangent.shape[1]
    pieces = []
    for offset in range(3):
        pieces.append(
            jnp.einsum(
                "bfhow,bfhcw->oc",
                cotangent,
                padded_act[:, offset : offset + frame_count],
                preferred_element_type=jnp.float32,
            )
        )
    return jnp.stack(pieces)


def local(frames_in, spatial_kernel, temporal_kernel, out_cotangent):
    spatial_full, temporal_full = (
        lax.all_gather(spatial_kernel, "seq", axis=1, tiled=True),
        lax.all_gather(temporal_kernel, "seq", axis=1, tiled=True),
    )
    pre_act = lax.optimization_barrier(
        spatial_forward(frames_in, spatial_full).astype(jnp.bfloat16)
    )
    pre_wide = pre_act.astype(jnp.float32)
    activated = jax.nn.silu(pre_wide).astype(jnp.bfloat16)
    act_rows = lax.all_to_all(activated, "seq", split_axis=2, concat_axis=1, tiled=True)
    padded_act = pad_frames(act_rows)
    temporal_rows = temporal_forward(padded_act, temporal_full).astype(jnp.bfloat16)
    temporal = lax.all_to_all(temporal_rows, "seq", split_axis=1, concat_axis=2, tiled=True)
    cot_rows = lax.all_to_all(out_cotangent, "seq", split_axis=2, concat_axis=1, tiled=True)
    grad_rows = temporal_backward(pad_frames(cot_rows), temporal_full).astype(jnp.bfloat16)
    act_grad = lax.all_to_all(grad_rows, "seq", split_axis=1, concat_axis=2, tiled=True)
    temporal_part = temporal_weight_grad(cot_rows, padded_act)
    block_out = (frames_in.astype(jnp.float32) + temporal.astype(jnp.float32)).astype(jnp.bfloat16)
    sigmoid_value = jax.nn.sigmoid(pre_wide)
    pre_grad = (
        act_grad.astype(jnp.float32) * sigmoid_value * (1.0 + pre_wide * (1.0 - sigmoid_value))
    ).astype(jnp.bfloat16)
    spatial_part = spatial_weight_grad(frames_in, pre_grad)
    input_grad = (
        out_cotangent.astype(jnp.float32) + spatial_backward(pre_grad, spatial_full)
    ).astype(jnp.bfloat16)
    clip_total = lax.axis_size("dp") * frames_in.shape[0]
    frame_total = lax.axis_size("seq") * frames_in.shape[1]
    grad_scale = 1.0 / math.sqrt(clip_total * frame_total * frames_in.shape[2] * frames_in.shape[4])
    spatial_part = spatial_part * grad_scale
    temporal_part = temporal_part * grad_scale
    replica_terms = lax.psum((spatial_part, temporal_part), "dp")
    spatial_grad, temporal_grad = (
        lax.psum_scatter(replica_terms[0], "seq", scatter_dimension=1, tiled=True),
        lax.psum_scatter(replica_terms[1], "seq", scatter_dimension=1, tiled=True),
    )
    return (block_out, input_grad, spatial_grad, temporal_grad)


def solution(mesh):
    placed = (
        P("dp", "seq", None, None, None),
        P(None, "seq", None),
        P(None, "seq", None),
        P("dp", "seq", None, None, None),
    )
    return jax.shard_map(
        local,
        mesh=mesh,
        in_specs=placed,
        out_specs=(
            P("dp", "seq", None, None, None),
            P("dp", "seq", None, None, None),
            P(None, "seq", None),
            P(None, "seq", None),
        ),
        check_vma=False,
    )
```

profile of v0, /device:TPU:0, one launch (start us, length us, event | category | flops | bytes accessed | tf_op | source)
XLA Modules:
  0.0 256.1 jit_solution(7793992973254205204)
XLA Ops:
  7.9 5.2 %all-to-all-start.2 = ((bf16[1,1,8,320,128]{4,3,1,0,2:T(8,128)(2,1)}), bf16[1,1,8,320,128]{4,3,1,0,2:T(8,128)(2,1)S(1)}, u32[]{:S(2)}, u32[]{:S(2)}) async-start(bf16[1,1,8,320,128]{4,3,1,0,2:T(8,128)(2,1)} %bitcast.315), calls=%async_computation.2 | async-start | bytes 1310720 | tf_op jit(solution)/shard_map/all_to_all | solution.py:142
  13.1 21.4 %all_gather.7 = bf16[3,320,320]{2,1,0:T(8,128)(2,1)S(1)} all-gather(bf16[3,80,320]{2,1,0:T(8,128)(2,1)S(1)} %copy-done.5), channel_id=1, replica_groups=mesh['seq'=4,'dp'=8] {'seq'}, dimensions={1}, use_global_device_ids=true | all-gather | bytes 768000 | tf_op jit(solution)/shard_map/all_gather | solution.py:131
  35.6 1.4 fusion.16
  37.0 3.7 %all-to-all-start.3 = ((bf16[1,4,2,320,128]{4,3,2,0,1:T(8,128)(2,1)}), bf16[1,4,2,320,128]{4,3,2,0,1:T(8,128)(2,1)S(1)}, u32[]{:S(2)}, u32[]{:S(2)}) async-start(bf16[1,4,2,320,128]{4,3,2,0,1:T(8,128)(2,1)} %fusion.16), calls=%async_computation.3 | async-start | bytes 1310720 | tf_op jit(solution)/shard_map/all_to_all | solution.py:144
  40.7 19.8 %all-gather.2.cloned.1.call-done = bf16[9,320,320]{2,1,0:T(8,128)(2,1)} async-done(((bf16[9,80,320]{2,1,0:T(8,128)(2,1)}), bf16[9,320,320]{2,1,0:T(8,128)(2,1)}) %all-gather.2.cloned.1.call-update) | async-done | bytes 1843216 | tf_op jit(solution)/shard_map/all_gather | solution.py:130
  60.5 1.7 fusion.93
  66.2 1.4 fusion.15
  67.6 2.6 fusion.12
  70.2 3.5 %all-to-all-start = ((bf16[1,1,8,320,128]{4,3,1,0,2:T(8,128)(2,1)}), bf16[1,1,8,320,128]{4,3,1,0,2:T(8,128)(2,1)S(1)}, u32[]{:S(2)}, u32[]{:S(2)}) async-start(bf16[1,1,8,320,128]{4,3,1,0,2:T(8,128)(2,1)} %get-tuple-element.15), calls=%async_computation | async-start | bytes 1310720 | tf_op jit(solution)/shard_map/all_to_all | solution.py:138
  73.7 1.4 fusion.25
  75.1 8.4 %all-to-all-done = bf16[1,1,8,320,128]{4,3,1,0,2:T(8,128)(2,1)S(1)} async-done(((bf16[1,1,8,320,128]{4,3,1,0,2:T(8,128)(2,1)}), bf16[1,1,8,320,128]{4,3,1,0,2:T(8,128)(2,1)S(1)}, u32[]{:S(2)}, u32[]{:S(2)}) %all-to-all-start) | async-done | bytes 655392 | tf_op jit(solution)/shard_map/all_to_all | solution.py:138
  86.3 3.7 %copy.67 = f32[3,320,320]{2,0,1:T(4,128)} copy(f32[3,320,320]{1,2,0:T(8,128)} %maximum_multiply_fusion) | data formatting | bytes 2457600
  90.0 3.6 %reshape.267 = f32[320,960]{1,0:T(8,128)} reshape(f32[320,3,320]{2,1,0:T(4,128)} %bitcast.314) | data formatting | bytes 2457600
  93.9 1.3 fusion.24
  95.2 1.4 fusion.23
  96.6 1.4 fusion.22
  98.0 1.3 fusion.21
  99.3 1.4 fusion.20
  100.7 1.4 fusion.19
  103.4 1.4 fusion.17
  104.8 4.9 %broadcast_multiply_fusion = f32[9,320,320]{2,1,0:T(8,128)} fusion(f32[9,320,320]{2,1,0:T(8,128)} %fusion.17), kind=kLoop, calls=%fused_computation.16 | loop fusion | flops 921600 | bytes 7372800 | tf_op jit(solution)/shard_map/mul | solution.py:158
  109.7 1.7 fusion.43
  114.7 1.8 convolution_add_fusion.12
  117.4 1.3 fusion.14
  118.7 4.2 %all-to-all-start.1 = ((bf16[1,4,2,320,128]{4,3,2,0,1:T(8,128)(2,1)}), bf16[1,4,2,320,128]{4,3,2,0,1:T(8,128)(2,1)}, u32[]{:S(2)}, u32[]{:S(2)}) async-start(bf16[1,4,2,320,128]{4,3,2,0,1:T(8,128)(2,1)} %fusion.14), calls=%async_computation.1 | async-start | bytes 1310720 | tf_op jit(solution)/shard_map/all_to_all | solution.py:141
  125.2 55.4 %reduce-scatter.5.cloned.1.call-done = f32[9,80,320]{2,1,0:T(8,128)} async-done(((f32[9,320,320]{2,1,0:T(8,128)}), f32[9,80,320]{2,1,0:T(8,128)}) %reduce-scatter.5.cloned.1.call-update) | async-done | bytes 921616 | tf_op jit(solution)/shard_map/reduce_scatter | solution.py:162
  180.6 1.6 convolution_add_fusion.11
  182.2 2.5 fusion.5
  184.7 2.1 fusion.13
  186.8 58.5 %all-reduce.7.cloned.1.call-done = (f32[9,80,320]{2,1,0:T(8,128)}, f32[3,80,320]{1,2,0:T(8,128)}) async-done(((f32[9,80,320]{2,1,0:T(8,128)}, f32[3,80,320]{1,2,0:T(8,128)}), (f32[9,80,320]{2,1,0:T(8,128)}, f32[3,80,320]{1,2,0:T(8,128)})) %all-reduce.7.cloned.1.call-update) | async-done | bytes 1228816 | tf_op jit(solution)/shard_map/psum | solution.py:160
  245.2 2.0 copy.37
  247.2 2.3 copy.79
  (47 shorter events, 16.5 us)
Async XLA Ops:
  7.2 5.9 %copy-start.5 = (bf16[3,80,320]{2,1,0:T(8,128)(2,1)S(1)}, bf16[3,80,320]{2,1,0:T(8,128)(2,1)}, u32[]{:S(2)}) copy-start(bf16[3,80,320]{2,1,0:T(8,128)(2,1)} %param.6) | copy-start | bytes 460804
  7.2 53.3 %all-gather.2.cloned.1.call-start = ((), (), s32[]{:S(2)}) async-start(), calls=%async_computation.6 | async-start | bytes 2764800 | tf_op jit(solution)/shard_map/all_gather | solution.py:130
  7.9 26.6 %all-to-all-start.2 = ((bf16[1,1,8,320,128]{4,3,1,0,2:T(8,128)(2,1)}), bf16[1,1,8,320,128]{4,3,1,0,2:T(8,128)(2,1)S(1)}, u32[]{:S(2)}, u32[]{:S(2)}) async-start(bf16[1,1,8,320,128]{4,3,1,0,2:T(8,128)(2,1)} %bitcast.315), calls=%async_computation.2 | async-start | bytes 1310720 | tf_op jit(solution)/shard_map/all_to_all | solution.py:142
  37.0 23.5 %copy-start = (bf16[1,1,8,320,128]{4,3,2,1,0:T(8,128)(2,1)S(1)}, bf16[1,1,8,320,128]{4,3,2,1,0:T(8,128)(2,1)}, u32[]{:S(2)}) copy-start(bf16[1,1,8,320,128]{4,3,2,1,0:T(8,128)(2,1)} %param.4) | copy-start | bytes 1966084
  37.0 30.6 %all-to-all-start.3 = ((bf16[1,4,2,320,128]{4,3,2,0,1:T(8,128)(2,1)}), bf16[1,4,2,320,128]{4,3,2,0,1:T(8,128)(2,1)S(1)}, u32[]{:S(2)}, u32[]{:S(2)}) async-start(bf16[1,4,2,320,128]{4,3,2,0,1:T(8,128)(2,1)} %fusion.16), calls=%async_computation.3 | async-start | bytes 1310720 | tf_op jit(solution)/shard_map/all_to_all | solution.py:144
  60.5 1.7 copy-start.1
  70.2 13.3 %all-to-all-start = ((bf16[1,1,8,320,128]{4,3,1,0,2:T(8,128)(2,1)}), bf16[1,1,8,320,128]{4,3,1,0,2:T(8,128)(2,1)S(1)}, u32[]{:S(2)}, u32[]{:S(2)}) async-start(bf16[1,1,8,320,128]{4,3,1,0,2:T(8,128)(2,1)} %get-tuple-element.15), calls=%async_computation | async-start | bytes 1310720 | tf_op jit(solution)/shard_map/all_to_all | solution.py:138
  73.6 49.3 %reduce-scatter.7.cloned.1.call-start = ((), (), s32[]{:S(2)}) async-start(), calls=%async_computation.8 | async-start | bytes 1638400
  93.6 87.0 %reduce-scatter.5.cloned.1.call-start = ((), (), s32[]{:S(2)}) async-start(), calls=%async_computation.7 | async-start | bytes 5529600 | tf_op jit(solution)/shard_map/reduce_scatter | solution.py:162
  109.7 1.8 copy-start.2
  118.7 66.0 %all-to-all-start.1 = ((bf16[1,4,2,320,128]{4,3,2,0,1:T(8,128)(2,1)}), bf16[1,4,2,320,128]{4,3,2,0,1:T(8,128)(2,1)}, u32[]{:S(2)}, u32[]{:S(2)}) async-start(bf16[1,4,2,320,128]{4,3,2,0,1:T(8,128)(2,1)} %fusion.14), calls=%async_computation.1 | async-start | bytes 1310720 | tf_op jit(solution)/shard_map/all_to_all | solution.py:141
  122.9 122.4 %all-reduce.7.cloned.1.call-start = ((), (), s32[]{:S(2)}) async-start(), calls=%async_computation.9 | async-start | bytes 3194880 | tf_op jit(solution)/shard_map/psum | solution.py:160
  124.1 56.5 %copy-start.3 = (f32[8,128,320]{1,2,0:T(8,128)S(1)}, f32[8,128,320]{1,2,0:T(8,128)}, u32[]{:S(2)}) copy-start(f32[8,128,320]{1,2,0:T(8,128)} %convolution_add_fusion.12) | copy-start | bytes 3932164
  180.6 1.6 copy-start.4
Sparse Core Ops, SparseCore 0:
  9.9 50.5 all-gather.1
  93.8 29.1 reduce-scatter.6
  126.0 54.5 reduce-scatter.4
  183.5 61.7 all-reduce.6
where the time goes:
time: 257 us; the launch traced here: 256 us
  waiting for transfers between devices  143 us (56%)
  matrix products  36.3 us (14%)
  blocking collectives  21.4 us (8%)
  starting transfers between devices  16.9 us (7%)
  between operations  14 us (5%)
  local copies, waits for them, and re-layouts  13.8 us (5%)
  other arithmetic  10.8 us (4%)
    psum x1, waiting for transfers between devices, local(): replica_terms = lax.psum((spatial_part, temporal_part), 'dp')  58.5 us
    reduce_scatter x1, waiting for transfers between devices, local(): lax.psum_scatter(replica_terms[0], 'seq', scatter_dimension=1, tiled=True)  55.4 us
    all_gather x1, blocking collectives, local(): lax.all_gather(temporal_kernel, 'seq', axis=1, tiled=True)  21.4 us
    all_gather x1, waiting for transfers between devices, local(): lax.all_gather(spatial_kernel, 'seq', axis=1, tiled=True)  19.8 us
    unnamed x18, local copies, waits for them, and re-layouts  13.8 us
    dot_general x9, matrix products, spatial_weight_grad(): jnp.einsum('bfhow,bfhcw->oc', pre_grad, window, preferred_element_type=jn...  12.3 us
    dot_general x9, matrix products, spatial_backward(): jnp.einsum('oc,bfhow->bfhcw', kernel[3 * offset_row + offset_col], window...  10.7 us
    all_to_all x1, waiting for transfers between devices, local(): lax.all_to_all(activated, 'seq', split_axis=2, concat_axis=1, tiled=True)  8.4 us
  transfers between devices with their start and end apart: 8, of which 4 were waited for; matrix products, arithmetic and copies ran while one was open for 17% of the time, Pallas kernels for 0%

commit v1 on v0

v1 whole, which is shorter than its diff:
```python
import functools
import math

import jax
import jax.numpy as jnp
from jax import lax
from jax.experimental import pallas as pl
from jax.experimental.pallas import tpu as pltpu
from jax.sharding import PartitionSpec as P

BF = jnp.bfloat16
F32 = jnp.float32
VMEM_LIMIT = 56 * 1024 * 1024


def call(body, outs, scratch, flops, moved, *args):
    return pl.pallas_call(
        body,
        out_shape=outs,
        in_specs=[pl.BlockSpec(memory_space=pltpu.VMEM)] * len(args),
        out_specs=jax.tree.map(lambda _: pl.BlockSpec(memory_space=pltpu.VMEM), outs),
        scratch_shapes=scratch,
        compiler_params=pltpu.CompilerParams(vmem_limit_bytes=VMEM_LIMIT),
        cost_estimate=pl.CostEstimate(flops=flops, bytes_accessed=moved, transcendentals=0),
    )(*args)


def shape(dims, dtype=BF):
    return jax.ShapeDtypeStruct(tuple(dims), dtype)


def columns_of(first, count, width):
    return pl.ds(pl.multiple_of(first * width, width), count * width)


def shifted(block, step):
    if step == 0:
        return block
    width = block.shape[1]
    wide = block.astype(F32)
    rolled = pltpu.roll(wide, (-step) % width, 1)
    column = lax.broadcasted_iota(jnp.int32, block.shape, 1)
    edge = 0 if step < 0 else width - 1
    return jnp.where(column == edge, 0.0, rolled).astype(block.dtype)


def fill_taps(target, source, order):
    rows, chans, width = source.shape
    target[:, :width] = jnp.zeros((target.shape[0], width), target.dtype)
    target[:, (rows + 1) * width :] = jnp.zeros((target.shape[0], width), target.dtype)

    def row(y, carry):
        block = source[y]
        for b, step in enumerate(order):
            target[b * chans : (b + 1) * chans, columns_of(y + 1, 1, width)] = shifted(block, step)
        return carry

    lax.fori_loop(0, rows, row, 0)


def place_taps(target, tap, pieces, shard):
    me = lax.axis_index("seq")
    for j, piece in enumerate(pieces):
        at = pl.multiple_of(jnp.bitwise_xor(me, j) * shard, shard)
        target[tap, pl.ds(at, shard), :] = piece


def spatial_forward(frames, weights):
    rows, chans, width = frames.shape

    def body(frames_ref, weights_ref, pre_ref, act_ref, taps_ref):
        fill_taps(taps_ref, frames_ref, (-1, 0, 1))

        def tile(i, carry):
            total = jnp.zeros((chans, 2 * width), F32)
            for a in range(3):
                total += jnp.dot(
                    weights_ref[a],
                    taps_ref[:, columns_of(2 * i + a, 2, width)],
                    preferred_element_type=F32,
                )
            pre = total.astype(BF)
            wide = pre.astype(F32)
            act = (wide / (1.0 + jnp.exp(-wide))).astype(BF)
            for r in range(2):
                pre_ref[2 * i + r] = pre[:, r * width : (r + 1) * width]
                act_ref[2 * i + r] = act[:, r * width : (r + 1) * width]
            return carry

        lax.fori_loop(0, rows // 2, tile, 0)

    return call(
        body,
        (shape(frames.shape), shape(frames.shape)),
        [pltpu.VMEM((3 * chans, (rows + 2) * width), BF)],
        18 * chans * chans * rows * width,
        6 * frames.size + 18 * chans * chans,
        frames,
        weights,
    )


def spatial_weight_grad(frames, pre_act, act_grad, scale):
    rows, chans, width = frames.shape

    def body(frames_ref, pre_ref, grad_ref, pg_ref, out_ref, taps_ref, flat_ref):
        fill_taps(taps_ref, frames_ref, (-1, 0, 1))

        def row(y, carry):
            wide = pre_ref[y].astype(F32)
            s = 1.0 / (1.0 + jnp.exp(-wide))
            pg = (grad_ref[y].astype(F32) * s * (1.0 + wide * (1.0 - s))).astype(BF)
            pg_ref[y] = pg
            flat_ref[:, columns_of(y, 1, width)] = pg
            return carry

        lax.fori_loop(0, rows, row, 0)
        for a in range(3):
            out_ref[a] = (
                lax.dot_general(
                    flat_ref[...],
                    taps_ref[:, a * width : (a + rows) * width],
                    (((1,), (1,)), ((), ())),
                    preferred_element_type=F32,
                )
                * scale
            ).astype(out_ref.dtype)

    return call(
        body,
        (shape(frames.shape), shape((3, chans, 3 * chans), F32)),
        [
            pltpu.VMEM((3 * chans, (rows + 2) * width), BF),
            pltpu.VMEM((chans, rows * width), BF),
        ],
        18 * chans * chans * rows * width,
        8 * frames.size + 36 * chans * chans,
        frames,
        pre_act,
        act_grad,
    )


def spatial_backward(pre_grad, cotangent, weights_t):
    rows, chans, width = pre_grad.shape

    def body(pg_ref, cot_ref, weights_ref, out_ref, taps_ref):
        fill_taps(taps_ref, pg_ref, (1, 0, -1))

        def tile(i, carry):
            total = jnp.zeros((chans, 2 * width), F32)
            for a in range(3):
                total += jnp.dot(
                    weights_ref[a],
                    taps_ref[:, columns_of(2 * i + 2 - a, 2, width)],
                    preferred_element_type=F32,
                )
            for r in range(2):
                wide = cot_ref[2 * i + r].astype(F32)
                out_ref[2 * i + r] = (wide + total[:, r * width : (r + 1) * width]).astype(BF)
            return carry

        lax.fori_loop(0, rows // 2, tile, 0)

    return call(
        body,
        shape(pre_grad.shape),
        [pltpu.VMEM((3 * chans, (rows + 2) * width), BF)],
        18 * chans * chans * rows * width,
        6 * pre_grad.size + 18 * chans * chans,
        pre_grad,
        cotangent,
        weights_t,
    )


def temporal_apply(values, weights, forward):
    frames, rows, chans, width = values.shape
    span = rows * width

    def body(values_ref, weights_ref, out_ref, taps_ref):
        taps_ref[...] = jnp.zeros(taps_ref.shape, BF)
        for k in range(3):
            step = k - 1 if forward else 1 - k
            for f in range(frames):
                if 0 <= f - step < frames:
                    for y in range(rows):
                        at = (f - step) * span + y * width
                        taps_ref[k * chans : (k + 1) * chans, at : at + width] = values_ref[f, y]
        for f in range(frames):
            total = jnp.dot(
                weights_ref[...],
                taps_ref[:, f * span : (f + 1) * span],
                preferred_element_type=F32,
            ).astype(BF)
            for y in range(rows):
                out_ref[f, y] = total[:, y * width : (y + 1) * width]

    return call(
        body,
        shape(values.shape),
        [pltpu.VMEM((3 * chans, frames * span), BF)],
        6 * chans * values.size,
        4 * values.size + 6 * chans * chans,
        values,
        weights,
    )


def temporal_weight_grad(cotangent, activated, scale):
    frames, rows, chans, width = activated.shape
    span = rows * width

    def body(cot_ref, act_ref, out_ref, cot_flat, taps_ref):
        taps_ref[...] = jnp.zeros(taps_ref.shape, BF)
        for f in range(frames):
            for y in range(rows):
                at = f * span + y * width
                cot_flat[:, at : at + width] = cot_ref[f, y]
                for k in range(3):
                    if 0 <= f - k + 1 < frames:
                        to = at + (1 - k) * span
                        taps_ref[k * chans : (k + 1) * chans, to : to + width] = act_ref[f, y]
        out_ref[...] = (
            lax.dot_general(
                cot_flat[...],
                taps_ref[...],
                (((1,), (1,)), ((), ())),
                preferred_element_type=F32,
            )
            * scale
        ).astype(out_ref.dtype)

    return call(
        body,
        shape((chans, 3 * chans), F32),
        [
            pltpu.VMEM((chans, frames * span), BF),
            pltpu.VMEM((3 * chans, frames * span), BF),
        ],
        6 * chans * activated.size,
        4 * activated.size + 12 * chans * chans,
        cotangent,
        activated,
    )


def swap(values, axis, bit):
    size = lax.axis_size(axis)
    return lax.ppermute(values, axis, [(i, i ^ bit) for i in range(size)])


def gather_taps(shards):
    size = lax.axis_size("seq")
    taps, shard, chans = shards.shape
    half = taps // 2
    core = lax.axis_index("dp") % 2
    mine = lax.dynamic_slice_in_dim(shards, core * half, half, 0)
    got = jnp.stack([swap(mine, "seq", j) for j in range(1, size)])
    other = swap(got, "dp", 1)
    low = jnp.where(core == 0, got, other)
    high = jnp.where(core == 0, other, got)
    return jnp.concatenate([shards[None], jnp.concatenate([low, high], axis=1)])


def ordered(pieces):
    size, taps, shard, chans = pieces.shape
    me = lax.axis_index("seq")
    full = jnp.zeros((taps, size * shard, chans), pieces.dtype)
    for j in range(size):
        full = lax.dynamic_update_slice_in_dim(full, pieces[j], (me ^ j) * shard, 1)
    return full


def reduce_half(values, axis, bit, dim):
    mine = lax.axis_index(axis) // bit % 2
    kept = lax.dynamic_index_in_dim(values, mine, dim, keepdims=False)
    sent = lax.dynamic_index_in_dim(values, 1 - mine, dim, keepdims=False)
    return kept + swap(sent.astype(BF), axis, bit).astype(F32)


def join_half(values, axis, bit, dim):
    mine = lax.axis_index(axis) // bit % 2
    other = swap(values, axis, bit)
    return jnp.stack(
        [jnp.where(mine == 0, values, other), jnp.where(mine == 0, other, values)], dim
    )


def reduce_kernels(partial):
    seq = lax.axis_size("seq")
    dp = lax.axis_size("dp")
    groups, chans, width = partial.shape
    values = reduce_half(partial.reshape(2, groups // 2, chans, width), "dp", 1, 0)
    bits = [1 << i for i in range(seq.bit_length() - 1)]
    done = []
    for g in range(groups // 2):
        order = bits if g % 2 == 0 else bits[::-1]
        part = values[g].reshape([2] * len(bits) + [chans // seq, width])
        left = bits[::-1]
        for bit in order:
            at = left.index(bit)
            part = reduce_half(part, "seq", bit, at)
            left = [b for b in left if b != bit]
        done.append(part)
    part = jnp.stack(done)
    part = part.reshape((2, groups // 4) + part.shape[1:])
    part = reduce_half(part, "dp", 2, 0)
    bit = 4
    while bit < dp:
        part = part.astype(BF).astype(F32) + swap(part.astype(BF), "dp", bit).astype(F32)
        bit *= 2
    part = part.astype(BF)
    part = join_half(part, "dp", 2, 0).reshape((groups // 2,) + part.shape[1:])
    part = join_half(part, "dp", 1, 0).reshape((groups,) + part.shape[1:])
    return part


def local(frames_in, spatial_kernel, temporal_kernel, out_cotangent):
    frames, cotangent = frames_in[0, 0], out_cotangent[0, 0]
    rows, chans, width = frames.shape
    seq = lax.axis_size("seq")
    shard = spatial_kernel.shape[1]
    scale = 1.0 / math.sqrt(lax.axis_size("dp") * seq * rows * width)

    cot_rows = lax.all_to_all(
        cotangent.reshape(seq, rows // seq, chans, width), "seq", 0, 0, tiled=True
    )
    kernels = ordered(gather_taps(jnp.concatenate([temporal_kernel, spatial_kernel])))
    temporal_t = kernels[:3].transpose(2, 0, 1).reshape(chans, 3 * chans)
    temporal_w = kernels[:3].transpose(1, 0, 2).reshape(chans, 3 * chans)
    spatial = kernels[3:].reshape(3, 3, chans, chans)
    spatial_w = spatial.transpose(0, 2, 1, 3).reshape(3, chans, 3 * chans)
    spatial_t = spatial.transpose(0, 3, 1, 2).reshape(3, chans, 3 * chans)

    grad_rows = temporal_apply(cot_rows, temporal_t, False)
    act_grad = lax.all_to_all(grad_rows, "seq", 0, 0, tiled=True).reshape(frames.shape)
    pre_act, activated = spatial_forward(frames, spatial_w)
    act_rows = lax.all_to_all(
        activated.reshape(seq, rows // seq, chans, width), "seq", 0, 0, tiled=True
    )
    temporal_rows = temporal_apply(act_rows, temporal_w, True)
    temporal = lax.all_to_all(temporal_rows, "seq", 0, 0, tiled=True).reshape(frames.shape)
    temporal_part = temporal_weight_grad(cot_rows, act_rows, scale)
    pre_grad, spatial_part = spatial_weight_grad(frames, pre_act, act_grad, scale)
    input_grad = spatial_backward(pre_grad, cotangent, spatial_t)
    block_out = (frames.astype(F32) + temporal.astype(F32)).astype(BF)
    total = reduce_kernels(jnp.concatenate([spatial_part, temporal_part[None]])).astype(F32)
    total = total.reshape(4, shard, 3, chans).transpose(0, 2, 1, 3).reshape(12, shard, chans)
    return (block_out[None, None], input_grad[None, None], total[:9], total[9:])


def solution(mesh):
    placed = (
        P("dp", "seq", None, None, None),
        P(None, "seq", None),
        P(None, "seq", None),
        P("dp", "seq", None, None, None),
    )
    return jax.shard_map(
        local,
        mesh=mesh,
        in_specs=placed,
        out_specs=(
            P("dp", "seq", None, None, None),
            P("dp", "seq", None, None, None),
            P(None, "seq", None),
            P(None, "seq", None),
        ),
        check_vma=False,
    )
```

time: 257 us -> 148 us (0.58)
  waiting for transfers between devices: 143 us -> 47.2 us
  matrix products: 36.3 us -> 0 us
  Pallas kernels: 0 us -> 30.3 us
  blocking collectives: 21.4 us -> 0 us
  local copies, waits for them, and re-layouts: 13.8 us -> 27.3 us
  between operations: 14 us -> 1.03 us
  starting transfers between devices: 16.9 us -> 28.9 us
    psum x1 -> x0, waiting for transfers between devices: 58.5 us -> none  [local(): replica_terms = lax.psum((spatial_part, temporal_part), 'dp')]
    reduce_scatter x1 -> x0, waiting for transfers between devices: 55.4 us -> none  [local(): lax.psum_scatter(replica_terms[0], 'seq', scatter_dimension=1, tiled=True)]
    ppermute x0 -> x13, waiting for transfers between devices: none -> 40.9 us  [swap(): return lax.ppermute(values, axis, [(i, i ^ bit) for i in range(size)])]
    dot_general x36 -> x0, matrix products: 36.3 us -> none  [the longest x9 12.3 us: spatial_weight_grad(): jnp.einsum('bfhow,bfhcw->oc', pre_grad, window, preferred_element_type=jn...]
    pallas_call x0 -> x6, Pallas kernels: none -> 30.3 us  [call(): pl.pallas_call(body, out_shape=outs, in_specs=[pl.BlockSpec(memory_space=...]
    all_gather x1 -> x0, blocking collectives: 21.4 us -> none  [local(): lax.all_gather(temporal_kernel, 'seq', axis=1, tiled=True)]
    all_gather x1 -> x0, waiting for transfers between devices: 19.8 us -> none  [local(): lax.all_gather(spatial_kernel, 'seq', axis=1, tiled=True)]
    ppermute x0 -> x13, starting transfers between devices: none -> 14.3 us  [swap(): return lax.ppermute(values, axis, [(i, i ^ bit) for i in range(size)])]
  transfers between devices with their start and end apart: 8 -> 17, of which waited for: 4 -> 12; matrix products, arithmetic and copies ran while one was open for 17% -> 14% of each run, Pallas kernels for 0% -> 16%
where the time goes in v1:
time: 148 us
  waiting for transfers between devices  47.2 us (32%)
  Pallas kernels  30.3 us (20%)
  starting transfers between devices  28.9 us (20%)
  local copies, waits for them, and re-layouts  27.3 us (18%)
  other arithmetic  12.9 us (9%)
    ppermute x13, waiting for transfers between devices, swap(): return lax.ppermute(values, axis, [(i, i ^ bit) for i in range(size)])  40.9 us
    pallas_call x6, Pallas kernels, call(): pl.pallas_call(body, out_shape=outs, in_specs=[pl.BlockSpec(memory_space=...  30.3 us
    ppermute x13, starting transfers between devices, swap(): return lax.ppermute(values, axis, [(i, i ^ bit) for i in range(size)])  14.3 us
    unnamed x15, local copies, waits for them, and re-layouts  7.61 us
    all_to_all x1, starting transfers between devices, local(): lax.all_to_all(activated.reshape(seq, rows // seq, chans, width), 'seq',...  4.16 us
    reshape x1, local copies, waits for them, and re-layouts, local(): spatial_w = spatial.transpose(0, 2, 1, 3).reshape(3, chans, 3 * chans)  4.06 us
    all_to_all x1, waiting for transfers between devices, local(): lax.all_to_all(cotangent.reshape(seq, rows // seq, chans, width), 'seq',...  4 us
    add x3, other arithmetic, reduce_half(): return kept + swap(sent.astype(BF), axis, bit).astype(F32)  3.89 us
  transfers between devices with their start and end apart: 17, of which 12 were waited for; matrix products, arithmetic and copies ran while one was open for 14% of the time, Pallas kernels for 16%

profile of v1, /device:TPU:0, one launch (start us, length us, event | category | flops | bytes accessed | tf_op | source)
XLA Modules:
  0.0 147.5 jit_solution(4785863098015502765)
XLA Ops:
  2.8 4.0 %collective-permute-start.2 = (bf16[6,80,320]{2,1,0:T(8,128)(2,1)S(1)}, bf16[6,80,320]{2,1,0:T(8,128)(2,1)S(1)}, u32[]{:S(2)}, u32[]{:S(2)}) collective-permute-start(bf16[6,80,320]{2,1,0:T(8,128)(2,1)S(1)} %constant_dynamic-slice_fusion), channel_id=1, source_target_pairs={{0,24},{8,16},{16,8},{24,0},{1,25},{9,17},{17,9},{25,1},{2,26},{10... | collective-permute-start | bytes 921608 | tf_op jit(solution)/shard_map/ppermute | solution.py:250
  7.4 8.8 %collective-permute-done.2 = bf16[6,80,320]{2,1,0:T(8,128)(2,1)S(1)} collective-permute-done((bf16[6,80,320]{2,1,0:T(8,128)(2,1)S(1)}, bf16[6,80,320]{2,1,0:T(8,128)(2,1)S(1)}, u32[]{:S(2)}, u32[]{:S(2)}) %collective-permute-start.2) | collective-permute-done | bytes 307232 | tf_op jit(solution)/shard_map/ppermute | solution.py:250
  16.2 7.0 %collective-permute-done.1 = bf16[6,80,320]{2,1,0:T(8,128)(2,1)S(1)} collective-permute-done((bf16[6,80,320]{2,1,0:T(8,128)(2,1)S(1)}, bf16[6,80,320]{2,1,0:T(8,128)(2,1)S(1)}, u32[]{:S(2)}, u32[]{:S(2)}) %collective-permute-start.1) | collective-permute-done | bytes 307232 | tf_op jit(solution)/shard_map/ppermute | solution.py:250
  24.8 3.5 %all-to-all-start.2 = ((bf16[4,2,320,128]{3,2,1,0:T(8,128)(2,1)}), bf16[4,2,320,128]{3,2,1,0:T(8,128)(2,1)S(1)}, u32[]{:S(2)}, u32[]{:S(2)}) async-start(bf16[4,2,320,128]{3,2,1,0:T(8,128)(2,1)} %bitcast.112), calls=%async_computation.2 | async-start | bytes 1310720 | tf_op jit(solution)/shard_map/all_to_all | solution.py:326
  28.8 1.6 %broadcast_select_fusion = (bf16[3,6,80,320]{3,2,1,0:T(8,128)(2,1)S(1)}, bf16[3,6,80,320]{3,2,1,0:T(8,128)(2,1)S(1)}) fusion(bf16[3,6,80,320]{3,2,1,0:T(8,128)(2,1)} %collective-permute-done.3, pred[]{:T(512)S(6)} %eq.20, bf16[1,6,80,320]{3,2,1,0:T(8,128)(2,1)S(1)} %bitcast.106, bf16[1,6,80,320]{3,2,1,0:T(8,128)(2,1)S(1)} %bitcast.108, ...), kind=kLoop, calls=%fused_computation.12 | loop fusion | flops 1843200 | bytes 3686401 | tf_op jit(solution)/shard_map/jit(_where)/select_n | solution.py:262
  30.9 1.6 %copy-done.1 = bf16[12,320,320]{2,1,0:T(8,128)(2,1)} copy-done((bf16[12,320,320]{2,1,0:T(8,128)(2,1)}, bf16[12,320,320]{2,1,0:T(8,128)(2,1)S(1)}, u32[]{:S(2)}) %copy-start.1) | copy-done | bytes 2457624
  34.6 4.0 %all-to-all-done.2.values_ref.cot_ref = bf16[4,2,320,128]{3,2,1,0:T(8,128)(2,1)S(1)} async-done(((bf16[4,2,320,128]{3,2,1,0:T(8,128)(2,1)}), bf16[4,2,320,128]{3,2,1,0:T(8,128)(2,1)S(1)}, u32[]{:S(2)}, u32[]{:S(2)}) %all-to-all-start.2) | async-done | bytes 655392 | tf_op jit(solution)/shard_map/all_to_all | solution.py:326
  39.5 3.1 %shard_map.77 = bf16[4,2,320,128]{3,2,1,0:T(8,128)(2,1)} custom-call(bf16[4,2,320,128]{3,2,1,0:T(8,128)(2,1)} %copy-done.4, bf16[320,960]{1,0:T(8,128)(2,1)} %copy.19.weights_ref), custom_call_target="tpu_custom_call" | custom-call | flops 629145600 | bytes 1925120 | tf_op jit(solution)/shard_map/pallas_call | solution.py:17
  42.6 3.5 %all-to-all-start.3 = ((bf16[4,2,320,128]{3,2,1,0:T(8,128)(2,1)}), bf16[4,2,320,128]{3,2,1,0:T(8,128)(2,1)S(1)}, u32[]{:S(2)}, u32[]{:S(2)}) async-start(bf16[4,2,320,128]{3,2,1,0:T(8,128)(2,1)} %shard_map.77), calls=%async_computation.3 | async-start | bytes 1310720 | tf_op jit(solution)/shard_map/all_to_all | solution.py:337
  46.1 1.9 %slice.61 = bf16[9,320,320]{2,1,0:T(8,128)(2,1)S(1)} slice(bf16[12,320,320]{2,1,0:T(8,128)(2,1)} %copy-done.1), slice={[3:12], [0:320], [0:320]} | slice | bytes 3686400 | tf_op jit(solution)/shard_map/slice | solution.py:332
  48.0 2.5 %copy.15 = bf16[3,320,3,320]{1,3,2,0:T(8,128)(2,1)} copy(bf16[3,320,3,320]{3,1,2,0:T(8,128)(2,1)S(1)} %bitcast.92) | data formatting | bytes 3686400 | tf_op jit(solution)/shard_map/transpose | solution.py:333
  50.5 4.1 %copy.16.weights_ref = bf16[3,320,960]{2,1,0:T(8,128)(2,1)} copy(bf16[3,320,960]{1,2,0:T(8,128)(2,1)} %bitcast.96) | data formatting | bytes 3686400 | tf_op jit(solution)/shard_map/reshape | solution.py:333
  54.5 6.7 %shard_map.75 = (bf16[8,320,128]{2,1,0:T(8,128)(2,1)}, bf16[8,320,128]{2,1,0:T(8,128)(2,1)}) custom-call(bf16[8,320,128]{2,1,0:T(8,128)(2,1)} %bitcast.116, bf16[3,320,960]{2,1,0:T(8,128)(2,1)} %copy.16.weights_ref), custom_call_target="tpu_custom_call" | custom-call | flops 1887436800 | bytes 3809280 | tf_op jit(solution)/shard_map/pallas_call | solution.py:17
  61.3 4.2 %all-to-all-start = ((bf16[4,2,320,128]{3,2,1,0:T(8,128)(2,1)}), bf16[4,2,320,128]{3,2,1,0:T(8,128)(2,1)S(1)}, u32[]{:S(2)}, u32[]{:S(2)}) async-start(bf16[4,2,320,128]{3,2,1,0:T(8,128)(2,1)} %bitcast.115), calls=%async_computation | async-start | bytes 1310720 | tf_op jit(solution)/shard_map/all_to_all | solution.py:339
  65.4 7.2 %shard_map.78 = (bf16[8,320,128]{2,1,0:T(8,128)(2,1)}, f32[3,320,960]{2,1,0:T(8,128)}) custom-call(bf16[8,320,128]{2,1,0:T(8,128)(2,1)} %bitcast.117, bf16[8,320,128]{2,1,0:T(8,128)(2,1)} %get-tuple-element.9.pre_ref, bf16[8,320,128]{2,1,0:T(8,128)(2,1)} %bitcast.114), custom_call_target="tpu_custom_call" | custom-call | flops 1887436800 | bytes 6307840 | tf_op jit(solution)/shard_map/pallas_call | solution.py:17
  72.7 1.8 %all-to-all-done.values_ref.act_ref = bf16[4,2,320,128]{3,2,1,0:T(8,128)(2,1)S(1)} async-done(((bf16[4,2,320,128]{3,2,1,0:T(8,128)(2,1)}), bf16[4,2,320,128]{3,2,1,0:T(8,128)(2,1)S(1)}, u32[]{:S(2)}, u32[]{:S(2)}) %all-to-all-start) | async-done | bytes 655392 | tf_op jit(solution)/shard_map/all_to_all | solution.py:339
  75.3 3.4 %shard_map.80 = f32[320,960]{1,0:T(8,128)} custom-call(bf16[4,2,320,128]{3,2,1,0:T(8,128)(2,1)} %copy-done.4, bf16[4,2,320,128]{3,2,1,0:T(8,128)(2,1)} %copy-done.3), custom_call_target="tpu_custom_call" | custom-call | flops 629145600 | bytes 2539520 | tf_op jit(solution)/shard_map/pallas_call | solution.py:17
  78.7 3.1 %pad_maximum_fusion = f32[4,320,960]{2,1,0:T(8,128)S(1)} fusion(f32[1,320,960]{2,1,0:T(8,128)} %bitcast.97, f32[3,320,960]{2,1,0:T(8,128)} %get-tuple-element.11), kind=kLoop, calls=%fused_computation | loop fusion | flops 1228800 | bytes 9830400 | tf_op jit(solution)/shard_map/concatenate | solution.py:348
  81.9 2.3 %copy-done = f32[4,320,960]{2,1,0:T(8,128)} copy-done((f32[4,320,960]{2,1,0:T(8,128)}, f32[4,320,960]{2,1,0:T(8,128)S(1)}, u32[]{:S(2)}) %copy-start) | copy-done | bytes 4915224
  84.5 3.1 %collective-permute-done.4 = bf16[2,320,960]{2,1,0:T(8,128)(2,1)} collective-permute-done((bf16[2,320,960]{2,1,0:T(8,128)(2,1)S(1)}, bf16[2,320,960]{2,1,0:T(8,128)(2,1)}, u32[]{:S(2)}, u32[]{:S(2)}) %collective-permute-start.4) | collective-permute-done | bytes 1228832 | tf_op jit(solution)/shard_map/ppermute | solution.py:250
  87.6 2.5 %bitcast_add_fusion = f32[2,320,960]{2,1,0:T(8,128)S(1)} fusion(bf16[2,320,960]{2,1,0:T(8,128)(2,1)} %collective-permute-done.4, f32[2,2,320,960]{3,2,1,0:T(8,128)} %bitcast.95, s32[]{:T(128)S(6)} %select_n.139), kind=kLoop, calls=%fused_computation.1 | loop fusion | flops 1228800 | bytes 6144004 | tf_op jit(solution)/shard_map/add | solution.py:279
  94.4 8.0 %collective-permute-done.5 = bf16[2,80,960]{2,1,0:T(8,128)(2,1)} collective-permute-done((bf16[2,80,960]{2,1,0:T(8,128)(2,1)}, bf16[2,80,960]{2,1,0:T(8,128)(2,1)}, u32[]{:S(2)}, u32[]{:S(2)}) %collective-permute-start.5) | collective-permute-done | bytes 307232 | tf_op jit(solution)/shard_map/ppermute | solution.py:250
  103.7 1.5 %collective-permute-start.6 = (bf16[80,960]{1,0:T(8,128)(2,1)S(1)}, bf16[80,960]{1,0:T(8,128)(2,1)S(1)}, u32[]{:S(2)}, u32[]{:S(2)}) collective-permute-start(bf16[80,960]{1,0:T(8,128)(2,1)S(1)} %fusion.19), channel_id=1, source_target_pairs={{0,16},{8,24},{16,0},{24,8},{1,17},{9,25},{17,1},{25,9},{2,18},{10... | collective-permute-start | bytes 460808 | tf_op jit(solution)/shard_map/ppermute | solution.py:250
  105.9 3.2 %collective-permute-done.6 = bf16[80,960]{1,0:T(8,128)(2,1)S(1)} collective-permute-done((bf16[80,960]{1,0:T(8,128)(2,1)S(1)}, bf16[80,960]{1,0:T(8,128)(2,1)S(1)}, u32[]{:S(2)}, u32[]{:S(2)}) %collective-permute-start.6) | collective-permute-done | bytes 153632 | tf_op jit(solution)/shard_map/ppermute | solution.py:250
  110.8 1.6 %collective-permute-start.9 = (bf16[1,80,960]{2,1,0:T(8,128)(2,1)S(1)}, bf16[1,80,960]{2,1,0:T(8,128)(2,1)S(1)}, u32[]{:S(2)}, u32[]{:S(2)}) collective-permute-start(bf16[1,80,960]{2,1,0:T(8,128)(2,1)S(1)} %fusion.13), channel_id=1, source_target_pairs={{0,2},{1,3},{2,0},{3,1},{4,6},{5,7},{6,4},{7,5},{8,10},{9,11},{10,... | collective-permute-start | bytes 460808 | tf_op jit(solution)/shard_map/ppermute | solution.py:250
  112.5 3.7 %collective-permute-done.9 = bf16[1,80,960]{2,1,0:T(8,128)(2,1)S(1)} collective-permute-done((bf16[1,80,960]{2,1,0:T(8,128)(2,1)S(1)}, bf16[1,80,960]{2,1,0:T(8,128)(2,1)S(1)}, u32[]{:S(2)}, u32[]{:S(2)}) %collective-permute-start.9) | collective-permute-done | bytes 153632 | tf_op jit(solution)/shard_map/ppermute | solution.py:250
  116.3 2.9 %collective-permute-start.10 = (bf16[1,80,960]{2,1,0:T(8,128)(2,1)S(1)}, bf16[1,80,960]{2,1,0:T(8,128)(2,1)S(1)}, u32[]{:S(2)}, u32[]{:S(2)}) collective-permute-start(bf16[1,80,960]{2,1,0:T(8,128)(2,1)S(1)} %fusion.16), channel_id=1, source_target_pairs={{0,4},{1,5},{2,6},{3,7},{4,0},{5,1},{6,2},{7,3},{8,12},{9,13},{10,... | collective-permute-start | bytes 460808 | tf_op jit(solution)/shard_map/ppermute | solution.py:250
  119.2 5.2 %collective-permute-done.10 = bf16[1,80,960]{2,1,0:T(8,128)(2,1)S(1)} collective-permute-done((bf16[1,80,960]{2,1,0:T(8,128)(2,1)S(1)}, bf16[1,80,960]{2,1,0:T(8,128)(2,1)S(1)}, u32[]{:S(2)}, u32[]{:S(2)}) %collective-permute-start.10) | collective-permute-done | bytes 153632 | tf_op jit(solution)/shard_map/ppermute | solution.py:250
  127.8 2.3 %copy.20.weights_ref = bf16[3,320,960]{2,1,0:T(8,128)(2,1)} copy(bf16[3,320,960]{1,2,0:T(8,128)(2,1)S(1)} %bitcast.93) | data formatting | bytes 3686400 | tf_op jit(solution)/shard_map/reshape | solution.py:334
  130.2 3.1 %shard_map.76 = bf16[4,2,320,128]{3,2,1,0:T(8,128)(2,1)} custom-call(bf16[4,2,320,128]{3,2,1,0:T(8,128)(2,1)} %copy-done.3, bf16[320,960]{1,0:T(8,128)(2,1)} %copy.18.weights_ref), custom_call_target="tpu_custom_call" | custom-call | flops 629145600 | bytes 1925120 | tf_op jit(solution)/shard_map/pallas_call | solution.py:17
  133.3 3.5 %all-to-all-start.1 = ((bf16[4,2,320,128]{3,2,1,0:T(8,128)(2,1)}), bf16[4,2,320,128]{3,2,1,0:T(8,128)(2,1)S(1)}, u32[]{:S(2)}, u32[]{:S(2)}) async-start(bf16[4,2,320,128]{3,2,1,0:T(8,128)(2,1)} %shard_map.76), calls=%async_computation.1 | async-start | bytes 1310720 | tf_op jit(solution)/shard_map/all_to_all | solution.py:343
  136.9 6.6 %shard_map.79 = bf16[8,320,128]{2,1,0:T(8,128)(2,1)} custom-call(bf16[8,320,128]{2,1,0:T(8,128)(2,1)} %get-tuple-element.10.pg_ref, bf16[8,320,128]{2,1,0:T(8,128)(2,1)} %bitcast.113, bf16[3,320,960]{2,1,0:T(8,128)(2,1)} %copy.20.weights_ref), custom_call_target="tpu_custom_call" | custom-call | flops 1887436800 | bytes 3809280 | tf_op jit(solution)/shard_map/pallas_call | solution.py:17
  (65 shorter events, 24.7 us)
Async XLA Ops:
  2.8 13.4 %collective-permute-start.2 = (bf16[6,80,320]{2,1,0:T(8,128)(2,1)S(1)}, bf16[6,80,320]{2,1,0:T(8,128)(2,1)S(1)}, u32[]{:S(2)}, u32[]{:S(2)}) collective-permute-start(bf16[6,80,320]{2,1,0:T(8,128)(2,1)S(1)} %constant_dynamic-slice_fusion), channel_id=1, source_target_pairs={{0,24},{8,16},{16,8},{24,0},{1,25},{9,17},{17,9},{25,1},{2,26},{10... | collective-permute-start | bytes 921608 | tf_op jit(solution)/shard_map/ppermute | solution.py:250
  6.8 16.5 %collective-permute-start.1 = (bf16[6,80,320]{2,1,0:T(8,128)(2,1)S(1)}, bf16[6,80,320]{2,1,0:T(8,128)(2,1)S(1)}, u32[]{:S(2)}, u32[]{:S(2)}) collective-permute-start(bf16[6,80,320]{2,1,0:T(8,128)(2,1)S(1)} %constant_dynamic-slice_fusion), channel_id=1, source_target_pairs={{0,16},{8,24},{16,0},{24,8},{1,17},{9,25},{17,1},{25,9},{2,18},{10... | collective-permute-start | bytes 921608 | tf_op jit(solution)/shard_map/ppermute | solution.py:250
  7.3 16.3 %collective-permute-start = (bf16[6,80,320]{2,1,0:T(8,128)(2,1)S(1)}, bf16[6,80,320]{2,1,0:T(8,128)(2,1)S(1)}, u32[]{:S(2)}, u32[]{:S(2)}) collective-permute-start(bf16[6,80,320]{2,1,0:T(8,128)(2,1)S(1)} %constant_dynamic-slice_fusion), channel_id=1, source_target_pairs={{0,8},{8,0},{16,24},{24,16},{1,9},{9,1},{17,25},{25,17},{2,10},{10... | collective-permute-start | bytes 921608 | tf_op jit(solution)/shard_map/ppermute | solution.py:250
  24.8 4.0 %collective-permute-start.3 = (bf16[3,6,80,320]{3,2,1,0:T(8,128)(2,1)}, bf16[3,6,80,320]{3,2,1,0:T(8,128)(2,1)}, u32[]{:S(2)}, u32[]{:S(2)}) collective-permute-start(bf16[3,6,80,320]{3,2,1,0:T(8,128)(2,1)} %pad_maximum_fusion.2), channel_id=1, source_target_pairs={{0,1},{1,0},{2,3},{3,2},{4,5},{5,4},{6,7},{7,6},{8,9},{9,8},{10,11... | collective-permute-start | bytes 2764808 | tf_op jit(solution)/shard_map/ppermute | solution.py:250
  24.8 13.8 %all-to-all-start.2 = ((bf16[4,2,320,128]{3,2,1,0:T(8,128)(2,1)}), bf16[4,2,320,128]{3,2,1,0:T(8,128)(2,1)S(1)}, u32[]{:S(2)}, u32[]{:S(2)}) async-start(bf16[4,2,320,128]{3,2,1,0:T(8,128)(2,1)} %bitcast.112), calls=%async_computation.2 | async-start | bytes 1310720 | tf_op jit(solution)/shard_map/all_to_all | solution.py:326
  30.9 1.6 %copy-start.1 = (bf16[12,320,320]{2,1,0:T(8,128)(2,1)}, bf16[12,320,320]{2,1,0:T(8,128)(2,1)S(1)}, u32[]{:S(2)}) copy-start(bf16[12,320,320]{2,1,0:T(8,128)(2,1)S(1)} %fusion.9) | copy-start | bytes 7372804
  38.6 0.8 copy-start.4
  42.6 18.6 %all-to-all-start.3 = ((bf16[4,2,320,128]{3,2,1,0:T(8,128)(2,1)}), bf16[4,2,320,128]{3,2,1,0:T(8,128)(2,1)S(1)}, u32[]{:S(2)}, u32[]{:S(2)}) async-start(bf16[4,2,320,128]{3,2,1,0:T(8,128)(2,1)} %shard_map.77), calls=%async_computation.3 | async-start | bytes 1310720 | tf_op jit(solution)/shard_map/all_to_all | solution.py:337
  61.3 4.2 %copy-start.5 = (bf16[4,2,320,128]{3,2,1,0:T(8,128)(2,1)}, bf16[4,2,320,128]{3,2,1,0:T(8,128)(2,1)S(1)}, u32[]{:S(2)}) copy-start(bf16[4,2,320,128]{3,2,1,0:T(8,128)(2,1)S(1)} %all-to-all-done.3) | copy-start | bytes 1966084
  61.3 13.2 %all-to-all-start = ((bf16[4,2,320,128]{3,2,1,0:T(8,128)(2,1)}), bf16[4,2,320,128]{3,2,1,0:T(8,128)(2,1)S(1)}, u32[]{:S(2)}, u32[]{:S(2)}) async-start(bf16[4,2,320,128]{3,2,1,0:T(8,128)(2,1)} %bitcast.115), calls=%async_computation | async-start | bytes 1310720 | tf_op jit(solution)/shard_map/all_to_all | solution.py:339
  74.4 0.8 copy-start.3
  81.9 2.3 %copy-start = (f32[4,320,960]{2,1,0:T(8,128)}, f32[4,320,960]{2,1,0:T(8,128)S(1)}, u32[]{:S(2)}) copy-start(f32[4,320,960]{2,1,0:T(8,128)S(1)} %pad_maximum_fusion) | copy-start | bytes 14745604
  84.4 3.2 %collective-permute-start.4 = (bf16[2,320,960]{2,1,0:T(8,128)(2,1)S(1)}, bf16[2,320,960]{2,1,0:T(8,128)(2,1)}, u32[]{:S(2)}, u32[]{:S(2)}) collective-permute-start(bf16[2,320,960]{2,1,0:T(8,128)(2,1)S(1)} %fusion), channel_id=1, source_target_pairs={{0,1},{1,0},{2,3},{3,2},{4,5},{5,4},{6,7},{7,6},{8,9},{9,8},{10,11... | collective-permute-start | bytes 3686408 | tf_op jit(solution)/shard_map/ppermute | solution.py:250
  90.4 1.1 copy-start.2
  92.3 10.1 %collective-permute-start.5 = (bf16[2,80,960]{2,1,0:T(8,128)(2,1)}, bf16[2,80,960]{2,1,0:T(8,128)(2,1)}, u32[]{:S(2)}, u32[]{:S(2)}) collective-permute-start(bf16[2,80,960]{2,1,0:T(8,128)(2,1)} %fusion.11), channel_id=1, source_target_pairs={{0,8},{8,0},{16,24},{24,16},{1,9},{9,1},{17,25},{25,17},{2,10},{10... | collective-permute-start | bytes 921608 | tf_op jit(solution)/shard_map/ppermute | solution.py:250
  93.8 11.4 %collective-permute-start.7 = (bf16[2,80,960]{2,1,0:T(8,128)(2,1)S(1)}, bf16[2,80,960]{2,1,0:T(8,128)(2,1)S(1)}, u32[]{:S(2)}, u32[]{:S(2)}) collective-permute-start(bf16[2,80,960]{2,1,0:T(8,128)(2,1)S(1)} %fusion.10), channel_id=1, source_target_pairs={{0,16},{8,24},{16,0},{24,8},{1,17},{9,25},{17,1},{25,9},{2,18},{10... | collective-permute-start | bytes 921608 | tf_op jit(solution)/shard_map/ppermute | solution.py:250
  103.7 5.5 %collective-permute-start.6 = (bf16[80,960]{1,0:T(8,128)(2,1)S(1)}, bf16[80,960]{1,0:T(8,128)(2,1)S(1)}, u32[]{:S(2)}, u32[]{:S(2)}) collective-permute-start(bf16[80,960]{1,0:T(8,128)(2,1)S(1)} %fusion.19), channel_id=1, source_target_pairs={{0,16},{8,24},{16,0},{24,8},{1,17},{9,25},{17,1},{25,9},{2,18},{10... | collective-permute-start | bytes 460808 | tf_op jit(solution)/shard_map/ppermute | solution.py:250
  105.3 5.4 %collective-permute-start.8 = (bf16[80,960]{1,0:T(8,128)(2,1)S(1)}, bf16[80,960]{1,0:T(8,128)(2,1)S(1)}, u32[]{:S(2)}, u32[]{:S(2)}) collective-permute-start(bf16[80,960]{1,0:T(8,128)(2,1)S(1)} %fusion.20), channel_id=1, source_target_pairs={{0,8},{8,0},{16,24},{24,16},{1,9},{9,1},{17,25},{25,17},{2,10},{10... | collective-permute-start | bytes 460808 | tf_op jit(solution)/shard_map/ppermute | solution.py:250
  110.8 5.4 %collective-permute-start.9 = (bf16[1,80,960]{2,1,0:T(8,128)(2,1)S(1)}, bf16[1,80,960]{2,1,0:T(8,128)(2,1)S(1)}, u32[]{:S(2)}, u32[]{:S(2)}) collective-permute-start(bf16[1,80,960]{2,1,0:T(8,128)(2,1)S(1)} %fusion.13), channel_id=1, source_target_pairs={{0,2},{1,3},{2,0},{3,1},{4,6},{5,7},{6,4},{7,5},{8,10},{9,11},{10,... | collective-permute-start | bytes 460808 | tf_op jit(solution)/shard_map/ppermute | solution.py:250
  116.3 8.1 %collective-permute-start.10 = (bf16[1,80,960]{2,1,0:T(8,128)(2,1)S(1)}, bf16[1,80,960]{2,1,0:T(8,128)(2,1)S(1)}, u32[]{:S(2)}, u32[]{:S(2)}) collective-permute-start(bf16[1,80,960]{2,1,0:T(8,128)(2,1)S(1)} %fusion.16), channel_id=1, source_target_pairs={{0,4},{1,5},{2,6},{3,7},{4,0},{5,1},{6,2},{7,3},{8,12},{9,13},{10,... | collective-permute-start | bytes 460808 | tf_op jit(solution)/shard_map/ppermute | solution.py:250
  124.5 12.3 %collective-permute-start.11 = (bf16[1,80,960]{2,1,0:T(8,128)(2,1)S(1)}, bf16[1,80,960]{2,1,0:T(8,128)(2,1)S(1)}, u32[]{:S(2)}, u32[]{:S(2)}) collective-permute-start(bf16[1,80,960]{2,1,0:T(8,128)(2,1)S(1)} %add_convert_fusion), channel_id=1, source_target_pairs={{0,2},{1,3},{2,0},{3,1},{4,6},{5,7},{6,4},{7,5},{8,10},{9,11},{10,... | collective-permute-start | bytes 460808 | tf_op jit(solution)/shard_map/ppermute | solution.py:250
  133.3 10.8 %all-to-all-start.1 = ((bf16[4,2,320,128]{3,2,1,0:T(8,128)(2,1)}), bf16[4,2,320,128]{3,2,1,0:T(8,128)(2,1)S(1)}, u32[]{:S(2)}, u32[]{:S(2)}) async-start(bf16[4,2,320,128]{3,2,1,0:T(8,128)(2,1)} %shard_map.76), calls=%async_computation.1 | async-start | bytes 1310720 | tf_op jit(solution)/shard_map/all_to_all | solution.py:343
  136.8 8.2 %collective-permute-start.12 = (bf16[2,80,960]{2,1,0:T(8,128)(2,1)S(1)}, bf16[2,80,960]{2,1,0:T(8,128)(2,1)S(1)}, u32[]{:S(2)}, u32[]{:S(2)}) collective-permute-start(bf16[2,80,960]{2,1,0:T(8,128)(2,1)S(1)} %maximum_bitcast_fusion), channel_id=1, source_target_pairs={{0,1},{1,0},{2,3},{3,2},{4,5},{5,4},{6,7},{7,6},{8,9},{9,8},{10,11... | collective-permute-start | bytes 921608 | tf_op jit(solution)/shard_map/ppermute | solution.py:250
  136.9 7.1 %copy-start.6 = (bf16[1,1,8,320,128]{4,3,2,1,0:T(8,128)(2,1)S(1)}, bf16[1,1,8,320,128]{4,3,2,1,0:T(8,128)(2,1)}, u32[]{:S(2)}) copy-start(bf16[1,1,8,320,128]{4,3,2,1,0:T(8,128)(2,1)} %param.4) | copy-start | bytes 1966084

commit v2 on v1

v2 whole, which is shorter than its diff:
```python
import math

import jax
import jax.numpy as jnp
from jax import lax
from jax.experimental import pallas as pl
from jax.experimental.pallas import tpu as pltpu
from jax.sharding import PartitionSpec as P

BF = jnp.bfloat16
F32 = jnp.float32
VMEM_LIMIT = 24 * 1024 * 1024
NT = (((1,), (1,)), ((), ()))


def call(body, outs, scratch, flops, *args):
    moved = sum(x.size * x.dtype.itemsize for x in (*args, *outs))
    return pl.pallas_call(
        body,
        out_shape=tuple(outs),
        in_specs=[pl.BlockSpec(memory_space=pltpu.VMEM)] * len(args),
        out_specs=tuple(pl.BlockSpec(memory_space=pltpu.VMEM) for _ in outs),
        scratch_shapes=scratch,
        compiler_params=pltpu.CompilerParams(vmem_limit_bytes=VMEM_LIMIT),
        cost_estimate=pl.CostEstimate(flops=flops, bytes_accessed=moved, transcendentals=0),
    )(*args)


def shape(dims, dtype=BF):
    return jax.ShapeDtypeStruct(tuple(dims), dtype)


def columns(first, count, width):
    return pl.ds(pl.multiple_of(first * width, width), count * width)


def place(step):
    return jnp.bitwise_xor(lax.axis_index("seq"), step)


def core():
    return lax.rem(lax.axis_index("dp"), 2)


def pair_bit():
    return lax.rem(lax.div(lax.axis_index("dp"), 2), 2)


def at_block(index, size, count, tile, use):
    if size % tile == 0:
        use(pl.ds(pl.multiple_of(index * size, size), size))
        return
    for fixed in range(count):

        @pl.when(index == fixed)
        def _():
            use(pl.ds(fixed * size, size))


def swap(values, axis, bit):
    size = lax.axis_size(axis)
    return lax.ppermute(values, axis, [(i, i ^ bit) for i in range(size)])


def spread(blocks):
    return [swap(block, "seq", j + 1) for j, block in enumerate(blocks)]


def after(value, *others):
    return lax.optimization_barrier((value, *others))[0]


def shifted(block, step):
    if step == 0:
        return block
    width = block.shape[1]
    rolled = pltpu.roll(block.astype(F32), (-step) % width, 1)
    column = lax.broadcasted_iota(jnp.int32, block.shape, 1)
    edge = 0 if step < 0 else width - 1
    return jnp.where(column == edge, 0.0, rolled).astype(block.dtype)


def fill_taps(target, source, order):
    rows, chans, width = source.shape
    target[:, :width] = jnp.zeros((target.shape[0], width), target.dtype)
    target[:, (rows + 1) * width :] = jnp.zeros((target.shape[0], width), target.dtype)

    def row(y, carry):
        block = source[y]
        for b, step in enumerate(order):
            target[b * chans : (b + 1) * chans, columns(y + 1, 1, width)] = shifted(block, step)
        return carry

    lax.fori_loop(0, rows, row, 0)


def transposed(block):
    size = block.shape[0]
    one = lax.broadcasted_iota(jnp.int32, (size, size), 0) == lax.broadcasted_iota(
        jnp.int32, (size, size), 1
    )
    return lax.dot_general(one.astype(BF), block, NT, preferred_element_type=F32).astype(BF)


def window_taps(frames):
    rows, chans, width = frames.shape
    return call(
        lambda source, target: fill_taps(target, source, (-1, 0, 1)),
        [shape((3 * chans, (rows + 2) * width))],
        [],
        frames.size,
        frames,
    )[0]


def temporal_maps(own, first, second):
    _, shard, chans = own.shape
    count = len(first)

    def body(*refs):
        own_ref = refs[0]
        mine, theirs = refs[1 : 1 + count], refs[1 + count : 1 + 2 * count]
        plain_ref, trans_ref, rows_ref = refs[1 + 2 * count :]

        def fill(pieces):
            for j, piece in enumerate((own_ref, *pieces)):

                def put(at):
                    for k in range(3):
                        rows_ref[k, at, :] = piece[k]

                at_block(place(j), shard, count + 1, 16, put)

        @pl.when(core() == 0)
        def _():
            fill(mine)

        @pl.when(core() == 1)
        def _():
            fill(theirs)

        for k in range(3):
            plain_ref[:, k * chans : (k + 1) * chans] = rows_ref[k]
            trans_ref[:, k * chans : (k + 1) * chans] = transposed(rows_ref[k])

    return call(
        body,
        [shape((chans, 3 * chans))] * 2,
        [pltpu.VMEM((3, chans, chans), BF)],
        6 * chans**3,
        own,
        *first,
        *second,
    )


def temporal_backward(cot_rows, weights_t):
    frames, rows, chans, width = cot_rows.shape
    span = rows * width

    def body(cot_ref, weights_ref, *refs):
        outs, taps_ref = refs[:frames], refs[frames]
        edge = jnp.zeros((chans, span), BF)
        taps_ref[:chans, (frames - 1) * span :] = edge
        taps_ref[2 * chans :, :span] = edge
        for f in range(frames):
            for k in range(3):
                at = f + k - 1
                if 0 <= at < frames:
                    for y in range(rows):
                        to = at * span + y * width
                        taps_ref[k * chans : (k + 1) * chans, to : to + width] = cot_ref[f, y]
        for j in range(frames):
            total = jnp.dot(
                weights_ref[...],
                taps_ref[:, columns(place(j), 1, span)],
                preferred_element_type=F32,
            ).astype(BF)
            for y in range(rows):
                outs[j][y] = total[:, y * width : (y + 1) * width]

    return call(
        body,
        [shape((rows, chans, width))] * frames,
        [pltpu.VMEM((3 * chans, frames * span), BF)],
        6 * chans * cot_rows.size,
        cot_rows,
        weights_t,
    )


def spatial_forward(taps, own, first_a, second_a, first_b, second_b, rows):
    _, shard, chans = own.shape
    count = len(first_a)
    width = taps.shape[1] // (rows + 2)
    block = rows // (count + 1)

    def body(*refs):
        taps_ref, own_ref = refs[:2]
        lists = [refs[2 + i * count : 2 + (i + 1) * count] for i in range(4)]
        refs = refs[2 + 4 * count :]
        pre_ref, weights_ref, outs, act_ref = refs[0], refs[1], refs[2:-1], refs[-1]

        def fill(row, pieces, first_tap):
            for j, piece in enumerate((own_ref, *pieces)):

                def put(at):
                    for b in range(3):
                        source = piece[first_tap + b] if j == 0 else piece[b]
                        weights_ref[row, at, b * chans : (b + 1) * chans] = source

                at_block(place(j), shard, count + 1, 16, put)

        @pl.when(core() == 0)
        def _():
            fill(0, lists[2], 0)
            fill(1, lists[1], 3)
            fill(2, lists[3], 6)

        @pl.when(core() == 1)
        def _():
            fill(0, lists[3], 0)
            fill(1, lists[0], 3)
            fill(2, lists[2], 6)

        def tile(i, carry):
            total = jnp.zeros((chans, 2 * width), F32)
            for a in range(3):
                total += jnp.dot(
                    weights_ref[a],
                    taps_ref[:, columns(2 * i + a, 2, width)],
                    preferred_element_type=F32,
                )
            pre = total.astype(BF)
            wide = pre.astype(F32)
            act = (wide / (1.0 + jnp.exp(-wide))).astype(BF)
            for r in range(2):
                pre_ref[2 * i + r] = pre[:, r * width : (r + 1) * width]
                act_ref[2 * i + r] = act[:, r * width : (r + 1) * width]
            return carry

        lax.fori_loop(0, rows // 2, tile, 0)
        for j, out in enumerate(outs):
            out[...] = act_ref[pl.ds(place(j) * block, block)]

    pre, weights, *acts = call(
        body,
        [shape((rows, chans, width)), shape((3, chans, 3 * chans))]
        + [shape((block, chans, width))] * (count + 1),
        [pltpu.VMEM((rows, chans, width), BF)],
        18 * chans * chans * rows * width,
        taps,
        own,
        *first_a,
        *second_a,
        *first_b,
        *second_b,
    )
    return pre, weights, acts


def activation_grad(pre_act, grads, shard):
    rows, chans, width = pre_act.shape
    block = rows // len(grads)
    half = shard // 2

    def body(*refs):
        pre_ref, grad_refs = refs[0], refs[1 : 1 + len(grads)]
        pg_ref, mine_ref, theirs_ref, act_ref = refs[1 + len(grads) :]
        for j, ref in enumerate(grad_refs):
            act_ref[pl.ds(place(j) * block, block)] = ref[...]

        def row(y, carry):
            wide = pre_ref[y].astype(F32)
            s = 1.0 / (1.0 + jnp.exp(-wide))
            pg = act_ref[y].astype(F32) * s * (1.0 + wide * (1.0 - s))
            pg_ref[y] = pg.astype(BF)
            low = [pg[at : at + half] for at in range(0, chans, shard)]
            high = [pg[at + half : at + shard] for at in range(0, chans, shard)]
            low = jnp.concatenate(low).astype(BF)
            high = jnp.concatenate(high).astype(BF)
            first = core() == 0
            mine_ref[:, columns(y, 1, width)] = jnp.where(first, low, high)
            theirs_ref[:, columns(y, 1, width)] = jnp.where(first, high, low)
            return carry

        lax.fori_loop(0, rows, row, 0)

    return call(
        body,
        [shape(pre_act.shape)] + [shape((chans // 2, rows * width))] * 2,
        [pltpu.VMEM(pre_act.shape, BF)],
        20 * pre_act.size,
        pre_act,
        *grads,
    )


def spatial_weight_grad(taps, other_taps, half_grad, other_half, owners, scale, width):
    wide = taps.shape[0]
    chans, span = half_grad.shape
    part = chans // owners

    def body(taps_ref, other_ref, mine_ref, theirs_ref, *refs):
        keep_ref, sends, stack_ref, total_ref = refs[0], refs[1:-2], refs[-2], refs[-1]
        edge = jnp.zeros((chans, width), BF)
        for q, source in enumerate((mine_ref, theirs_ref)):
            at = q * span
            stack_ref[:chans, at + span - width : at + span] = edge
            stack_ref[:chans, at : at + span - width] = source[:, width:]
            stack_ref[chans : 2 * chans, at : at + span] = source[...]
            stack_ref[2 * chans :, at : at + width] = edge
            stack_ref[2 * chans :, at + width : at + span] = source[:, : span - width]
        total = jnp.zeros((3 * chans, wide), F32)
        for q, source in enumerate((taps_ref, other_ref)):
            total += lax.dot_general(
                stack_ref[:, q * span : (q + 1) * span],
                source[:, width : width + span],
                NT,
                preferred_element_type=F32,
            )
        for a in range(3):
            total_ref[a] = total[a * chans : (a + 1) * chans] * scale
        for j in range(owners):

            def put(at):
                for a in range(3):
                    value = total_ref[a, at, :]
                    if j == 0:
                        keep_ref[a] = value
                    else:
                        sends[j - 1][a] = value.astype(BF)

            at_block(place(j), part, owners, 8, put)

    return call(
        body,
        [shape((3, part, wide), F32)] + [shape((3, part, wide))] * (owners - 1),
        [pltpu.VMEM((3 * chans, 2 * span), BF), pltpu.VMEM((3, chans, wide), F32)],
        12 * chans * wide * span,
        taps,
        other_taps,
        half_grad,
        other_half,
    )


def spatial_backward(pre_grad, cotangent, weights):
    rows, chans, width = pre_grad.shape

    def body(pg_ref, cot_ref, weights_ref, out_ref, taps_ref, trans_ref):
        for a in range(3):
            for b in range(3):
                at = slice(b * chans, (b + 1) * chans)
                trans_ref[a, :, at] = transposed(weights_ref[a, :, at])
        fill_taps(taps_ref, pg_ref, (1, 0, -1))

        def tile(i, carry):
            total = jnp.zeros((chans, 2 * width), F32)
            for a in range(3):
                total += jnp.dot(
                    trans_ref[a],
                    taps_ref[:, columns(2 * i + 2 - a, 2, width)],
                    preferred_element_type=F32,
                )
            for r in range(2):
                wide = cot_ref[2 * i + r].astype(F32)
                out_ref[2 * i + r] = (wide + total[:, r * width : (r + 1) * width]).astype(BF)
            return carry

        lax.fori_loop(0, rows // 2, tile, 0)

    return call(
        body,
        [shape(pre_grad.shape)],
        [
            pltpu.VMEM((3 * chans, (rows + 2) * width), BF),
            pltpu.VMEM((3, chans, 3 * chans), BF),
        ],
        18 * chans * chans * rows * width,
        pre_grad,
        cotangent,
        weights,
    )[0]


def temporal_forward(acts, cot_rows, weights, shard, scale):
    frames, rows, chans, width = cot_rows.shape
    span = rows * width
    half = shard // 2

    def body(*refs):
        act_refs = refs[:frames]
        cot_ref, weights_ref = refs[frames : frames + 2]
        outs = refs[frames + 2 : 2 * frames + 2]
        keep_ref, send_ref, flat_ref, taps_ref, cots_ref = refs[2 * frames + 2 :]
        for j, ref in enumerate(act_refs):
            for y in range(rows):
                at = pl.multiple_of(place(j) * span + y * width, width)
                flat_ref[:, pl.ds(at, width)] = ref[y]
        edge = jnp.zeros((chans, span), BF)
        whole = frames * span
        taps_ref[:chans, :span] = edge
        taps_ref[:chans, span:] = flat_ref[:, : whole - span]
        taps_ref[chans : 2 * chans, :] = flat_ref[...]
        taps_ref[2 * chans :, whole - span :] = edge
        taps_ref[2 * chans :, : whole - span] = flat_ref[:, span:]
        for f in range(frames):
            for y in range(rows):
                at = f * span + y * width
                cots_ref[:, at : at + width] = cot_ref[f, y]
        for j in range(frames):
            total = jnp.dot(
                weights_ref[...],
                taps_ref[:, columns(place(j), 1, span)],
                preferred_element_type=F32,
            ).astype(BF)
            for y in range(rows):
                outs[j][y] = total[:, y * width : (y + 1) * width]
        total = (
            lax.dot_general(cots_ref[...], taps_ref[...], NT, preferred_element_type=F32) * scale
        )
        first = core() == 0
        for s in range(chans // shard):
            low = total[s * shard : s * shard + half]
            high = total[s * shard + half : (s + 1) * shard]
            keep_ref[s] = jnp.where(first, low, high)
            send_ref[s] = jnp.where(first, high, low).astype(BF)

    owners = chans // shard
    *outs, keep, send = call(
        body,
        [shape((rows, chans, width))] * frames
        + [shape((owners, half, 3 * chans), F32), shape((owners, half, 3 * chans))],
        [
            pltpu.VMEM((chans, frames * span), BF),
            pltpu.VMEM((3 * chans, frames * span), BF),
            pltpu.VMEM((chans, frames * span), BF),
        ],
        12 * chans * cot_rows.size,
        *acts,
        cot_rows,
        weights,
    )
    return outs, keep, send


def pair_sum(keep, other):
    owners, half, wide = keep.shape

    def body(keep_ref, other_ref, own_ref, *sends):
        for j in range(owners):
            at = place(j)
            value = keep_ref[at] + other_ref[at].astype(F32)
            if j == 0:
                own_ref[...] = value
            else:
                sends[j - 1][...] = value.astype(BF)

    return call(
        body,
        [shape((half, wide), F32)] + [shape((half, wide))] * (owners - 1),
        [],
        keep.size,
        keep,
        other,
    )


def owner_sum(spatial, spatial_in, temporal, temporal_in):
    _, half, wide = spatial.shape
    count = len(spatial_in)

    def body(*refs):
        spatial_ref, temporal_ref = refs[:2]
        others, temporal_others = refs[2 : 2 + count], refs[2 + count : 2 + 2 * count]
        keep_ref, send_ref, sum_ref = refs[2 + 2 * count :]
        for a in range(3):
            value = spatial_ref[a]
            for ref in others:
                value += ref[a].astype(F32)
            sum_ref[a] = value
        value = temporal_ref[...]
        for ref in temporal_others:
            value += ref[...].astype(F32)
        sum_ref[3] = value
        bit = pair_bit()
        keep_ref[...] = sum_ref[pl.ds(2 * bit, 2)]
        send_ref[...] = sum_ref[pl.ds(2 - 2 * bit, 2)].astype(BF)

    return call(
        body,
        [shape((2, half, wide), F32), shape((2, half, wide))],
        [pltpu.VMEM((4, half, wide), F32)],
        4 * spatial.size,
        spatial,
        temporal,
        *spatial_in,
        *temporal_in,
    )


def add_rounded(keep, other):
    def body(keep_ref, other_ref, out_ref):
        out_ref[...] = (keep_ref[...].astype(F32) + other_ref[...].astype(F32)).astype(BF)

    return call(body, [shape(keep.shape)], [], keep.size, keep, other)[0]


def kernel_outputs(parts, chans):
    _, half, wide = parts[0].shape

    def body(own_ref, next_ref, core_ref, both_ref, spatial_ref, temporal_ref, sum_ref):
        bit, mine = pair_bit(), core()
        for ref, group, side in (
            (own_ref, bit, mine),
            (next_ref, 1 - bit, mine),
            (core_ref, bit, 1 - mine),
            (both_ref, 1 - bit, 1 - mine),
        ):

            def put(at):
                for g in range(2):
                    sum_ref[2 * group + g, at, :] = ref[g].astype(F32)

            at_block(side, half, 2, 8, put)
        for a in range(3):
            for b in range(3):
                spatial_ref[3 * a + b] = sum_ref[a, :, b * chans : (b + 1) * chans]
        for k in range(3):
            temporal_ref[k] = sum_ref[3, :, k * chans : (k + 1) * chans]

    return call(
        body,
        [shape((9, 2 * half, chans), F32), shape((3, 2 * half, chans), F32)],
        [pltpu.VMEM((4, 2 * half, wide), F32)],
        8 * parts[0].size,
        *parts,
    )


def block_output(frames, parts):
    rows, chans, width = frames.shape
    block = rows // len(parts)

    def body(frames_ref, *refs):
        parts_in, out_ref = refs[:-1], refs[-1]
        for j, ref in enumerate(parts_in):
            at = pl.ds(place(j) * block, block)
            out_ref[at] = (frames_ref[at].astype(F32) + ref[...].astype(F32)).astype(BF)

    return call(body, [shape(frames.shape)], [], frames.size, frames, *parts)[0]


def local(frames_in, spatial_kernel, temporal_kernel, out_cotangent):
    frames, cotangent = frames_in[0, 0], out_cotangent[0, 0]
    rows, chans, width = frames.shape
    seq, dp = lax.axis_size("seq"), lax.axis_size("dp")
    shard = spatial_kernel.shape[1]
    scale = 1.0 / math.sqrt(dp * seq * rows * width)

    first = core() == 0
    mine_a = jnp.where(first, temporal_kernel, spatial_kernel[3:6])
    mine_b = jnp.where(first, spatial_kernel[:3], spatial_kernel[6:])
    got_a = spread([mine_a] * (seq - 1))
    cot_rows = lax.all_to_all(
        cotangent.reshape(seq, rows // seq, chans, width), "seq", 0, 0, tiled=True
    )
    got_b = spread([mine_b] * (seq - 1))
    other_frames = swap(frames, "dp", 1)
    pair_a = [swap(piece, "dp", 1) for piece in got_a]
    pair_b = [swap(piece, "dp", 1) for piece in got_b]
    taps = window_taps(frames)
    other_taps = window_taps(other_frames)
    temporal_w, temporal_t = temporal_maps(temporal_kernel, got_a, pair_a)

    grads = temporal_backward(cot_rows, temporal_t)
    act_grad = [grads[0], *spread(grads[1:])]
    pre_act, weights, acts = spatial_forward(
        taps, spatial_kernel, got_a, pair_a, got_b, pair_b, rows
    )
    act_rows = [acts[0], *spread(acts[1:])]
    pre_grad, half_mine, half_theirs = activation_grad(pre_act, act_grad, shard)
    half_other = swap(half_theirs, "dp", 1)
    spatial_keep, *spatial_send = spatial_weight_grad(
        taps, other_taps, half_mine, half_other, seq, scale, width
    )
    spatial_got = spread(spatial_send)
    temporal_rows, temporal_keep, temporal_send = temporal_forward(
        act_rows, cot_rows, temporal_w, shard, scale
    )
    temporal_own, *temporal_sends = pair_sum(temporal_keep, swap(temporal_send, "dp", 1))
    temporal_got = spread(temporal_sends)
    input_grad = spatial_backward(pre_grad, cotangent, weights)
    keep, send = owner_sum(
        after(spatial_keep, input_grad), spatial_got, temporal_own, temporal_got
    )
    temporal = [temporal_rows[0], *spread(temporal_rows[1:])]
    total = add_rounded(keep, swap(send, "dp", 2))
    block_out = block_output(frames, temporal)
    bit = 4
    while bit < dp:
        total = add_rounded(total, swap(total, "dp", bit))
        bit *= 2
    total = after(total, block_out)
    near = swap(total, "dp", 2)
    spatial_grad, temporal_grad = kernel_outputs(
        (total, near, swap(total, "dp", 1), swap(near, "dp", 1)), chans
    )
    return (block_out[None, None], input_grad[None, None], spatial_grad, temporal_grad)


def solution(mesh):
    placed = (
        P("dp", "seq", None, None, None),
        P(None, "seq", None),
        P(None, "seq", None),
        P("dp", "seq", None, None, None),
    )
    return jax.shard_map(
        local,
        mesh=mesh,
        in_specs=placed,
        out_specs=(
            P("dp", "seq", None, None, None),
            P("dp", "seq", None, None, None),
            P(None, "seq", None),
            P(None, "seq", None),
        ),
        check_vma=False,
    )
```

time: 148 us -> 115 us (0.78)
  local copies, waits for them, and re-layouts: 27.3 us -> 9.8 us
  other arithmetic: 12.9 us -> 1.24 us
  starting transfers between devices: 28.9 us -> 38.3 us
  waiting for transfers between devices: 47.2 us -> 38 us
  Pallas kernels: 30.3 us -> 25.8 us
    ppermute x13 -> x35, starting transfers between devices: 14.3 us -> 33 us  [swap(): return lax.ppermute(values, axis, [(i, i ^ bit) for i in range(size)])]
    all_to_all x3 -> x0, starting transfers between devices: 11.1 us -> none  [the longest x1 4.16 us: local(): lax.all_to_all(activated.reshape(seq, rows // seq, chans, width), 'seq',...]
    reshape x4 -> x0, local copies, waits for them, and re-layouts: 8.62 us -> none  [the longest x1 4.06 us: local(): spatial_w = spatial.transpose(0, 2, 1, 3).reshape(3, chans, 3 * chans)]
    pallas_call x6 -> x15, Pallas kernels: 30.3 us -> 25.8 us  [call(): pl.pallas_call(body, out_shape=tuple(outs), in_specs=[pl.BlockSpec(memory...]
    slice x5 -> x0, local copies, waits for them, and re-layouts: 4.36 us -> none  [the longest x1 1.85 us: local(): spatial = kernels[3:].reshape(3, 3, chans, chans)]
    all_to_all x1, waiting for transfers between devices: 4 us -> 0.01 us  [local(): lax.all_to_all(cotangent.reshape(seq, rows // seq, chans, width), 'seq',...]
    transpose x2 -> x0, local copies, waits for them, and re-layouts: 3.98 us -> none  [the longest x1 2.5 us: local(): spatial_w = spatial.transpose(0, 2, 1, 3).reshape(3, chans, 3 * chans)]
    add x3 -> x0, other arithmetic: 3.89 us -> none  [reduce_half(): return kept + swap(sent.astype(BF), axis, bit).astype(F32)]
  transfers between devices with their start and end apart: 17 -> 36, of which waited for: 12 -> 13; matrix products, arithmetic and copies ran while one was open for 14% -> 1% of each run, Pallas kernels for 16% -> 21%
where the time goes in v2:
time: 115 us; the launch traced here: 114 us
  starting transfers between devices  38.3 us (33%)
  waiting for transfers between devices  38 us (33%)
  Pallas kernels  25.8 us (22%)
  local copies, waits for them, and re-layouts  9.8 us (9%)
  other arithmetic  1.24 us (1%)
    ppermute x35, waiting for transfers between devices, swap(): return lax.ppermute(values, axis, [(i, i ^ bit) for i in range(size)])  38 us
    ppermute x35, starting transfers between devices, swap(): return lax.ppermute(values, axis, [(i, i ^ bit) for i in range(size)])  33 us
    pallas_call x15, Pallas kernels, call(): pl.pallas_call(body, out_shape=tuple(outs), in_specs=[pl.BlockSpec(memory...  25.8 us
    unnamed x36, local copies, waits for them, and re-layouts  9.8 us
    all_to_all x1, starting transfers between devices, local(): lax.all_to_all(cotangent.reshape(seq, rows // seq, chans, width), 'seq',...  5.31 us
  transfers between devices with their start and end apart: 36, of which 13 were waited for; matrix products, arithmetic and copies ran while one was open for 1% of the time, Pallas kernels for 21%

profile of v2, /device:TPU:0, one launch (start us, length us, event | category | flops | bytes accessed | tf_op | source)
XLA Modules:
  0.0 114.0 jit_solution(6086452014438287659)
XLA Ops:
  0.7 5.3 %all-to-all-start = ((bf16[4,2,320,128]{3,2,1,0:T(8,128)(2,1)}), bf16[4,2,320,128]{3,2,1,0:T(8,128)(2,1)}, u32[]{:S(2)}, u32[]{:S(2)}) async-start(bf16[4,2,320,128]{3,2,1,0:T(8,128)(2,1)} %bitcast.8), calls=%async_computation | async-start | bytes 1310720 | tf_op jit(solution)/shard_map/all_to_all | solution.py:566
  7.2 2.1 %collective-permute-start = (bf16[3,80,320]{2,1,0:T(8,128)(2,1)S(1)}, bf16[3,80,320]{2,1,0:T(8,128)(2,1)S(1)}, u32[]{:S(2)}, u32[]{:S(2)}) collective-permute-start(bf16[3,80,320]{2,1,0:T(8,128)(2,1)S(1)} %get-tuple-element.75), channel_id=1, source_target_pairs={{0,8},{8,0},{16,24},{24,16},{1,9},{9,1},{17,25},{25,17},{2,10},{10... | collective-permute-start | bytes 460808 | tf_op jit(solution)/shard_map/ppermute | solution.py:62
  9.3 1.5 %collective-permute-start.1 = (bf16[3,80,320]{2,1,0:T(8,128)(2,1)S(1)}, bf16[3,80,320]{2,1,0:T(8,128)(2,1)S(1)}, u32[]{:S(2)}, u32[]{:S(2)}) collective-permute-start(bf16[3,80,320]{2,1,0:T(8,128)(2,1)S(1)} %get-tuple-element.75), channel_id=1, source_target_pairs={{0,16},{8,24},{16,0},{24,8},{1,17},{9,25},{17,1},{25,9},{2,18},{10... | collective-permute-start | bytes 460808 | tf_op jit(solution)/shard_map/ppermute | solution.py:62
  10.8 1.9 %collective-permute-start.6 = (bf16[3,80,320]{2,1,0:T(8,128)(2,1)S(1)}, bf16[3,80,320]{2,1,0:T(8,128)(2,1)}, u32[]{:S(2)}, u32[]{:S(2)}) collective-permute-start(bf16[3,80,320]{2,1,0:T(8,128)(2,1)S(1)} %get-tuple-element.74), channel_id=1, source_target_pairs={{0,8},{8,0},{16,24},{24,16},{1,9},{9,1},{17,25},{25,17},{2,10},{10... | collective-permute-start | bytes 460808 | tf_op jit(solution)/shard_map/ppermute | solution.py:62
  12.8 1.5 %collective-permute-start.7 = (bf16[3,80,320]{2,1,0:T(8,128)(2,1)S(1)}, bf16[3,80,320]{2,1,0:T(8,128)(2,1)}, u32[]{:S(2)}, u32[]{:S(2)}) collective-permute-start(bf16[3,80,320]{2,1,0:T(8,128)(2,1)S(1)} %get-tuple-element.74), channel_id=1, source_target_pairs={{0,16},{8,24},{16,0},{24,8},{1,17},{9,25},{17,1},{25,9},{2,18},{10... | collective-permute-start | bytes 460808 | tf_op jit(solution)/shard_map/ppermute | solution.py:62
  14.2 6.5 %collective-permute-done.refs_2_.refs_1_ = bf16[3,80,320]{2,1,0:T(8,128)(2,1)S(1)} collective-permute-done((bf16[3,80,320]{2,1,0:T(8,128)(2,1)S(1)}, bf16[3,80,320]{2,1,0:T(8,128)(2,1)S(1)}, u32[]{:S(2)}, u32[]{:S(2)}) %collective-permute-start) | collective-permute-done | bytes 153632 | tf_op jit(solution)/shard_map/ppermute | solution.py:62
  20.7 1.5 %collective-permute-start.8 = (bf16[3,80,320]{2,1,0:T(8,128)(2,1)S(1)}, bf16[3,80,320]{2,1,0:T(8,128)(2,1)}, u32[]{:S(2)}, u32[]{:S(2)}) collective-permute-start(bf16[3,80,320]{2,1,0:T(8,128)(2,1)S(1)} %get-tuple-element.74), channel_id=1, source_target_pairs={{0,24},{8,16},{16,8},{24,0},{1,25},{9,17},{17,9},{25,1},{2,26},{10... | collective-permute-start | bytes 460808 | tf_op jit(solution)/shard_map/ppermute | solution.py:62
  22.2 3.4 %collective-permute-done.2.refs_4_.refs_3_ = bf16[3,80,320]{2,1,0:T(8,128)(2,1)S(1)} collective-permute-done((bf16[3,80,320]{2,1,0:T(8,128)(2,1)S(1)}, bf16[3,80,320]{2,1,0:T(8,128)(2,1)S(1)}, u32[]{:S(2)}, u32[]{:S(2)}) %collective-permute-start.2) | collective-permute-done | bytes 153632 | tf_op jit(solution)/shard_map/ppermute | solution.py:62
  25.6 3.2 %collective-permute-done.6.refs_8_ = bf16[3,80,320]{2,1,0:T(8,128)(2,1)} collective-permute-done((bf16[3,80,320]{2,1,0:T(8,128)(2,1)S(1)}, bf16[3,80,320]{2,1,0:T(8,128)(2,1)}, u32[]{:S(2)}, u32[]{:S(2)}) %collective-permute-start.6) | collective-permute-done | bytes 153632 | tf_op jit(solution)/shard_map/ppermute | solution.py:62
  29.3 3.4 %collective-permute-done.8.refs_10_ = bf16[3,80,320]{2,1,0:T(8,128)(2,1)} collective-permute-done((bf16[3,80,320]{2,1,0:T(8,128)(2,1)S(1)}, bf16[3,80,320]{2,1,0:T(8,128)(2,1)}, u32[]{:S(2)}, u32[]{:S(2)}) %collective-permute-start.8) | collective-permute-done | bytes 153632 | tf_op jit(solution)/shard_map/ppermute | solution.py:62
  39.3 2.2 %shard_map.80 = (bf16[2,320,128]{2,1,0:T(8,128)(2,1)S(1)}, bf16[2,320,128]{2,1,0:T(8,128)(2,1)S(1)}, bf16[2,320,128]{2,1,0:T(8,128)(2,1)S(1)}, bf16[2,320,128]{2,1,0:T(8,128)(2,1)S(1)}) custom-call(bf16[4,2,320,128]{3,2,1,0:T(8,128)(2,1)} %all-to-all-done.refs_4_.cot_ref, bf16[320,960]{1,0:T(8,128)(2,1)S(1)} %copy-done.17), custom_call_target="tpu_custom_call" | custom-call | flops 629145600 | bytes 1925120 | tf_op jit(solution)/shard_map/pallas_call | solution.py:18
  43.0 2.0 %collective-permute-start.20 = (bf16[2,320,128]{2,1,0:T(8,128)(2,1)S(1)}, bf16[2,320,128]{2,1,0:T(8,128)(2,1)S(1)}, u32[]{:S(2)}, u32[]{:S(2)}) collective-permute-start(bf16[2,320,128]{2,1,0:T(8,128)(2,1)S(1)} %get-tuple-element.53), channel_id=1, source_target_pairs={{0,24},{8,16},{16,8},{24,0},{1,25},{9,17},{17,9},{25,1},{2,26},{10... | collective-permute-start | bytes 491528 | tf_op jit(solution)/shard_map/ppermute | solution.py:62
  50.7 4.9 %shard_map.76 = (bf16[8,320,128]{2,1,0:T(8,128)(2,1)S(1)}, bf16[3,320,960]{2,1,0:T(8,128)(2,1)S(1)}, bf16[2,320,128]{2,1,0:T(8,128)(2,1)S(1)}, bf16[2,320,128]{2...) custom-call(bf16[960,1280]{1,0:T(8,128)(2,1)S(1)} %shard_map.75.refs_0_.taps_ref, ...), custom_call_target="tpu_custom_call" | custom-call | flops 1887436800 | bytes 7915520 | tf_op jit(solution)/shard_map/pallas_call | solution.py:18
  57.2 2.0 %collective-permute-start.14 = (bf16[2,320,128]{2,1,0:T(8,128)(2,1)S(1)}, bf16[2,320,128]{2,1,0:T(8,128)(2,1)S(1)}, u32[]{:S(2)}, u32[]{:S(2)}) collective-permute-start(bf16[2,320,128]{2,1,0:T(8,128)(2,1)S(1)} %get-tuple-element.42), channel_id=1, source_target_pairs={{0,24},{8,16},{16,8},{24,0},{1,25},{9,17},{17,9},{25,1},{2,26},{10... | collective-permute-start | bytes 491528 | tf_op jit(solution)/shard_map/ppermute | solution.py:62
  60.0 2.8 %collective-permute-done.12.refs_1_ = bf16[2,320,128]{2,1,0:T(8,128)(2,1)S(1)} collective-permute-done((bf16[2,320,128]{2,1,0:T(8,128)(2,1)S(1)}, bf16[2,320,128]{2,1,0:T(8,128)(2,1)S(1)}, u32[]{:S(2)}, u32[]{:S(2)}) %collective-permute-start.12) | collective-permute-done | bytes 163872 | tf_op jit(solution)/shard_map/ppermute | solution.py:62
  62.8 2.4 %collective-permute-done.13.refs_2_ = bf16[2,320,128]{2,1,0:T(8,128)(2,1)S(1)} collective-permute-done((bf16[2,320,128]{2,1,0:T(8,128)(2,1)S(1)}, bf16[2,320,128]{2,1,0:T(8,128)(2,1)S(1)}, u32[]{:S(2)}, u32[]{:S(2)}) %collective-permute-start.13) | collective-permute-done | bytes 163872 | tf_op jit(solution)/shard_map/ppermute | solution.py:62
  65.2 3.0 %shard_map.78 = (bf16[2,320,128]{2,1,0:T(8,128)(2,1)S(1)}, bf16[2,320,128]{2,1,0:T(8,128)(2,1)S(1)}, bf16[2,320,128]{2,1,0:T(8,128)(2,1)S(1)}, bf16[2,320,128]{2...) custom-call(bf16[2,320,128]{2,1,0:T(8,128)(2,1)S(1)} %get-tuple-element.39.refs_0_, ...), custom_call_target="tpu_custom_call" | custom-call | flops 1258291200 | bytes 3502080 | tf_op jit(solution)/shard_map/pallas_call | solution.py:18
  68.3 2.1 %shard_map.83.other_ref = bf16[960,1280]{1,0:T(8,128)(2,1)S(1)} custom-call(bf16[8,320,128]{2,1,0:T(8,128)(2,1)} %collective-permute-done.21.source), custom_call_target="tpu_custom_call" | custom-call | flops 327680 | bytes 3112960 | tf_op jit(solution)/shard_map/pallas_call | solution.py:18
  70.4 1.5 %collective-permute-start.27 = (bf16[40,960]{1,0:T(8,128)(2,1)S(1)}, bf16[40,960]{1,0:T(8,128)(2,1)S(1)}, u32[]{:S(2)}, u32[]{:S(2)}) collective-permute-start(bf16[40,960]{1,0:T(8,128)(2,1)S(1)} %get-tuple-element.66), channel_id=1, source_target_pairs={{0,8},{8,0},{16,24},{24,16},{1,9},{9,1},{17,25},{25,17},{2,10},{10... | collective-permute-start | bytes 230408 | tf_op jit(solution)/shard_map/ppermute | solution.py:62
  72.0 2.3 %shard_map.84 = (f32[3,40,960]{2,1,0:T(8,128)S(1)}, bf16[3,40,960]{2,1,0:T(8,128)(2,1)S(1)}, bf16[3,40,960]{2,1,0:T(8,128)(2,1)S(1)}, bf16[3,40,960]{2,1,0:T(8,128)(2,1)S(1)}) custom-call(bf16[960,1280]{1,0:T(8,128)(2,1)S(1)} %shard_map.75.refs_0_.taps_ref, bf16[960,1280]{1,0:T(8,128)(2,1)S(1)} %shard_map.83.other_ref, ...), custom_call_target="tpu_custom_call" | custom-call | flops 1887436800 | bytes 6722560 | tf_op jit(solution)/shard_map/pallas_call | solution.py:18
  76.1 1.7 %collective-permute-start.26 = (bf16[3,40,960]{2,1,0:T(8,128)(2,1)S(1)}, bf16[3,40,960]{2,1,0:T(8,128)(2,1)S(1)}, u32[]{:S(2)}, u32[]{:S(2)}) collective-permute-start(bf16[3,40,960]{2,1,0:T(8,128)(2,1)S(1)} %get-tuple-element.65), channel_id=1, source_target_pairs={{0,24},{8,16},{16,8},{24,0},{1,25},{9,17},{17,9},{25,1},{2,26},{10... | collective-permute-start | bytes 691208 | tf_op jit(solution)/shard_map/ppermute | solution.py:62
  78.4 1.5 %collective-permute-start.29 = (bf16[40,960]{1,0:T(8,128)(2,1)S(1)}, bf16[40,960]{1,0:T(8,128)(2,1)S(1)}, u32[]{:S(2)}, u32[]{:S(2)}) collective-permute-start(bf16[40,960]{1,0:T(8,128)(2,1)S(1)} %get-tuple-element.68), channel_id=1, source_target_pairs={{0,24},{8,16},{16,8},{24,0},{1,25},{9,17},{17,9},{25,1},{2,26},{10... | collective-permute-start | bytes 230408 | tf_op jit(solution)/shard_map/ppermute | solution.py:62
  79.9 6.1 %shard_map.82 = bf16[8,320,128]{2,1,0:T(8,128)(2,1)} custom-call(bf16[8,320,128]{2,1,0:T(8,128)(2,1)S(1)} %get-tuple-element.54.pg_ref, bf16[8,320,128]{2,1,0:T(8,128)(2,1)S(1)} %bitcast.9, bf16[3,320,960]{2,1,0:T(8,128)(2,1)S(1)} %get-tuple-element.55.weights_ref), custom_call_target="tpu_custom_call" | custom-call | flops 1887436800 | bytes 3809280 | tf_op jit(solution)/shard_map/pallas_call | solution.py:18
  86.0 5.5 %collective-permute-done.28.refs_6_ = bf16[40,960]{1,0:T(8,128)(2,1)S(1)} collective-permute-done((bf16[40,960]{1,0:T(8,128)(2,1)S(1)}, bf16[40,960]{1,0:T(8,128)(2,1)S(1)}, u32[]{:S(2)}, u32[]{:S(2)}) %collective-permute-start.28) | collective-permute-done | bytes 76832 | tf_op jit(solution)/shard_map/ppermute | solution.py:62
  91.7 1.8 %collective-permute-start.30 = (bf16[2,40,960]{2,1,0:T(8,128)(2,1)S(1)}, bf16[2,40,960]{2,1,0:T(8,128)(2,1)S(1)}, u32[]{:S(2)}, u32[]{:S(2)}) collective-permute-start(bf16[2,40,960]{2,1,0:T(8,128)(2,1)S(1)} %get-tuple-element.70), channel_id=1, source_target_pairs={{0,2},{1,3},{2,0},{3,1},{4,6},{5,7},{6,4},{7,5},{8,10},{9,11},{10,... | collective-permute-start | bytes 460808 | tf_op jit(solution)/shard_map/ppermute | solution.py:62
  93.6 1.5 %collective-permute-start.15 = (bf16[2,320,128]{2,1,0:T(8,128)(2,1)S(1)}, bf16[2,320,128]{2,1,0:T(8,128)(2,1)S(1)}, u32[]{:S(2)}, u32[]{:S(2)}) collective-permute-start(bf16[2,320,128]{2,1,0:T(8,128)(2,1)S(1)} %get-tuple-element.45), channel_id=1, source_target_pairs={{0,8},{8,0},{16,24},{24,16},{1,9},{9,1},{17,25},{25,17},{2,10},{10... | collective-permute-start | bytes 491528 | tf_op jit(solution)/shard_map/ppermute | solution.py:62
  95.6 1.5 %collective-permute-start.17 = (bf16[2,320,128]{2,1,0:T(8,128)(2,1)S(1)}, bf16[2,320,128]{2,1,0:T(8,128)(2,1)S(1)}, u32[]{:S(2)}, u32[]{:S(2)}) collective-permute-start(bf16[2,320,128]{2,1,0:T(8,128)(2,1)S(1)} %get-tuple-element.47), channel_id=1, source_target_pairs={{0,24},{8,16},{16,8},{24,0},{1,25},{9,17},{17,9},{25,1},{2,26},{10... | collective-permute-start | bytes 491528 | tf_op jit(solution)/shard_map/ppermute | solution.py:62
  97.2 2.8 %collective-permute-start.31 = (bf16[2,40,960]{2,1,0:T(8,128)(2,1)S(1)}, bf16[2,40,960]{2,1,0:T(8,128)(2,1)S(1)}, u32[]{:S(2)}, u32[]{:S(2)}) collective-permute-start(bf16[2,40,960]{2,1,0:T(8,128)(2,1)S(1)} %shard_map.87.keep_ref), channel_id=1, source_target_pairs={{0,4},{1,5},{2,6},{3,7},{4,0},{5,1},{6,2},{7,3},{8,12},{9,13},{10,... | collective-permute-start | bytes 460808 | tf_op jit(solution)/shard_map/ppermute | solution.py:62
  100.5 2.7 %collective-permute-done.16.refs_2_ = bf16[2,320,128]{2,1,0:T(8,128)(2,1)S(1)} collective-permute-done((bf16[2,320,128]{2,1,0:T(8,128)(2,1)S(1)}, bf16[2,320,128]{2,1,0:T(8,128)(2,1)S(1)}, u32[]{:S(2)}, u32[]{:S(2)}) %collective-permute-start.16) | collective-permute-done | bytes 163872 | tf_op jit(solution)/shard_map/ppermute | solution.py:62
  104.2 1.6 %collective-permute-done.31.other_ref = bf16[2,40,960]{2,1,0:T(8,128)(2,1)S(1)} collective-permute-done((bf16[2,40,960]{2,1,0:T(8,128)(2,1)S(1)}, bf16[2,40,960]{2,1,0:T(8,128)(2,1)S(1)}, u32[]{:S(2)}, u32[]{:S(2)}) %collective-permute-start.31) | collective-permute-done | bytes 153632 | tf_op jit(solution)/shard_map/ppermute | solution.py:62
  106.6 4.6 %collective-permute-done.32.next_ref = bf16[2,40,960]{2,1,0:T(8,128)(2,1)S(1)} collective-permute-done((bf16[2,40,960]{2,1,0:T(8,128)(2,1)S(1)}, bf16[2,40,960]{2,1,0:T(8,128)(2,1)S(1)}, u32[]{:S(2)}, u32[]{:S(2)}) %collective-permute-start.32) | collective-permute-done | bytes 153632 | tf_op jit(solution)/shard_map/ppermute | solution.py:62
  111.2 1.4 %collective-permute-done.34.both_ref = bf16[2,40,960]{2,1,0:T(8,128)(2,1)S(1)} collective-permute-done((bf16[2,40,960]{2,1,0:T(8,128)(2,1)S(1)}, bf16[2,40,960]{2,1,0:T(8,128)(2,1)S(1)}, u32[]{:S(2)}, u32[]{:S(2)}) %collective-permute-start.34) | collective-permute-done | bytes 153632 | tf_op jit(solution)/shard_map/ppermute | solution.py:62
  (92 shorter events, 24.9 us)
Async XLA Ops:
  0.7 37.5 %all-to-all-start = ((bf16[4,2,320,128]{3,2,1,0:T(8,128)(2,1)}), bf16[4,2,320,128]{3,2,1,0:T(8,128)(2,1)}, u32[]{:S(2)}, u32[]{:S(2)}) async-start(bf16[4,2,320,128]{3,2,1,0:T(8,128)(2,1)} %bitcast.8), calls=%async_computation | async-start | bytes 1310720 | tf_op jit(solution)/shard_map/all_to_all | solution.py:566
  7.2 13.5 %collective-permute-start = (bf16[3,80,320]{2,1,0:T(8,128)(2,1)S(1)}, bf16[3,80,320]{2,1,0:T(8,128)(2,1)S(1)}, u32[]{:S(2)}, u32[]{:S(2)}) collective-permute-start(bf16[3,80,320]{2,1,0:T(8,128)(2,1)S(1)} %get-tuple-element.75), channel_id=1, source_target_pairs={{0,8},{8,0},{16,24},{24,16},{1,9},{9,1},{17,25},{25,17},{2,10},{10... | collective-permute-start | bytes 460808 | tf_op jit(solution)/shard_map/ppermute | solution.py:62
  9.3 12.9 %collective-permute-start.1 = (bf16[3,80,320]{2,1,0:T(8,128)(2,1)S(1)}, bf16[3,80,320]{2,1,0:T(8,128)(2,1)S(1)}, u32[]{:S(2)}, u32[]{:S(2)}) collective-permute-start(bf16[3,80,320]{2,1,0:T(8,128)(2,1)S(1)} %get-tuple-element.75), channel_id=1, source_target_pairs={{0,16},{8,24},{16,0},{24,8},{1,17},{9,25},{17,1},{25,9},{2,18},{10... | collective-permute-start | bytes 460808 | tf_op jit(solution)/shard_map/ppermute | solution.py:62
  10.8 14.9 %collective-permute-start.2 = (bf16[3,80,320]{2,1,0:T(8,128)(2,1)S(1)}, bf16[3,80,320]{2,1,0:T(8,128)(2,1)S(1)}, u32[]{:S(2)}, u32[]{:S(2)}) collective-permute-start(bf16[3,80,320]{2,1,0:T(8,128)(2,1)S(1)} %get-tuple-element.75), channel_id=1, source_target_pairs={{0,24},{8,16},{16,8},{24,0},{1,25},{9,17},{17,9},{25,1},{2,26},{10... | collective-permute-start | bytes 460808 | tf_op jit(solution)/shard_map/ppermute | solution.py:62
  10.8 18.0 %collective-permute-start.6 = (bf16[3,80,320]{2,1,0:T(8,128)(2,1)S(1)}, bf16[3,80,320]{2,1,0:T(8,128)(2,1)}, u32[]{:S(2)}, u32[]{:S(2)}) collective-permute-start(bf16[3,80,320]{2,1,0:T(8,128)(2,1)S(1)} %get-tuple-element.74), channel_id=1, source_target_pairs={{0,8},{8,0},{16,24},{24,16},{1,9},{9,1},{17,25},{25,17},{2,10},{10... | collective-permute-start | bytes 460808 | tf_op jit(solution)/shard_map/ppermute | solution.py:62
  12.8 16.0 %collective-permute-start.7 = (bf16[3,80,320]{2,1,0:T(8,128)(2,1)S(1)}, bf16[3,80,320]{2,1,0:T(8,128)(2,1)}, u32[]{:S(2)}, u32[]{:S(2)}) collective-permute-start(bf16[3,80,320]{2,1,0:T(8,128)(2,1)S(1)} %get-tuple-element.74), channel_id=1, source_target_pairs={{0,16},{8,24},{16,0},{24,8},{1,17},{9,25},{17,1},{25,9},{2,18},{10... | collective-permute-start | bytes 460808 | tf_op jit(solution)/shard_map/ppermute | solution.py:62
  20.7 12.0 %collective-permute-start.8 = (bf16[3,80,320]{2,1,0:T(8,128)(2,1)S(1)}, bf16[3,80,320]{2,1,0:T(8,128)(2,1)}, u32[]{:S(2)}, u32[]{:S(2)}) collective-permute-start(bf16[3,80,320]{2,1,0:T(8,128)(2,1)S(1)} %get-tuple-element.74), channel_id=1, source_target_pairs={{0,24},{8,16},{16,8},{24,0},{1,25},{9,17},{17,9},{25,1},{2,26},{10... | collective-permute-start | bytes 460808 | tf_op jit(solution)/shard_map/ppermute | solution.py:62
  22.2 10.5 %collective-permute-start.3 = (bf16[3,80,320]{2,1,0:T(8,128)(2,1)S(1)}, bf16[3,80,320]{2,1,0:T(8,128)(2,1)S(1)}, u32[]{:S(2)}, u32[]{:S(2)}) collective-permute-start(bf16[3,80,320]{2,1,0:T(8,128)(2,1)S(1)} %collective-permute-done.refs_2_.refs_1_), channel_id=1, source_target_pairs={{0,1},{1,0},{2,3},{3,2},{4,5},{5,4},{6,7},{7,6},{8,9},{9,8},{10,11... | collective-permute-start | bytes 460808 | tf_op jit(solution)/shard_map/ppermute | solution.py:62
  25.6 8.6 %collective-permute-start.4 = (bf16[3,80,320]{2,1,0:T(8,128)(2,1)S(1)}, bf16[3,80,320]{2,1,0:T(8,128)(2,1)S(1)}, u32[]{:S(2)}, u32[]{:S(2)}) collective-permute-start(bf16[3,80,320]{2,1,0:T(8,128)(2,1)S(1)} %collective-permute-done.1.refs_3_.refs_2_), channel_id=1, source_target_pairs={{0,1},{1,0},{2,3},{3,2},{4,5},{5,4},{6,7},{7,6},{8,9},{9,8},{10,11... | collective-permute-start | bytes 460808 | tf_op jit(solution)/shard_map/ppermute | solution.py:62
  28.8 5.6 %collective-permute-start.5 = (bf16[3,80,320]{2,1,0:T(8,128)(2,1)S(1)}, bf16[3,80,320]{2,1,0:T(8,128)(2,1)S(1)}, u32[]{:S(2)}, u32[]{:S(2)}) collective-permute-start(bf16[3,80,320]{2,1,0:T(8,128)(2,1)S(1)} %collective-permute-done.2.refs_4_.refs_3_), channel_id=1, source_target_pairs={{0,1},{1,0},{2,3},{3,2},{4,5},{5,4},{6,7},{7,6},{8,9},{9,8},{10,11... | collective-permute-start | bytes 460808 | tf_op jit(solution)/shard_map/ppermute | solution.py:62
  28.8 13.3 %collective-permute-start.9 = (bf16[3,80,320]{2,1,0:T(8,128)(2,1)}, bf16[3,80,320]{2,1,0:T(8,128)(2,1)}, u32[]{:S(2)}, u32[]{:S(2)}) collective-permute-start(bf16[3,80,320]{2,1,0:T(8,128)(2,1)} %collective-permute-done.6.refs_8_), channel_id=1, source_target_pairs={{0,1},{1,0},{2,3},{3,2},{4,5},{5,4},{6,7},{7,6},{8,9},{9,8},{10,11... | collective-permute-start | bytes 460808 | tf_op jit(solution)/shard_map/ppermute | solution.py:62
  32.7 10.3 %collective-permute-start.10 = (bf16[3,80,320]{2,1,0:T(8,128)(2,1)}, bf16[3,80,320]{2,1,0:T(8,128)(2,1)}, u32[]{:S(2)}, u32[]{:S(2)}) collective-permute-start(bf16[3,80,320]{2,1,0:T(8,128)(2,1)} %collective-permute-done.7.refs_9_), channel_id=1, source_target_pairs={{0,1},{1,0},{2,3},{3,2},{4,5},{5,4},{6,7},{7,6},{8,9},{9,8},{10,11... | collective-permute-start | bytes 460808 | tf_op jit(solution)/shard_map/ppermute | solution.py:62
  32.7 12.3 %collective-permute-start.11 = (bf16[3,80,320]{2,1,0:T(8,128)(2,1)}, bf16[3,80,320]{2,1,0:T(8,128)(2,1)}, u32[]{:S(2)}, u32[]{:S(2)}) collective-permute-start(bf16[3,80,320]{2,1,0:T(8,128)(2,1)} %collective-permute-done.8.refs_10_), channel_id=1, source_target_pairs={{0,1},{1,0},{2,3},{3,2},{4,5},{5,4},{6,7},{7,6},{8,9},{9,8},{10,11... | collective-permute-start | bytes 460808 | tf_op jit(solution)/shard_map/ppermute | solution.py:62
  34.2 34.0 %collective-permute-start.21 = (bf16[8,320,128]{2,1,0:T(8,128)(2,1)S(1)}, bf16[8,320,128]{2,1,0:T(8,128)(2,1)}, u32[]{:S(2)}, u32[]{:S(2)}) collective-permute-start(bf16[8,320,128]{2,1,0:T(8,128)(2,1)S(1)} %bitcast.6), channel_id=1, source_target_pairs={{0,1},{1,0},{2,3},{3,2},{4,5},{5,4},{6,7},{7,6},{8,9},{9,8},{10,11... | collective-permute-start | bytes 1966088 | tf_op jit(solution)/shard_map/ppermute | solution.py:62
  41.5 14.8 %collective-permute-start.18 = (bf16[2,320,128]{2,1,0:T(8,128)(2,1)S(1)}, bf16[2,320,128]{2,1,0:T(8,128)(2,1)S(1)}, u32[]{:S(2)}, u32[]{:S(2)}) collective-permute-start(bf16[2,320,128]{2,1,0:T(8,128)(2,1)S(1)} %get-tuple-element.51), channel_id=1, source_target_pairs={{0,8},{8,0},{16,24},{24,16},{1,9},{9,1},{17,25},{25,17},{2,10},{10... | collective-permute-start | bytes 491528 | tf_op jit(solution)/shard_map/ppermute | solution.py:62
  42.1 15.1 %collective-permute-start.19 = (bf16[2,320,128]{2,1,0:T(8,128)(2,1)S(1)}, bf16[2,320,128]{2,1,0:T(8,128)(2,1)S(1)}, u32[]{:S(2)}, u32[]{:S(2)}) collective-permute-start(bf16[2,320,128]{2,1,0:T(8,128)(2,1)S(1)} %get-tuple-element.52), channel_id=1, source_target_pairs={{0,16},{8,24},{16,0},{24,8},{1,17},{9,25},{17,1},{25,9},{2,18},{10... | collective-permute-start | bytes 491528 | tf_op jit(solution)/shard_map/ppermute | solution.py:62
  43.0 16.2 %collective-permute-start.20 = (bf16[2,320,128]{2,1,0:T(8,128)(2,1)S(1)}, bf16[2,320,128]{2,1,0:T(8,128)(2,1)S(1)}, u32[]{:S(2)}, u32[]{:S(2)}) collective-permute-start(bf16[2,320,128]{2,1,0:T(8,128)(2,1)S(1)} %get-tuple-element.53), channel_id=1, source_target_pairs={{0,24},{8,16},{16,8},{24,0},{1,25},{9,17},{17,9},{25,1},{2,26},{10... | collective-permute-start | bytes 491528 | tf_op jit(solution)/shard_map/ppermute | solution.py:62
  55.6 7.2 %collective-permute-start.12 = (bf16[2,320,128]{2,1,0:T(8,128)(2,1)S(1)}, bf16[2,320,128]{2,1,0:T(8,128)(2,1)S(1)}, u32[]{:S(2)}, u32[]{:S(2)}) collective-permute-start(bf16[2,320,128]{2,1,0:T(8,128)(2,1)S(1)} %get-tuple-element.40), channel_id=1, source_target_pairs={{0,8},{8,0},{16,24},{24,16},{1,9},{9,1},{17,25},{25,17},{2,10},{10... | collective-permute-start | bytes 491528 | tf_op jit(solution)/shard_map/ppermute | solution.py:62
  56.3 8.9 %collective-permute-start.13 = (bf16[2,320,128]{2,1,0:T(8,128)(2,1)S(1)}, bf16[2,320,128]{2,1,0:T(8,128)(2,1)S(1)}, u32[]{:S(2)}, u32[]{:S(2)}) collective-permute-start(bf16[2,320,128]{2,1,0:T(8,128)(2,1)S(1)} %get-tuple-element.41), channel_id=1, source_target_pairs={{0,16},{8,24},{16,0},{24,8},{1,17},{9,25},{17,1},{25,9},{2,18},{10... | collective-permute-start | bytes 491528 | tf_op jit(solution)/shard_map/ppermute | solution.py:62
  57.2 8.0 %collective-permute-start.14 = (bf16[2,320,128]{2,1,0:T(8,128)(2,1)S(1)}, bf16[2,320,128]{2,1,0:T(8,128)(2,1)S(1)}, u32[]{:S(2)}, u32[]{:S(2)}) collective-permute-start(bf16[2,320,128]{2,1,0:T(8,128)(2,1)S(1)} %get-tuple-element.42), channel_id=1, source_target_pairs={{0,24},{8,16},{16,8},{24,0},{1,25},{9,17},{17,9},{25,1},{2,26},{10... | collective-permute-start | bytes 491528 | tf_op jit(solution)/shard_map/ppermute | solution.py:62
  60.0 12.0 %collective-permute-start.22 = (bf16[160,1024]{1,0:T(8,128)(2,1)S(1)}, bf16[160,1024]{1,0:T(8,128)(2,1)S(1)}, u32[]{:S(2)}, u32[]{:S(2)}) collective-permute-start(bf16[160,1024]{1,0:T(8,128)(2,1)S(1)} %get-tuple-element.57), channel_id=1, source_target_pairs={{0,1},{1,0},{2,3},{3,2},{4,5},{5,4},{6,7},{7,6},{8,9},{9,8},{10,11... | collective-permute-start | bytes 983048 | tf_op jit(solution)/shard_map/ppermute | solution.py:62
  70.4 8.0 %collective-permute-start.27 = (bf16[40,960]{1,0:T(8,128)(2,1)S(1)}, bf16[40,960]{1,0:T(8,128)(2,1)S(1)}, u32[]{:S(2)}, u32[]{:S(2)}) collective-permute-start(bf16[40,960]{1,0:T(8,128)(2,1)S(1)} %get-tuple-element.66), channel_id=1, source_target_pairs={{0,8},{8,0},{16,24},{24,16},{1,9},{9,1},{17,25},{25,17},{2,10},{10... | collective-permute-start | bytes 230408 | tf_op jit(solution)/shard_map/ppermute | solution.py:62
  74.3 17.2 %collective-permute-start.24 = (bf16[3,40,960]{2,1,0:T(8,128)(2,1)S(1)}, bf16[3,40,960]{2,1,0:T(8,128)(2,1)S(1)}, u32[]{:S(2)}, u32[]{:S(2)}) collective-permute-start(bf16[3,40,960]{2,1,0:T(8,128)(2,1)S(1)} %get-tuple-element.63), channel_id=1, source_target_pairs={{0,8},{8,0},{16,24},{24,16},{1,9},{9,1},{17,25},{25,17},{2,10},{10... | collective-permute-start | bytes 691208 | tf_op jit(solution)/shard_map/ppermute | solution.py:62
  74.9 16.6 %collective-permute-start.25 = (bf16[3,40,960]{2,1,0:T(8,128)(2,1)S(1)}, bf16[3,40,960]{2,1,0:T(8,128)(2,1)S(1)}, u32[]{:S(2)}, u32[]{:S(2)}) collective-permute-start(bf16[3,40,960]{2,1,0:T(8,128)(2,1)S(1)} %get-tuple-element.64), channel_id=1, source_target_pairs={{0,16},{8,24},{16,0},{24,8},{1,17},{9,25},{17,1},{25,9},{2,18},{10... | collective-permute-start | bytes 691208 | tf_op jit(solution)/shard_map/ppermute | solution.py:62
  76.1 15.4 %collective-permute-start.26 = (bf16[3,40,960]{2,1,0:T(8,128)(2,1)S(1)}, bf16[3,40,960]{2,1,0:T(8,128)(2,1)S(1)}, u32[]{:S(2)}, u32[]{:S(2)}) collective-permute-start(bf16[3,40,960]{2,1,0:T(8,128)(2,1)S(1)} %get-tuple-element.65), channel_id=1, source_target_pairs={{0,24},{8,16},{16,8},{24,0},{1,25},{9,17},{17,9},{25,1},{2,26},{10... | collective-permute-start | bytes 691208 | tf_op jit(solution)/shard_map/ppermute | solution.py:62
  77.9 13.6 %collective-permute-start.28 = (bf16[40,960]{1,0:T(8,128)(2,1)S(1)}, bf16[40,960]{1,0:T(8,128)(2,1)S(1)}, u32[]{:S(2)}, u32[]{:S(2)}) collective-permute-start(bf16[40,960]{1,0:T(8,128)(2,1)S(1)} %get-tuple-element.67), channel_id=1, source_target_pairs={{0,16},{8,24},{16,0},{24,8},{1,17},{9,25},{17,1},{25,9},{2,18},{10... | collective-permute-start | bytes 230408 | tf_op jit(solution)/shard_map/ppermute | solution.py:62
  78.4 13.1 %collective-permute-start.29 = (bf16[40,960]{1,0:T(8,128)(2,1)S(1)}, bf16[40,960]{1,0:T(8,128)(2,1)S(1)}, u32[]{:S(2)}, u32[]{:S(2)}) collective-permute-start(bf16[40,960]{1,0:T(8,128)(2,1)S(1)} %get-tuple-element.68), channel_id=1, source_target_pairs={{0,24},{8,16},{16,8},{24,0},{1,25},{9,17},{17,9},{25,1},{2,26},{10... | collective-permute-start | bytes 230408 | tf_op jit(solution)/shard_map/ppermute | solution.py:62
  91.7 5.4 %collective-permute-start.30 = (bf16[2,40,960]{2,1,0:T(8,128)(2,1)S(1)}, bf16[2,40,960]{2,1,0:T(8,128)(2,1)S(1)}, u32[]{:S(2)}, u32[]{:S(2)}) collective-permute-start(bf16[2,40,960]{2,1,0:T(8,128)(2,1)S(1)} %get-tuple-element.70), channel_id=1, source_target_pairs={{0,2},{1,3},{2,0},{3,1},{4,6},{5,7},{6,4},{7,5},{8,10},{9,11},{10,... | collective-permute-start | bytes 460808 | tf_op jit(solution)/shard_map/ppermute | solution.py:62
  93.6 6.9 %collective-permute-start.15 = (bf16[2,320,128]{2,1,0:T(8,128)(2,1)S(1)}, bf16[2,320,128]{2,1,0:T(8,128)(2,1)S(1)}, u32[]{:S(2)}, u32[]{:S(2)}) collective-permute-start(bf16[2,320,128]{2,1,0:T(8,128)(2,1)S(1)} %get-tuple-element.45), channel_id=1, source_target_pairs={{0,8},{8,0},{16,24},{24,16},{1,9},{9,1},{17,25},{25,17},{2,10},{10... | collective-permute-start | bytes 491528 | tf_op jit(solution)/shard_map/ppermute | solution.py:62
  95.1 8.1 %collective-permute-start.16 = (bf16[2,320,128]{2,1,0:T(8,128)(2,1)S(1)}, bf16[2,320,128]{2,1,0:T(8,128)(2,1)S(1)}, u32[]{:S(2)}, u32[]{:S(2)}) collective-permute-start(bf16[2,320,128]{2,1,0:T(8,128)(2,1)S(1)} %get-tuple-element.46), channel_id=1, source_target_pairs={{0,16},{8,24},{16,0},{24,8},{1,17},{9,25},{17,1},{25,9},{2,18},{10... | collective-permute-start | bytes 491528 | tf_op jit(solution)/shard_map/ppermute | solution.py:62
  95.6 7.6 %collective-permute-start.17 = (bf16[2,320,128]{2,1,0:T(8,128)(2,1)S(1)}, bf16[2,320,128]{2,1,0:T(8,128)(2,1)S(1)}, u32[]{:S(2)}, u32[]{:S(2)}) collective-permute-start(bf16[2,320,128]{2,1,0:T(8,128)(2,1)S(1)} %get-tuple-element.47), channel_id=1, source_target_pairs={{0,24},{8,16},{16,8},{24,0},{1,25},{9,17},{17,9},{25,1},{2,26},{10... | collective-permute-start | bytes 491528 | tf_op jit(solution)/shard_map/ppermute | solution.py:62
  97.2 8.6 %collective-permute-start.31 = (bf16[2,40,960]{2,1,0:T(8,128)(2,1)S(1)}, bf16[2,40,960]{2,1,0:T(8,128)(2,1)S(1)}, u32[]{:S(2)}, u32[]{:S(2)}) collective-permute-start(bf16[2,40,960]{2,1,0:T(8,128)(2,1)S(1)} %shard_map.87.keep_ref), channel_id=1, source_target_pairs={{0,4},{1,5},{2,6},{3,7},{4,0},{5,1},{6,2},{7,3},{8,12},{9,13},{10,... | collective-permute-start | bytes 460808 | tf_op jit(solution)/shard_map/ppermute | solution.py:62
  (22 other events, 134.7 us)

commit v3 on v2

v3 whole, which is shorter than its diff:
```python
import math

import jax
import jax.numpy as jnp
from jax import lax
from jax.experimental import pallas as pl
from jax.experimental.pallas import tpu as pltpu
from jax.sharding import PartitionSpec as P

BF = jnp.bfloat16
F32 = jnp.float32
VMEM_LIMIT = 24 * 1024 * 1024
NT = (((1,), (1,)), ((), ()))


def call(body, outs, scratch, flops, *args, far=(), sent=(), light=False):
    def spec(i):
        return pl.BlockSpec(memory_space=pltpu.HBM if i in far else pltpu.VMEM)

    args = [
        pltpu.with_memory_space_constraint(arg, pltpu.HBM) if i in far else arg
        for i, arg in enumerate(args)
    ]
    factor = 0 if light else 10
    moved = sum(x.size * x.dtype.itemsize for x in (*args, *outs))
    return pl.pallas_call(
        body,
        out_shape=tuple(
            pltpu.HBM(out.shape, out.dtype) if len(args) + i in (*far, *sent) else out
            for i, out in enumerate(outs)
        ),
        in_specs=[spec(i) for i in range(len(args))],
        out_specs=tuple(spec(len(args) + i) for i in range(len(outs))),
        scratch_shapes=scratch,
        compiler_params=pltpu.CompilerParams(vmem_limit_bytes=VMEM_LIMIT),
        cost_estimate=pl.CostEstimate(flops=factor * flops + 1, bytes_accessed=factor * moved + 1, transcendentals=0),
    )(*args)


def shape(dims, dtype=BF):
    return jax.ShapeDtypeStruct(tuple(dims), dtype)


def columns(first, count, width):
    return pl.ds(pl.multiple_of(first * width, width), count * width)


def place(step):
    return jnp.bitwise_xor(lax.axis_index("seq"), step)


def core():
    return lax.rem(lax.axis_index("dp"), 2)


def pair_bit():
    return lax.rem(lax.div(lax.axis_index("dp"), 2), 2)


def at_block(index, size, count, tile, use):
    if size % tile == 0:
        use(pl.ds(pl.multiple_of(index * size, size), size))
        return
    for fixed in range(count):

        @pl.when(index == fixed)
        def _():
            use(pl.ds(fixed * size, size))


def swap(values, axis, bit):
    size = lax.axis_size(axis)
    return lax.ppermute(values, axis, [(i, i ^ bit) for i in range(size)])


def spread(blocks):
    return [swap(block, "seq", j + 1) for j, block in enumerate(blocks)]


def exchange(blocks):
    return lax.all_to_all(blocks, "seq", 0, 0, tiled=True)


def after(value, *others):
    return lax.optimization_barrier((value, *others))[0]


def shifted(block, step):
    if step == 0:
        return block
    width = block.shape[1]
    rolled = pltpu.roll(block.astype(F32), (-step) % width, 1)
    column = lax.broadcasted_iota(jnp.int32, block.shape, 1)
    edge = 0 if step < 0 else width - 1
    return jnp.where(column == edge, 0.0, rolled).astype(block.dtype)


def fill_taps(target, source, order):
    rows, chans, width = source.shape
    target[:, :width] = jnp.zeros((target.shape[0], width), target.dtype)
    target[:, (rows + 1) * width :] = jnp.zeros((target.shape[0], width), target.dtype)

    def row(y, carry):
        block = source[y]
        for b, step in enumerate(order):
            target[b * chans : (b + 1) * chans, columns(y + 1, 1, width)] = shifted(block, step)
        return carry

    lax.fori_loop(0, rows, row, 0)


def transposed(block):
    size = block.shape[0]
    one = lax.broadcasted_iota(jnp.int32, (size, size), 0) == lax.broadcasted_iota(
        jnp.int32, (size, size), 1
    )
    return lax.dot_general(one.astype(BF), block, NT, preferred_element_type=F32).astype(BF)


def window_taps(frames, light=False):
    rows, chans, width = frames.shape
    dims = (3 * chans, (rows + 2) * width)

    def body(frames_ref, far_ref, taps_ref, done):
        fill_taps(taps_ref, frames_ref, (-1, 0, 1))
        copy = pltpu.make_async_copy(taps_ref, far_ref, done)
        copy.start()
        copy.wait()

    return call(
        body,
        [shape(dims)],
        [pltpu.VMEM(dims, BF), pltpu.SemaphoreType.DMA],
        frames.size,
        frames,
        far=(1,),
        light=light,
    )[0]


def kernel_maps(own, spatial, first, second):
    _, shard, chans = own.shape
    count = len(first)

    def body(*refs):
        own_ref, spatial_ref = refs[:2]
        mine, theirs = refs[2 : 2 + count], refs[2 + count : 2 + 2 * count]
        far_trans, far_plain, far_mid, *refs = refs[2 + 2 * count :]
        trans_ref, plain_ref, mid_ref, rows_ref, done = refs

        def fill_mid(pieces):
            for j, piece in enumerate((spatial_ref, *pieces)):

                def put(at):
                    for b in range(3):
                        source = piece[3 + b] if j == 0 else piece[b]
                        mid_ref[at, b * chans : (b + 1) * chans] = source

                at_block(place(j), shard, count + 1, 16, put)

        def fill(pieces):
            for j, piece in enumerate((own_ref, *pieces)):

                def put(at):
                    for k in range(3):
                        rows_ref[k, at, :] = piece[k]

                at_block(place(j), shard, count + 1, 16, put)

        @pl.when(core() == 0)
        def _():
            fill(mine)
            fill_mid(theirs)

        @pl.when(core() == 1)
        def _():
            fill(theirs)
            fill_mid(mine)

        for k in range(3):
            plain_ref[:, k * chans : (k + 1) * chans] = rows_ref[k]
        for k in range(3):
            trans_ref[:, k * chans : (k + 1) * chans] = transposed(rows_ref[k])
        copies = [
            pltpu.make_async_copy(near, far, done.at[i])
            for i, (near, far) in enumerate(
                ((trans_ref, far_trans), (plain_ref, far_plain), (mid_ref, far_mid))
            )
        ]
        for copy in copies:
            copy.start()
        for copy in copies:
            copy.wait()

    return call(
        body,
        [shape((chans, 3 * chans))] * 3,
        [
            pltpu.VMEM((chans, 3 * chans), BF),
            pltpu.VMEM((chans, 3 * chans), BF),
            pltpu.VMEM((chans, 3 * chans), BF),
            pltpu.VMEM((3, chans, chans), BF),
            pltpu.SemaphoreType.DMA((3,)),
        ],
        6 * chans**3,
        own,
        spatial,
        *first,
        *second,
        far=(2 + 2 * count, 3 + 2 * count, 4 + 2 * count),
    )


def temporal_backward(cot_rows, weights_t):
    frames, rows, chans, width = cot_rows.shape
    span = rows * width

    def body(cot_ref, far_ref, out_ref, weights_ref, taps_ref, done):
        load = pltpu.make_async_copy(far_ref, weights_ref, done)
        load.start()
        edge = jnp.zeros((chans, span), BF)
        taps_ref[:chans, (frames - 1) * span :] = edge
        taps_ref[2 * chans :, :span] = edge
        for f in range(frames):
            for k in range(3):
                at = f + k - 1
                if 0 <= at < frames:
                    for y in range(rows):
                        to = at * span + y * width
                        taps_ref[k * chans : (k + 1) * chans, to : to + width] = cot_ref[f, y]
        load.wait()
        for f in range(frames):
            total = jnp.dot(
                weights_ref[...],
                taps_ref[:, f * span : (f + 1) * span],
                preferred_element_type=F32,
            ).astype(BF)
            for y in range(rows):
                out_ref[f, y] = total[:, y * width : (y + 1) * width]

    return call(
        body,
        [shape(cot_rows.shape)],
        [
            pltpu.VMEM(weights_t.shape, BF),
            pltpu.VMEM((3 * chans, frames * span), BF),
            pltpu.SemaphoreType.DMA,
        ],
        6 * chans * cot_rows.size,
        cot_rows,
        weights_t,
        far=(1,),
        sent=(2,),
    )[0]


def spatial_forward(taps, own, middle, pieces, rows):
    _, shard, chans = own.shape
    width = taps.shape[1] // (rows + 2)
    count = len(pieces)
    owners = count // 2 + 1
    tiles = rows // 2

    def body(*refs):
        far_taps, far_middle, far_sources = refs[0], refs[1], refs[2 : 3 + count]
        pre_ref, far_act, far_weights, taps_ref, act_ref, weights_ref, done = refs[3 + count : -2]
        own_ref, pieces_ref = refs[-2:]
        sources = [own_ref] + [pieces_ref.at[i] for i in range(count)]
        fetched = [
            pltpu.make_async_copy(far, near, done.at[tiles + 2 + i])
            for i, (far, near) in enumerate(zip(far_sources, sources))
        ]
        for copy in fetched:
            copy.start()
        middle_load = pltpu.make_async_copy(far_middle, weights_ref.at[1], done.at[tiles + 1])
        middle_load.start()

        def load(i):
            at = columns(2 * i, 2, width)
            return pltpu.make_async_copy(far_taps.at[:, at], taps_ref.at[:, at], done.at[i])

        def start(i, carry):
            load(i).start()
            return carry

        lax.fori_loop(0, tiles + 1, start, 0)

        for copy in fetched:
            copy.wait()
        lists = [sources[1 + i * (owners - 1) : 1 + (i + 1) * (owners - 1)] for i in range(2)]
        for side, order in enumerate(((0, 1), (1, 0))):

            @pl.when(core() == side)
            def _():
                for j in range(owners):

                    def put(at):
                        for a in (0, 2):
                            for b in range(3):
                                if j == 0:
                                    value = sources[0][3 * a + b]
                                else:
                                    value = lists[order[a // 2]][j - 1][b]
                                weights_ref[a, at, b * chans : (b + 1) * chans] = value

                    at_block(place(j), shard, owners, 16, put)

        middle_load.wait()
        store = pltpu.make_async_copy(weights_ref, far_weights, done.at[tiles + 1])
        store.start()
        load(jnp.int32(0)).wait()

        def act_store(i):
            at = pl.ds(2 * i, 2)
            return pltpu.make_async_copy(act_ref.at[at], far_act.at[at], done.at[i])

        def tile(i, carry):
            load(i + 1).wait()
            total = jnp.zeros((chans, 2 * width), F32)
            for a in range(3):
                total += jnp.dot(
                    weights_ref[a],
                    taps_ref[:, columns(2 * i + a, 2, width)],
                    preferred_element_type=F32,
                )
            pre = total.astype(BF)
            wide = pre.astype(F32)
            act = (wide / (1.0 + jnp.exp(-wide))).astype(BF)
            for r in range(2):
                pre_ref[2 * i + r] = pre[:, r * width : (r + 1) * width]
                act_ref[2 * i + r] = act[:, r * width : (r + 1) * width]
            act_store(i).start()
            return carry

        lax.fori_loop(0, tiles, tile, 0)

        def finish(i, carry):
            act_store(i).wait()
            return carry

        lax.fori_loop(0, tiles, finish, 0)
        store.wait()

    return call(
        body,
        [shape((rows, chans, width)), shape((rows, chans, width)), shape((3, chans, 3 * chans))],
        [
            pltpu.VMEM(taps.shape, BF),
            pltpu.VMEM((rows, chans, width), BF),
            pltpu.VMEM((3, chans, 3 * chans), BF),
            pltpu.SemaphoreType.DMA((tiles + 3 + count,)),
            pltpu.VMEM(own.shape, BF),
            pltpu.VMEM((count, 3, shard, chans), BF),
        ],
        18 * chans * chans * rows * width,
        taps,
        middle,
        own,
        *pieces,
        far=(*range(3 + count), 4 + count, 5 + count),
    )


def activation_grad(pre_act, act_grad, shard):
    rows, chans, width = pre_act.shape
    half = shard // 2

    def body(pre_ref, act_ref, mine_ref, theirs_ref, far_ref, pg_ref, done):
        def row(y, carry):
            wide = pre_ref[y].astype(F32)
            s = 1.0 / (1.0 + jnp.exp(-wide))
            pg = act_ref[y].astype(F32) * s * (1.0 + wide * (1.0 - s))
            pg_ref[y] = pg.astype(BF)
            low = [pg[at : at + half] for at in range(0, chans, shard)]
            high = [pg[at + half : at + shard] for at in range(0, chans, shard)]
            low = jnp.concatenate(low).astype(BF)
            high = jnp.concatenate(high).astype(BF)
            first = core() == 0
            mine_ref[:, columns(y, 1, width)] = jnp.where(first, low, high)
            theirs_ref[:, columns(y, 1, width)] = jnp.where(first, high, low)
            return carry

        copies = []
        for i in range(2):
            lax.fori_loop(i * rows // 2, (i + 1) * rows // 2, row, 0)
            at = pl.ds(i * rows // 2, rows // 2)
            copies.append(pltpu.make_async_copy(pg_ref.at[at], far_ref.at[at], done.at[i]))
            copies[i].start()
        for copy in copies:
            copy.wait()

    return call(
        body,
        [shape((chans // 2, rows * width))] * 2 + [shape(pre_act.shape)],
        [pltpu.VMEM(pre_act.shape, BF), pltpu.SemaphoreType.DMA((2,))],
        20 * pre_act.size,
        pre_act,
        act_grad,
        far=(4,),
    )


def spatial_weight_grad(taps, other_taps, half_grad, other_half, owners, scale, rows):
    wide = taps.shape[0]
    chans, span = half_grad.shape
    width = span // rows
    part = chans // owners

    def body(far_taps, far_other, mine_ref, theirs_ref, *refs):
        keep_ref, sends = refs[0], refs[1:owners]
        stack_ref, taps_ref, total_ref, done = refs[owners:]
        loads = [
            pltpu.make_async_copy(far, taps_ref.at[q], done.at[q])
            for q, far in enumerate((far_taps, far_other))
        ]
        for copy in loads:
            copy.start()
        edge = jnp.zeros((chans, width), BF)
        for q, source in enumerate((mine_ref, theirs_ref)):
            at = q * span
            stack_ref[:chans, at + span - width : at + span] = edge
            stack_ref[:chans, at : at + span - width] = source[:, width:]
            stack_ref[chans : 2 * chans, at : at + span] = source[...]
            stack_ref[2 * chans :, at : at + width] = edge
            stack_ref[2 * chans :, at + width : at + span] = source[:, : span - width]
        total = jnp.zeros((3 * chans, wide), F32)
        for q, copy in enumerate(loads):
            copy.wait()
            total += lax.dot_general(
                stack_ref[:, q * span : (q + 1) * span],
                taps_ref[q, :, width : width + span],
                NT,
                preferred_element_type=F32,
            )
        for a in range(3):
            total_ref[a] = total[a * chans : (a + 1) * chans] * scale
        for j in range(owners):

            def put(at):
                for a in range(3):
                    value = total_ref[a, at, :]
                    if j == 0:
                        keep_ref[a] = value
                    else:
                        sends[j - 1][a] = value.astype(BF)

            at_block(place(j), part, owners, 8, put)

    return call(
        body,
        [shape((3, part, wide), F32)] + [shape((3, part, wide))] * (owners - 1),
        [
            pltpu.VMEM((3 * chans, 2 * span), BF),
            pltpu.VMEM((2,) + taps.shape, BF),
            pltpu.VMEM((3, chans, wide), F32),
            pltpu.SemaphoreType.DMA((2,)),
        ],
        12 * chans * wide * span,
        taps,
        other_taps,
        half_grad,
        other_half,
        far=(0, 1),
        sent=tuple(range(5, 4 + owners)),
        light=True,
    )


def spatial_backward(pre_grad, cotangent, weights):
    rows, chans, width = pre_grad.shape

    def body(far_pg, far_cot, far_weights, out_ref, *refs):
        pg_ref, cot_ref, weights_ref, taps_ref, trans_ref, done = refs
        loads = [
            pltpu.make_async_copy(far, near, done.at[i])
            for i, (far, near) in enumerate(
                ((far_pg, pg_ref), (far_weights, weights_ref), (far_cot, cot_ref))
            )
        ]
        for copy in loads:
            copy.start()
        loads[0].wait()
        fill_taps(taps_ref, pg_ref, (1, 0, -1))
        loads[1].wait()
        for a in range(3):
            for b in range(3):
                at = slice(b * chans, (b + 1) * chans)
                trans_ref[a, :, at] = transposed(weights_ref[a, :, at])
        loads[2].wait()

        def tile(i, carry):
            total = jnp.zeros((chans, 2 * width), F32)
            for a in range(3):
                total += jnp.dot(
                    trans_ref[a],
                    taps_ref[:, columns(2 * i + 2 - a, 2, width)],
                    preferred_element_type=F32,
                )
            for r in range(2):
                wide = cot_ref[2 * i + r].astype(F32)
                out_ref[2 * i + r] = (wide + total[:, r * width : (r + 1) * width]).astype(BF)
            return carry

        lax.fori_loop(0, rows // 2, tile, 0)

    return call(
        body,
        [shape(pre_grad.shape)],
        [
            pltpu.VMEM(pre_grad.shape, BF),
            pltpu.VMEM(pre_grad.shape, BF),
            pltpu.VMEM((3, chans, 3 * chans), BF),
            pltpu.VMEM((3 * chans, (rows + 2) * width), BF),
            pltpu.VMEM((3, chans, 3 * chans), BF),
            pltpu.SemaphoreType.DMA((3,)),
        ],
        18 * chans * chans * rows * width,
        pre_grad,
        cotangent,
        weights,
        far=(0, 1, 2),
    )[0]


def temporal_forward(acts, cot_rows, weights, shard, scale):
    frames, rows, chans, width = cot_rows.shape
    span = rows * width
    half = shard // 2

    def body(act_ref, cot_ref, far_ref, out_ref, keep_ref, send_ref, *refs):
        weights_ref, taps_ref, cots_ref, done = refs
        load = pltpu.make_async_copy(far_ref, weights_ref, done)
        load.start()
        edge = jnp.zeros((chans, span), BF)
        taps_ref[:chans, :span] = edge
        taps_ref[2 * chans :, (frames - 1) * span :] = edge
        for f in range(frames):
            for y in range(rows):
                at = f * span + y * width
                cots_ref[:, at : at + width] = cot_ref[f, y]
                for k in range(3):
                    if 0 <= f - k + 1 < frames:
                        to = at + (1 - k) * span
                        taps_ref[k * chans : (k + 1) * chans, to : to + width] = act_ref[f, y]
        load.wait()
        for f in range(frames):
            total = jnp.dot(
                weights_ref[...],
                taps_ref[:, f * span : (f + 1) * span],
                preferred_element_type=F32,
            ).astype(BF)
            for y in range(rows):
                out_ref[f, y] = total[:, y * width : (y + 1) * width]
        total = (
            lax.dot_general(cots_ref[...], taps_ref[...], NT, preferred_element_type=F32) * scale
        )
        first = core() == 0
        for s in range(chans // shard):
            low = total[s * shard : s * shard + half]
            high = total[s * shard + half : (s + 1) * shard]
            keep_ref[s] = jnp.where(first, low, high)
            send_ref[s] = jnp.where(first, high, low).astype(BF)

    owners = chans // shard
    return call(
        body,
        [
            shape(cot_rows.shape),
            shape((owners, half, 3 * chans), F32),
            shape((owners, half, 3 * chans)),
        ],
        [
            pltpu.VMEM(weights.shape, BF),
            pltpu.VMEM((3 * chans, frames * span), BF),
            pltpu.VMEM((chans, frames * span), BF),
            pltpu.SemaphoreType.DMA,
        ],
        12 * chans * cot_rows.size,
        acts,
        cot_rows,
        weights,
        far=(2,),
        sent=(3,),
    )


def owner_sum(spatial, others, temporal):
    _, half, wide = spatial.shape
    count = len(others)

    def body(spatial_ref, temporal_ref, *refs):
        other_refs, (keep_ref, send_ref, sum_ref) = refs[:count], refs[count:]
        for a in range(3):
            value = spatial_ref[a]
            for ref in other_refs:
                value += ref[a].astype(F32)
            sum_ref[a] = value
        value = temporal_ref[0].astype(F32)
        for s in range(1, count + 1):
            value += temporal_ref[s].astype(F32)
        sum_ref[3] = value
        bit = pair_bit()
        keep_ref[...] = sum_ref[pl.ds(2 * bit, 2)]
        send_ref[...] = sum_ref[pl.ds(2 - 2 * bit, 2)].astype(BF)

    return call(
        body,
        [shape((2, half, wide), F32), shape((2, half, wide))],
        [pltpu.VMEM((4, half, wide), F32)],
        4 * spatial.size,
        spatial,
        temporal,
        *others,
    )


def add_rounded(keep, other):
    def body(keep_ref, other_ref, out_ref):
        out_ref[...] = (keep_ref[...].astype(F32) + other_ref[...].astype(F32)).astype(BF)

    return call(body, [shape(keep.shape)], [], keep.size, keep, other)[0]


def kernel_outputs(parts, chans):
    _, half, wide = parts[0].shape

    def body(own_ref, next_ref, core_ref, both_ref, spatial_ref, temporal_ref, sum_ref):
        bit, mine = pair_bit(), core()
        for ref, group, side in (
            (own_ref, bit, mine),
            (next_ref, 1 - bit, mine),
            (core_ref, bit, 1 - mine),
            (both_ref, 1 - bit, 1 - mine),
        ):

            def put(at):
                for g in range(2):
                    sum_ref[2 * group + g, at, :] = ref[g].astype(F32)

            at_block(side, half, 2, 8, put)
        for a in range(3):
            for b in range(3):
                spatial_ref[3 * a + b] = sum_ref[a, :, b * chans : (b + 1) * chans]
        for k in range(3):
            temporal_ref[k] = sum_ref[3, :, k * chans : (k + 1) * chans]

    return call(
        body,
        [shape((9, 2 * half, chans), F32), shape((3, 2 * half, chans), F32)],
        [pltpu.VMEM((4, 2 * half, wide), F32)],
        8 * parts[0].size,
        *parts,
    )


def block_output(frames, temporal):
    def body(frames_ref, temporal_ref, out_ref):
        out_ref[...] = (frames_ref[...].astype(F32) + temporal_ref[...].astype(F32)).astype(BF)

    return call(body, [shape(frames.shape)], [], frames.size, frames, temporal)[0]


def local(frames_in, spatial_kernel, temporal_kernel, out_cotangent):
    frames, cotangent = frames_in[0, 0], out_cotangent[0, 0]
    rows, chans, width = frames.shape
    seq, dp = lax.axis_size("seq"), lax.axis_size("dp")
    shard = spatial_kernel.shape[1]
    scale = 1.0 / math.sqrt(dp * seq * rows * width)

    first = core() == 0
    mine_a = jnp.where(first, temporal_kernel, spatial_kernel[3:6])
    mine_b = jnp.where(first, spatial_kernel[:3], spatial_kernel[6:])
    got_a = spread([mine_a] * (seq - 1))
    cot_rows = exchange(cotangent.reshape(seq, rows // seq, chans, width))
    got_b = spread([mine_b] * (seq - 1))
    pair_a = [swap(piece, "dp", 1) for piece in got_a]
    temporal_t, temporal_w, middle = kernel_maps(
        temporal_kernel, spatial_kernel, got_a, pair_a
    )
    taps = window_taps(frames)
    temporal_t, taps = lax.optimization_barrier((temporal_t, taps))
    grad_rows = temporal_backward(cot_rows, temporal_t)
    act_grad = exchange(grad_rows).reshape(frames.shape)
    grad_rows, *got_b = lax.optimization_barrier((grad_rows, *got_b))
    pair_b = [swap(piece, "dp", 1) for piece in got_b]
    other_frames = swap(after(frames, middle), "dp", 1)
    pre_act, activated, weights = spatial_forward(
        taps, spatial_kernel, middle, (*got_b, *pair_b), rows
    )
    half_mine, half_theirs, pre_grad = activation_grad(pre_act, act_grad, shard)
    half_other = swap(half_theirs, "dp", 1)
    other_taps = window_taps(after(other_frames, half_theirs), light=True)
    act_rows = exchange(activated.reshape(cot_rows.shape))
    spatial_keep, *spatial_send = spatial_weight_grad(
        taps, other_taps, half_mine, half_other, seq, scale, rows
    )
    spatial_got = spread(spatial_send)
    temporal_rows, temporal_keep, temporal_send = temporal_forward(
        act_rows, cot_rows, after(temporal_w, spatial_keep), shard, scale
    )
    temporal_part = exchange(add_rounded(temporal_keep, swap(temporal_send, "dp", 1)))
    keep, send = owner_sum(spatial_keep, spatial_got, temporal_part)
    temporal_rows = exchange(after(temporal_rows, keep)).reshape(frames.shape)
    total = add_rounded(keep, swap(send, "dp", 2))
    input_grad = spatial_backward(after(pre_grad, keep), cotangent, weights)
    bit = 4
    while bit < dp:
        other = swap(total, "dp", bit)
        total = add_rounded(after(total, input_grad), other)
        bit *= 2
    block_out = block_output(frames, temporal_rows)
    near = swap(total, "dp", 2)
    near, block_out = lax.optimization_barrier((near, block_out))
    spatial_grad, temporal_grad = kernel_outputs(
        (total, near, swap(total, "dp", 1), swap(near, "dp", 1)), chans
    )
    return (block_out[None, None], input_grad[None, None], spatial_grad, temporal_grad)


def solution(mesh):
    placed = (
        P("dp", "seq", None, None, None),
        P(None, "seq", None),
        P(None, "seq", None),
        P("dp", "seq", None, None, None),
    )
    return jax.shard_map(
        local,
        mesh=mesh,
        in_specs=placed,
        out_specs=(
            P("dp", "seq", None, None, None),
            P("dp", "seq", None, None, None),
            P(None, "seq", None),
            P(None, "seq", None),
        ),
        check_vma=False,
    )
```

time: 115 us -> 105 us (0.913)
  waiting for transfers between devices: 38 us -> 25.7 us
  Pallas kernels: 25.8 us -> 37.2 us
  local copies, waits for them, and re-layouts: 9.8 us -> 1.39 us
    ppermute x35 -> x23, waiting for transfers between devices: 38 us -> 21.3 us  [swap(): return lax.ppermute(values, axis, [(i, i ^ bit) for i in range(size)])]
    ppermute x35 -> x23, starting transfers between devices: 33 us -> 19.2 us  [swap(): return lax.ppermute(values, axis, [(i, i ^ bit) for i in range(size)])]
    all_to_all x1 -> x5, starting transfers between devices: 5.31 us -> 19 us  [exchange(): return lax.all_to_all(blocks, 'seq', 0, 0, tiled=True)]
    pallas_call x15, Pallas kernels: 25.8 us -> 37.2 us  [call(): pl.pallas_call(body, out_shape=tuple((pltpu.HBM(out.shape, out.dtype) if...]
    unnamed x36 -> x20, local copies, waits for them, and re-layouts: 9.8 us -> 1.39 us
    all_to_all x1 -> x5, waiting for transfers between devices: 0.01 us -> 4.38 us  [exchange(): return lax.all_to_all(blocks, 'seq', 0, 0, tiled=True)]
  transfers between devices with their start and end apart: 36 -> 28, of which waited for: 13 -> 12; matrix products, arithmetic and copies ran while one was open for 1% -> 0% of each run, Pallas kernels for 21% -> 31%
where the time goes in v3:
time: 105 us
  starting transfers between devices  38.3 us (36%)
  Pallas kernels  37.2 us (35%)
  waiting for transfers between devices  25.7 us (24%)
  local copies, waits for them, and re-layouts  1.39 us (1%)
  other arithmetic  1.3 us (1%)
    pallas_call x15, Pallas kernels, call(): pl.pallas_call(body, out_shape=tuple((pltpu.HBM(out.shape, out.dtype) if...  37.2 us
    ppermute x23, waiting for transfers between devices, swap(): return lax.ppermute(values, axis, [(i, i ^ bit) for i in range(size)])  21.3 us
    ppermute x23, starting transfers between devices, swap(): return lax.ppermute(values, axis, [(i, i ^ bit) for i in range(size)])  19.2 us
    all_to_all x5, starting transfers between devices, exchange(): return lax.all_to_all(blocks, 'seq', 0, 0, tiled=True)  19 us
    all_to_all x5, waiting for transfers between devices, exchange(): return lax.all_to_all(blocks, 'seq', 0, 0, tiled=True)  4.38 us
  transfers between devices with their start and end apart: 28, of which 12 were waited for; matrix products, arithmetic and copies ran while one was open for 0% of the time, Pallas kernels for 31%

profile of v3, /device:TPU:0, one launch (start us, length us, event | category | flops | bytes accessed | tf_op | source)
XLA Modules:
  0.0 104.8 jit_solution(16378713572216817634)
XLA Ops:
  0.6 1.3 %slice_select_fusion = (bf16[3,80,320]{2,1,0:T(8,128)(2,1)S(1)}, bf16[3,80,320]{2,1,0:T(8,128)(2,1)S(1)}) fusion(bf16[9,80,320]{2,1,0:T(8,128)(2,1)} %refs_2_.1, pred[]{:T(512)S(6)} %eq.3, bf16[3,80,320]{2,1,0:T(8,128)(2,1)} %refs_0_.1), kind=kLoop, calls=%fused_computation | loop fusion | flops 153600 | bytes 921601 | tf_op jit(solution)/shard_map/jit(_where)/select_n | solution.py:672
  2.0 4.0 %collective-permute-start.2 = (bf16[3,80,320]{2,1,0:T(8,128)(2,1)S(1)}, bf16[3,80,320]{2,1,0:T(8,128)(2,1)S(1)}, u32[]{:S(2)}, u32[]{:S(2)}) collective-permute-start(bf16[3,80,320]{2,1,0:T(8,128)(2,1)S(1)} %get-tuple-element.71), channel_id=1, source_target_pairs={{0,24},{8,16},{16,8},{24,0},{1,25},{9,17},{17,9},{25,1},{2,26},{10... | collective-permute-start | bytes 460808 | tf_op jit(solution)/shard_map/ppermute | solution.py:73
  6.6 4.1 %all-to-all-start = ((bf16[4,2,320,128]{3,2,1,0:T(8,128)(2,1)}), bf16[4,2,320,128]{3,2,1,0:T(8,128)(2,1)S(1)}, u32[]{:S(2)}, u32[]{:S(2)}) async-start(bf16[4,2,320,128]{3,2,1,0:T(8,128)(2,1)} %bitcast.13), calls=%async_computation | async-start | bytes 1310720 | tf_op jit(solution)/shard_map/all_to_all | solution.py:81
  11.4 4.0 %collective-permute-done.1.refs_3_ = bf16[3,80,320]{2,1,0:T(8,128)(2,1)S(1)} collective-permute-done((bf16[3,80,320]{2,1,0:T(8,128)(2,1)S(1)}, bf16[3,80,320]{2,1,0:T(8,128)(2,1)S(1)}, u32[]{:S(2)}, u32[]{:S(2)}) %collective-permute-start.1) | collective-permute-done | bytes 153632 | tf_op jit(solution)/shard_map/ppermute | solution.py:73
  16.0 1.7 %collective-permute-start.9 = (bf16[3,80,320]{2,1,0:T(8,128)(2,1)S(1)}, bf16[3,80,320]{2,1,0:T(8,128)(2,1)S(1)}, u32[]{:S(2)}, u32[]{:S(2)}) collective-permute-start(bf16[3,80,320]{2,1,0:T(8,128)(2,1)S(1)} %get-tuple-element.70), channel_id=1, source_target_pairs={{0,24},{8,16},{16,8},{24,0},{1,25},{9,17},{17,9},{25,1},{2,26},{10... | collective-permute-start | bytes 460808 | tf_op jit(solution)/shard_map/ppermute | solution.py:73
  17.7 1.2 %collective-permute-start.8 = (bf16[3,80,320]{2,1,0:T(8,128)(2,1)S(1)}, bf16[3,80,320]{2,1,0:T(8,128)(2,1)S(1)}, u32[]{:S(2)}, u32[]{:S(2)}) collective-permute-start(bf16[3,80,320]{2,1,0:T(8,128)(2,1)S(1)} %get-tuple-element.70), channel_id=1, source_target_pairs={{0,16},{8,24},{16,0},{24,8},{1,17},{9,25},{17,1},{25,9},{2,18},{10... | collective-permute-start | bytes 460808 | tf_op jit(solution)/shard_map/ppermute | solution.py:73
  18.9 2.4 %shard_map.76.refs_0_.far_taps = bf16[960,1280]{1,0:T(8,128)(2,1)} custom-call(bf16[8,320,128]{2,1,0:T(8,128)(2,1)S(1)} %bitcast.10), custom_call_target="tpu_custom_call" | custom-call | flops 3276801 | bytes 31129600 | tf_op jit(solution)/shard_map/pallas_call | solution.py:26
  22.0 2.1 %shard_map.75 = (bf16[320,960]{1,0:T(8,128)(2,1)}, bf16[320,960]{1,0:T(8,128)(2,1)}, bf16[320,960]{1,0:T(8,128)(2,1)}) custom-call(bf16[3,80,320]{2,1,0:T(8,128)(2,1)S(1)} %copy-done.2, bf16[9,80,320]{2,1,0:T(8,128)(2,1)S(1)} %copy-done.1, bf16[3,80,320]{2,1,0:T(8,128)(2,1)S(1)} %collective-permute-done.refs_2_, ...), custom_call_target="tpu_custom_call" | custom-call | flops 1966080000 | bytes 33792000 | tf_op jit(solution)/shard_map/pallas_call | solution.py:26
  24.1 2.8 %shard_map.77 = bf16[4,2,320,128]{3,2,1,0:T(8,128)(2,1)} custom-call(bf16[4,2,320,128]{3,2,1,0:T(8,128)(2,1)S(1)} %all-to-all-done.cot_ref, bf16[320,960]{1,0:T(8,128)(2,1)} %get-tuple-element.41.far_ref), custom_call_target="tpu_custom_call" | custom-call | flops 6291456000 | bytes 19251200 | tf_op jit(solution)/shard_map/pallas_call | solution.py:26
  27.0 2.4 %collective-permute-done.8.refs_4_ = bf16[3,80,320]{2,1,0:T(8,128)(2,1)S(1)} collective-permute-done((bf16[3,80,320]{2,1,0:T(8,128)(2,1)S(1)}, bf16[3,80,320]{2,1,0:T(8,128)(2,1)S(1)}, u32[]{:S(2)}, u32[]{:S(2)}) %collective-permute-start.8) | collective-permute-done | bytes 153632 | tf_op jit(solution)/shard_map/ppermute | solution.py:73
  30.8 3.6 %all-to-all-start.1 = ((bf16[4,2,320,128]{3,2,1,0:T(8,128)(2,1)}), bf16[4,2,320,128]{3,2,1,0:T(8,128)(2,1)S(1)}, u32[]{:S(2)}, u32[]{:S(2)}) async-start(bf16[4,2,320,128]{3,2,1,0:T(8,128)(2,1)} %shard_map.77), calls=%async_computation.1 | async-start | bytes 1310720 | tf_op jit(solution)/shard_map/all_to_all | solution.py:81
  35.8 5.7 %shard_map.78 = (bf16[8,320,128]{2,1,0:T(8,128)(2,1)S(1)}, bf16[8,320,128]{2,1,0:T(8,128)(2,1)}, bf16[3,320,960]{2,1,0:T(8,128)(2,1)}) custom-call(bf16[960,1280]{1,0:T(8,128)(2,1)} %shard_map.76.refs_0_.far_taps, bf16[320,960]{1,0:T(8,128)(2,1)} %get-tuple-element.39.refs_1_, bf16[9,80,320]{2,1,0:T(8,128)(2,1)} %refs_2_.1, bf16[3,80,320]{2,1,0:T(8,128)(2,1)} %copy-done.6, ...), custom_call_target="tpu_custom_call" | custom-call | flops 18874368000 | bytes 76083200 | tf_op jit(solution)/shard_map/pallas_call | solution.py:26
  41.4 2.7 %all-to-all-done.1 = bf16[4,2,320,128]{3,2,1,0:T(8,128)(2,1)S(1)} async-done(((bf16[4,2,320,128]{3,2,1,0:T(8,128)(2,1)}), bf16[4,2,320,128]{3,2,1,0:T(8,128)(2,1)S(1)}, u32[]{:S(2)}, u32[]{:S(2)}) %all-to-all-start.1) | async-done | bytes 655392 | tf_op jit(solution)/shard_map/all_to_all | solution.py:81
  44.1 3.5 %all-to-all-start.2 = ((bf16[4,2,320,128]{3,2,1,0:T(8,128)(2,1)}), bf16[4,2,320,128]{3,2,1,0:T(8,128)(2,1)S(1)}, u32[]{:S(2)}, u32[]{:S(2)}) async-start(bf16[4,2,320,128]{3,2,1,0:T(8,128)(2,1)} %bitcast.15), calls=%async_computation.2 | async-start | bytes 1310720 | tf_op jit(solution)/shard_map/all_to_all | solution.py:81
  47.6 1.5 %shard_map.79 = (bf16[160,1024]{1,0:T(8,128)(2,1)S(1)}, bf16[160,1024]{1,0:T(8,128)(2,1)S(1)}, bf16[8,320,128]{2,1,0:T(8,128)(2,1)}) custom-call(bf16[8,320,128]{2,1,0:T(8,128)(2,1)S(1)} %get-tuple-element.45.pre_ref, bf16[8,320,128]{2,1,0:T(8,128)(2,1)S(1)} %bitcast.8), custom_call_target="tpu_custom_call" | custom-call | flops 65536000 | bytes 26214400 | tf_op jit(solution)/shard_map/pallas_call | solution.py:26
  49.2 3.6 %shard_map.80.far_other = bf16[960,1280]{1,0:T(8,128)(2,1)} custom-call(bf16[8,320,128]{2,1,0:T(8,128)(2,1)} %collective-permute-done.6.frames_ref), custom_call_target="tpu_custom_call" | custom-call | flops 1 | bytes 1 | tf_op jit(solution)/shard_map/pallas_call | solution.py:26
  52.7 5.6 %shard_map.81 = (f32[3,40,960]{2,1,0:T(8,128)S(1)}, bf16[3,40,960]{2,1,0:T(8,128)(2,1)}, bf16[3,40,960]{2,1,0:T(8,128)(2,1)}, bf16[3,40,960]{2,1,0:T(8,128)(2,1)}) custom-call(bf16[960,1280]{1,0:T(8,128)(2,1)} %shard_map.76.refs_0_.far_taps, bf16[960,1280]{1,0:T(8,128)(2,1)} %shard_map.80.far_other, bf16[160,1024]{1,0:T(8,128)(2,1)S(1)} %get-tuple-element.48.mine_ref, ...), custom_call_target="tpu_custom_call" | custom-call | flops 1 | bytes 1 | tf_op jit(solution)/shard_map/pallas_call | solution.py:26
  58.4 2.8 %shard_map.82 = (bf16[4,2,320,128]{3,2,1,0:T(8,128)(2,1)}, f32[4,40,960]{2,1,0:T(8,128)S(1)}, bf16[4,40,960]{2,1,0:T(8,128)(2,1)S(1)}) custom-call(bf16[4,2,320,128]{3,2,1,0:T(8,128)(2,1)S(1)} %all-to-all-done.2.act_ref, bf16[4,2,320,128]{3,2,1,0:T(8,128)(2,1)S(1)} %all-to-all-done.cot_ref, bf16[320,960]{1,0:T(8,128)(2,1)} %get-tuple-element.52.far_ref), custom_call_target="tpu_custom_call" | custom-call | flops 12582912000 | bytes 35020800 | tf_op jit(solution)/shard_map/pallas_call | solution.py:26
  61.8 2.0 %collective-permute-start.15 = (bf16[3,40,960]{2,1,0:T(8,128)(2,1)}, bf16[3,40,960]{2,1,0:T(8,128)(2,1)S(1)}, u32[]{:S(2)}, u32[]{:S(2)}) collective-permute-start(bf16[3,40,960]{2,1,0:T(8,128)(2,1)} %get-tuple-element.55), channel_id=1, source_target_pairs={{0,8},{8,0},{16,24},{24,16},{1,9},{9,1},{17,25},{25,17},{2,10},{10... | collective-permute-start | bytes 691208 | tf_op jit(solution)/shard_map/ppermute | solution.py:73
  63.8 1.5 %collective-permute-start.16 = (bf16[3,40,960]{2,1,0:T(8,128)(2,1)}, bf16[3,40,960]{2,1,0:T(8,128)(2,1)S(1)}, u32[]{:S(2)}, u32[]{:S(2)}) collective-permute-start(bf16[3,40,960]{2,1,0:T(8,128)(2,1)} %get-tuple-element.56), channel_id=1, source_target_pairs={{0,16},{8,24},{16,0},{24,8},{1,17},{9,25},{17,1},{25,9},{2,18},{10... | collective-permute-start | bytes 691208 | tf_op jit(solution)/shard_map/ppermute | solution.py:73
  66.0 4.2 %all-to-all-start.3 = ((bf16[4,40,960]{2,1,0:T(8,128)(2,1)}), bf16[4,40,960]{2,1,0:T(8,128)(2,1)S(1)}, u32[]{:S(2)}, u32[]{:S(2)}) async-start(bf16[4,40,960]{2,1,0:T(8,128)(2,1)} %shard_map.83), calls=%async_computation.3 | async-start | bytes 655360 | tf_op jit(solution)/shard_map/all_to_all | solution.py:81
  70.8 7.9 %collective-permute-done.16.refs_1_ = bf16[3,40,960]{2,1,0:T(8,128)(2,1)S(1)} collective-permute-done((bf16[3,40,960]{2,1,0:T(8,128)(2,1)}, bf16[3,40,960]{2,1,0:T(8,128)(2,1)S(1)}, u32[]{:S(2)}, u32[]{:S(2)}) %collective-permute-start.16) | collective-permute-done | bytes 230432 | tf_op jit(solution)/shard_map/ppermute | solution.py:73
  78.7 1.7 %all-to-all-done.3.temporal_ref = bf16[4,40,960]{2,1,0:T(8,128)(2,1)S(1)} async-done(((bf16[4,40,960]{2,1,0:T(8,128)(2,1)}), bf16[4,40,960]{2,1,0:T(8,128)(2,1)S(1)}, u32[]{:S(2)}, u32[]{:S(2)}) %all-to-all-start.3) | async-done | bytes 307232 | tf_op jit(solution)/shard_map/all_to_all | solution.py:81
  80.6 1.6 %collective-permute-start.18 = (bf16[2,40,960]{2,1,0:T(8,128)(2,1)S(1)}, bf16[2,40,960]{2,1,0:T(8,128)(2,1)S(1)}, u32[]{:S(2)}, u32[]{:S(2)}) collective-permute-start(bf16[2,40,960]{2,1,0:T(8,128)(2,1)S(1)} %get-tuple-element.59), channel_id=1, source_target_pairs={{0,2},{1,3},{2,0},{3,1},{4,6},{5,7},{6,4},{7,5},{8,10},{9,11},{10,... | collective-permute-start | bytes 460808 | tf_op jit(solution)/shard_map/ppermute | solution.py:73
  82.3 3.7 %all-to-all-start.4 = ((bf16[4,2,320,128]{3,2,1,0:T(8,128)(2,1)}), bf16[4,2,320,128]{3,2,1,0:T(8,128)(2,1)S(1)}, u32[]{:S(2)}, u32[]{:S(2)}) async-start(bf16[4,2,320,128]{3,2,1,0:T(8,128)(2,1)} %get-tuple-element.65), calls=%async_computation.4 | async-start | bytes 1310720 | tf_op jit(solution)/shard_map/all_to_all | solution.py:81
  86.6 2.7 %collective-permute-start.19 = (bf16[2,40,960]{2,1,0:T(8,128)(2,1)S(1)}, bf16[2,40,960]{2,1,0:T(8,128)(2,1)S(1)}, u32[]{:S(2)}, u32[]{:S(2)}) collective-permute-start(bf16[2,40,960]{2,1,0:T(8,128)(2,1)S(1)} %shard_map.85.keep_ref), channel_id=1, source_target_pairs={{0,4},{1,5},{2,6},{3,7},{4,0},{5,1},{6,2},{7,3},{8,12},{9,13},{10,... | collective-permute-start | bytes 460808 | tf_op jit(solution)/shard_map/ppermute | solution.py:73
  89.2 7.3 %shard_map.86 = bf16[8,320,128]{2,1,0:T(8,128)(2,1)} custom-call(bf16[8,320,128]{2,1,0:T(8,128)(2,1)} %get-tuple-element.61.far_pg, bf16[8,320,128]{2,1,0:T(8,128)(2,1)} %bitcast.14, bf16[3,320,960]{2,1,0:T(8,128)(2,1)} %get-tuple-element.62.far_weights), custom_call_target="tpu_custom_call" | custom-call | flops 18874368000 | bytes 38092800 | tf_op jit(solution)/shard_map/pallas_call | solution.py:26
  96.6 1.6 %collective-permute-start.20 = (bf16[2,40,960]{2,1,0:T(8,128)(2,1)S(1)}, bf16[2,40,960]{2,1,0:T(8,128)(2,1)S(1)}, u32[]{:S(2)}, u32[]{:S(2)}) collective-permute-start(bf16[2,40,960]{2,1,0:T(8,128)(2,1)S(1)} %shard_map.87.own_ref), channel_id=1, source_target_pairs={{0,2},{1,3},{2,0},{3,1},{4,6},{5,7},{6,4},{7,5},{8,10},{9,11},{10,... | collective-permute-start | bytes 460808 | tf_op jit(solution)/shard_map/ppermute | solution.py:73
  98.3 1.0 shard_map.88
  99.2 2.7 %collective-permute-done.20.next_ref = bf16[2,40,960]{2,1,0:T(8,128)(2,1)S(1)} collective-permute-done((bf16[2,40,960]{2,1,0:T(8,128)(2,1)S(1)}, bf16[2,40,960]{2,1,0:T(8,128)(2,1)S(1)}, u32[]{:S(2)}, u32[]{:S(2)}) %collective-permute-start.20) | collective-permute-done | bytes 153632 | tf_op jit(solution)/shard_map/ppermute | solution.py:73
  102.0 1.4 %collective-permute-done.22.both_ref = bf16[2,40,960]{2,1,0:T(8,128)(2,1)S(1)} collective-permute-done((bf16[2,40,960]{2,1,0:T(8,128)(2,1)S(1)}, bf16[2,40,960]{2,1,0:T(8,128)(2,1)S(1)}, u32[]{:S(2)}, u32[]{:S(2)}) %collective-permute-start.22) | collective-permute-done | bytes 153632 | tf_op jit(solution)/shard_map/ppermute | solution.py:73
  103.4 1.4 %shard_map.89 = (f32[9,80,320]{2,1,0:T(8,128)}, f32[3,80,320]{2,1,0:T(8,128)}) custom-call(bf16[2,40,960]{2,1,0:T(8,128)(2,1)S(1)} %shard_map.87.own_ref, bf16[2,40,960]{2,1,0:T(8,128)(2,1)S(1)} %collective-permute-done.20.next_ref, bf16[2,40,960]{2,1,0:T(8,128)(2,1)S(1)} %collective-permute-done.21.core_ref, ...), custom_call_target="tpu_custom_call" | custom-call | flops 6144001 | bytes 18432000 | tf_op jit(solution)/shard_map/pallas_call | solution.py:26
  (60 shorter events, 8.3 us)
Async XLA Ops:
  0.6 18.3 %copy-start = (bf16[1,1,8,320,128]{4,3,2,1,0:T(8,128)(2,1)S(1)}, bf16[1,1,8,320,128]{4,3,2,1,0:T(8,128)(2,1)}, u32[]{:S(2)}) copy-start(bf16[1,1,8,320,128]{4,3,2,1,0:T(8,128)(2,1)} %param.4) | copy-start | bytes 1966084
  1.9 20.0 %copy-start.1 = (bf16[9,80,320]{2,1,0:T(8,128)(2,1)S(1)}, bf16[9,80,320]{2,1,0:T(8,128)(2,1)}, u32[]{:S(2)}) copy-start(bf16[9,80,320]{2,1,0:T(8,128)(2,1)} %refs_2_.1) | copy-start | bytes 1382404
  2.0 20.0 %copy-start.2 = (bf16[3,80,320]{2,1,0:T(8,128)(2,1)S(1)}, bf16[3,80,320]{2,1,0:T(8,128)(2,1)}, u32[]{:S(2)}) copy-start(bf16[3,80,320]{2,1,0:T(8,128)(2,1)} %refs_0_.1) | copy-start | bytes 460804
  2.0 9.4 %collective-permute-start.2 = (bf16[3,80,320]{2,1,0:T(8,128)(2,1)S(1)}, bf16[3,80,320]{2,1,0:T(8,128)(2,1)S(1)}, u32[]{:S(2)}, u32[]{:S(2)}) collective-permute-start(bf16[3,80,320]{2,1,0:T(8,128)(2,1)S(1)} %get-tuple-element.71), channel_id=1, source_target_pairs={{0,24},{8,16},{16,8},{24,0},{1,25},{9,17},{17,9},{25,1},{2,26},{10... | collective-permute-start | bytes 460808 | tf_op jit(solution)/shard_map/ppermute | solution.py:73
  5.9 9.5 %collective-permute-start.1 = (bf16[3,80,320]{2,1,0:T(8,128)(2,1)S(1)}, bf16[3,80,320]{2,1,0:T(8,128)(2,1)S(1)}, u32[]{:S(2)}, u32[]{:S(2)}) collective-permute-start(bf16[3,80,320]{2,1,0:T(8,128)(2,1)S(1)} %get-tuple-element.71), channel_id=1, source_target_pairs={{0,16},{8,24},{16,0},{24,8},{1,17},{9,25},{17,1},{25,9},{2,18},{10... | collective-permute-start | bytes 460808 | tf_op jit(solution)/shard_map/ppermute | solution.py:73
  6.4 9.5 %collective-permute-start = (bf16[3,80,320]{2,1,0:T(8,128)(2,1)S(1)}, bf16[3,80,320]{2,1,0:T(8,128)(2,1)S(1)}, u32[]{:S(2)}, u32[]{:S(2)}) collective-permute-start(bf16[3,80,320]{2,1,0:T(8,128)(2,1)S(1)} %get-tuple-element.71), channel_id=1, source_target_pairs={{0,8},{8,0},{16,24},{24,16},{1,9},{9,1},{17,25},{25,17},{2,10},{10... | collective-permute-start | bytes 460808 | tf_op jit(solution)/shard_map/ppermute | solution.py:73
  6.6 17.6 %all-to-all-start = ((bf16[4,2,320,128]{3,2,1,0:T(8,128)(2,1)}), bf16[4,2,320,128]{3,2,1,0:T(8,128)(2,1)S(1)}, u32[]{:S(2)}, u32[]{:S(2)}) async-start(bf16[4,2,320,128]{3,2,1,0:T(8,128)(2,1)} %bitcast.13), calls=%async_computation | async-start | bytes 1310720 | tf_op jit(solution)/shard_map/all_to_all | solution.py:81
  11.4 9.9 %collective-permute-start.5 = (bf16[3,80,320]{2,1,0:T(8,128)(2,1)S(1)}, bf16[3,80,320]{2,1,0:T(8,128)(2,1)S(1)}, u32[]{:S(2)}, u32[]{:S(2)}) collective-permute-start(bf16[3,80,320]{2,1,0:T(8,128)(2,1)S(1)} %collective-permute-done.2.refs_4_), channel_id=1, source_target_pairs={{0,1},{1,0},{2,3},{3,2},{4,5},{5,4},{6,7},{7,6},{8,9},{9,8},{10,11... | collective-permute-start | bytes 460808 | tf_op jit(solution)/shard_map/ppermute | solution.py:73
  15.5 6.5 %collective-permute-start.4 = (bf16[3,80,320]{2,1,0:T(8,128)(2,1)S(1)}, bf16[3,80,320]{2,1,0:T(8,128)(2,1)S(1)}, u32[]{:S(2)}, u32[]{:S(2)}) collective-permute-start(bf16[3,80,320]{2,1,0:T(8,128)(2,1)S(1)} %collective-permute-done.1.refs_3_), channel_id=1, source_target_pairs={{0,1},{1,0},{2,3},{3,2},{4,5},{5,4},{6,7},{7,6},{8,9},{9,8},{10,11... | collective-permute-start | bytes 460808 | tf_op jit(solution)/shard_map/ppermute | solution.py:73
  16.0 6.0 %collective-permute-start.3 = (bf16[3,80,320]{2,1,0:T(8,128)(2,1)S(1)}, bf16[3,80,320]{2,1,0:T(8,128)(2,1)S(1)}, u32[]{:S(2)}, u32[]{:S(2)}) collective-permute-start(bf16[3,80,320]{2,1,0:T(8,128)(2,1)S(1)} %collective-permute-done.refs_2_), channel_id=1, source_target_pairs={{0,1},{1,0},{2,3},{3,2},{4,5},{5,4},{6,7},{7,6},{8,9},{9,8},{10,11... | collective-permute-start | bytes 460808 | tf_op jit(solution)/shard_map/ppermute | solution.py:73
  16.0 11.0 %collective-permute-start.9 = (bf16[3,80,320]{2,1,0:T(8,128)(2,1)S(1)}, bf16[3,80,320]{2,1,0:T(8,128)(2,1)S(1)}, u32[]{:S(2)}, u32[]{:S(2)}) collective-permute-start(bf16[3,80,320]{2,1,0:T(8,128)(2,1)S(1)} %get-tuple-element.70), channel_id=1, source_target_pairs={{0,24},{8,16},{16,8},{24,0},{1,25},{9,17},{17,9},{25,1},{2,26},{10... | collective-permute-start | bytes 460808 | tf_op jit(solution)/shard_map/ppermute | solution.py:73
  17.7 11.6 %collective-permute-start.8 = (bf16[3,80,320]{2,1,0:T(8,128)(2,1)S(1)}, bf16[3,80,320]{2,1,0:T(8,128)(2,1)S(1)}, u32[]{:S(2)}, u32[]{:S(2)}) collective-permute-start(bf16[3,80,320]{2,1,0:T(8,128)(2,1)S(1)} %get-tuple-element.70), channel_id=1, source_target_pairs={{0,16},{8,24},{16,0},{24,8},{1,17},{9,25},{17,1},{25,9},{2,18},{10... | collective-permute-start | bytes 460808 | tf_op jit(solution)/shard_map/ppermute | solution.py:73
  21.3 8.4 %collective-permute-start.7 = (bf16[3,80,320]{2,1,0:T(8,128)(2,1)S(1)}, bf16[3,80,320]{2,1,0:T(8,128)(2,1)S(1)}, u32[]{:S(2)}, u32[]{:S(2)}) collective-permute-start(bf16[3,80,320]{2,1,0:T(8,128)(2,1)S(1)} %get-tuple-element.70), channel_id=1, source_target_pairs={{0,8},{8,0},{16,24},{24,16},{1,9},{9,1},{17,25},{25,17},{2,10},{10... | collective-permute-start | bytes 460808 | tf_op jit(solution)/shard_map/ppermute | solution.py:73
  26.9 7.5 %copy-start.4 = (bf16[3,80,320]{2,1,0:T(8,128)(2,1)}, bf16[3,80,320]{2,1,0:T(8,128)(2,1)S(1)}, u32[]{:S(2)}) copy-start(bf16[3,80,320]{2,1,0:T(8,128)(2,1)S(1)} %collective-permute-done.9.refs_5_) | copy-start | bytes 460804
  29.7 4.6 %collective-permute-start.10 = (bf16[3,80,320]{2,1,0:T(8,128)(2,1)S(1)}, bf16[3,80,320]{2,1,0:T(8,128)(2,1)S(1)}, u32[]{:S(2)}, u32[]{:S(2)}) collective-permute-start(bf16[3,80,320]{2,1,0:T(8,128)(2,1)S(1)} %collective-permute-done.7.refs_3_), channel_id=1, source_target_pairs={{0,1},{1,0},{2,3},{3,2},{4,5},{5,4},{6,7},{7,6},{8,9},{9,8},{10,11... | collective-permute-start | bytes 460808 | tf_op jit(solution)/shard_map/ppermute | solution.py:73
  29.7 4.6 %collective-permute-start.11 = (bf16[3,80,320]{2,1,0:T(8,128)(2,1)S(1)}, bf16[3,80,320]{2,1,0:T(8,128)(2,1)S(1)}, u32[]{:S(2)}, u32[]{:S(2)}) collective-permute-start(bf16[3,80,320]{2,1,0:T(8,128)(2,1)S(1)} %collective-permute-done.8.refs_4_), channel_id=1, source_target_pairs={{0,1},{1,0},{2,3},{3,2},{4,5},{5,4},{6,7},{7,6},{8,9},{9,8},{10,11... | collective-permute-start | bytes 460808 | tf_op jit(solution)/shard_map/ppermute | solution.py:73
  30.2 4.1 %collective-permute-start.12 = (bf16[3,80,320]{2,1,0:T(8,128)(2,1)S(1)}, bf16[3,80,320]{2,1,0:T(8,128)(2,1)S(1)}, u32[]{:S(2)}, u32[]{:S(2)}) collective-permute-start(bf16[3,80,320]{2,1,0:T(8,128)(2,1)S(1)} %collective-permute-done.9.refs_5_), channel_id=1, source_target_pairs={{0,1},{1,0},{2,3},{3,2},{4,5},{5,4},{6,7},{7,6},{8,9},{9,8},{10,11... | collective-permute-start | bytes 460808 | tf_op jit(solution)/shard_map/ppermute | solution.py:73
  30.3 18.9 %collective-permute-start.6 = (bf16[8,320,128]{2,1,0:T(8,128)(2,1)S(1)}, bf16[8,320,128]{2,1,0:T(8,128)(2,1)}, u32[]{:S(2)}, u32[]{:S(2)}) collective-permute-start(bf16[8,320,128]{2,1,0:T(8,128)(2,1)S(1)} %bitcast.11), channel_id=1, source_target_pairs={{0,1},{1,0},{2,3},{3,2},{4,5},{5,4},{6,7},{7,6},{8,9},{9,8},{10,11... | collective-permute-start | bytes 1966088 | tf_op jit(solution)/shard_map/ppermute | solution.py:73
  30.8 13.3 %all-to-all-start.1 = ((bf16[4,2,320,128]{3,2,1,0:T(8,128)(2,1)}), bf16[4,2,320,128]{3,2,1,0:T(8,128)(2,1)S(1)}, u32[]{:S(2)}, u32[]{:S(2)}) async-start(bf16[4,2,320,128]{3,2,1,0:T(8,128)(2,1)} %shard_map.77), calls=%async_computation.1 | async-start | bytes 1310720 | tf_op jit(solution)/shard_map/all_to_all | solution.py:81
  44.1 14.3 %all-to-all-start.2 = ((bf16[4,2,320,128]{3,2,1,0:T(8,128)(2,1)}), bf16[4,2,320,128]{3,2,1,0:T(8,128)(2,1)S(1)}, u32[]{:S(2)}, u32[]{:S(2)}) async-start(bf16[4,2,320,128]{3,2,1,0:T(8,128)(2,1)} %bitcast.15), calls=%async_computation.2 | async-start | bytes 1310720 | tf_op jit(solution)/shard_map/all_to_all | solution.py:81
  49.1 3.7 %collective-permute-start.13 = (bf16[160,1024]{1,0:T(8,128)(2,1)S(1)}, bf16[160,1024]{1,0:T(8,128)(2,1)S(1)}, u32[]{:S(2)}, u32[]{:S(2)}) collective-permute-start(bf16[160,1024]{1,0:T(8,128)(2,1)S(1)} %get-tuple-element.46), channel_id=1, source_target_pairs={{0,1},{1,0},{2,3},{3,2},{4,5},{5,4},{6,7},{7,6},{8,9},{9,8},{10,11... | collective-permute-start | bytes 983048 | tf_op jit(solution)/shard_map/ppermute | solution.py:73
  61.2 4.0 %collective-permute-start.14 = (bf16[4,40,960]{2,1,0:T(8,128)(2,1)S(1)}, bf16[4,40,960]{2,1,0:T(8,128)(2,1)S(1)}, u32[]{:S(2)}, u32[]{:S(2)}) collective-permute-start(bf16[4,40,960]{2,1,0:T(8,128)(2,1)S(1)} %get-tuple-element.54), channel_id=1, source_target_pairs={{0,1},{1,0},{2,3},{3,2},{4,5},{5,4},{6,7},{7,6},{8,9},{9,8},{10,11... | collective-permute-start | bytes 921608 | tf_op jit(solution)/shard_map/ppermute | solution.py:73
  61.8 9.0 %collective-permute-start.15 = (bf16[3,40,960]{2,1,0:T(8,128)(2,1)}, bf16[3,40,960]{2,1,0:T(8,128)(2,1)S(1)}, u32[]{:S(2)}, u32[]{:S(2)}) collective-permute-start(bf16[3,40,960]{2,1,0:T(8,128)(2,1)} %get-tuple-element.55), channel_id=1, source_target_pairs={{0,8},{8,0},{16,24},{24,16},{1,9},{9,1},{17,25},{25,17},{2,10},{10... | collective-permute-start | bytes 691208 | tf_op jit(solution)/shard_map/ppermute | solution.py:73
  63.8 14.9 %collective-permute-start.16 = (bf16[3,40,960]{2,1,0:T(8,128)(2,1)}, bf16[3,40,960]{2,1,0:T(8,128)(2,1)S(1)}, u32[]{:S(2)}, u32[]{:S(2)}) collective-permute-start(bf16[3,40,960]{2,1,0:T(8,128)(2,1)} %get-tuple-element.56), channel_id=1, source_target_pairs={{0,16},{8,24},{16,0},{24,8},{1,17},{9,25},{17,1},{25,9},{2,18},{10... | collective-permute-start | bytes 691208 | tf_op jit(solution)/shard_map/ppermute | solution.py:73
  65.2 13.5 %collective-permute-start.17 = (bf16[3,40,960]{2,1,0:T(8,128)(2,1)S(1)}, bf16[3,40,960]{2,1,0:T(8,128)(2,1)S(1)}, u32[]{:S(2)}, u32[]{:S(2)}) collective-permute-start(bf16[3,40,960]{2,1,0:T(8,128)(2,1)S(1)} %copy-done.3), channel_id=1, source_target_pairs={{0,24},{8,16},{16,8},{24,0},{1,25},{9,17},{17,9},{25,1},{2,26},{10... | collective-permute-start | bytes 691208 | tf_op jit(solution)/shard_map/ppermute | solution.py:73
  66.0 14.4 %all-to-all-start.3 = ((bf16[4,40,960]{2,1,0:T(8,128)(2,1)}), bf16[4,40,960]{2,1,0:T(8,128)(2,1)S(1)}, u32[]{:S(2)}, u32[]{:S(2)}) async-start(bf16[4,40,960]{2,1,0:T(8,128)(2,1)} %shard_map.83), calls=%async_computation.3 | async-start | bytes 655360 | tf_op jit(solution)/shard_map/all_to_all | solution.py:81
  80.6 5.9 %collective-permute-start.18 = (bf16[2,40,960]{2,1,0:T(8,128)(2,1)S(1)}, bf16[2,40,960]{2,1,0:T(8,128)(2,1)S(1)}, u32[]{:S(2)}, u32[]{:S(2)}) collective-permute-start(bf16[2,40,960]{2,1,0:T(8,128)(2,1)S(1)} %get-tuple-element.59), channel_id=1, source_target_pairs={{0,2},{1,3},{2,0},{3,1},{4,6},{5,7},{6,4},{7,5},{8,10},{9,11},{10,... | collective-permute-start | bytes 460808 | tf_op jit(solution)/shard_map/ppermute | solution.py:73
  82.3 16.0 %all-to-all-start.4 = ((bf16[4,2,320,128]{3,2,1,0:T(8,128)(2,1)}), bf16[4,2,320,128]{3,2,1,0:T(8,128)(2,1)S(1)}, u32[]{:S(2)}, u32[]{:S(2)}) async-start(bf16[4,2,320,128]{3,2,1,0:T(8,128)(2,1)} %get-tuple-element.65), calls=%async_computation.4 | async-start | bytes 1310720 | tf_op jit(solution)/shard_map/all_to_all | solution.py:81
  86.6 10.0 %collective-permute-start.19 = (bf16[2,40,960]{2,1,0:T(8,128)(2,1)S(1)}, bf16[2,40,960]{2,1,0:T(8,128)(2,1)S(1)}, u32[]{:S(2)}, u32[]{:S(2)}) collective-permute-start(bf16[2,40,960]{2,1,0:T(8,128)(2,1)S(1)} %shard_map.85.keep_ref), channel_id=1, source_target_pairs={{0,4},{1,5},{2,6},{3,7},{4,0},{5,1},{6,2},{7,3},{8,12},{9,13},{10,... | collective-permute-start | bytes 460808 | tf_op jit(solution)/shard_map/ppermute | solution.py:73
  96.6 5.4 %collective-permute-start.20 = (bf16[2,40,960]{2,1,0:T(8,128)(2,1)S(1)}, bf16[2,40,960]{2,1,0:T(8,128)(2,1)S(1)}, u32[]{:S(2)}, u32[]{:S(2)}) collective-permute-start(bf16[2,40,960]{2,1,0:T(8,128)(2,1)S(1)} %shard_map.87.own_ref), channel_id=1, source_target_pairs={{0,2},{1,3},{2,0},{3,1},{4,6},{5,7},{6,4},{7,5},{8,10},{9,11},{10,... | collective-permute-start | bytes 460808 | tf_op jit(solution)/shard_map/ppermute | solution.py:73
  98.2 3.7 %collective-permute-start.21 = (bf16[2,40,960]{2,1,0:T(8,128)(2,1)S(1)}, bf16[2,40,960]{2,1,0:T(8,128)(2,1)S(1)}, u32[]{:S(2)}, u32[]{:S(2)}) collective-permute-start(bf16[2,40,960]{2,1,0:T(8,128)(2,1)S(1)} %shard_map.87.own_ref), channel_id=1, source_target_pairs={{0,1},{1,0},{2,3},{3,2},{4,5},{5,4},{6,7},{7,6},{8,9},{9,8},{10,11... | collective-permute-start | bytes 460808 | tf_op jit(solution)/shard_map/ppermute | solution.py:73
  102.0 1.4 %collective-permute-start.22 = (bf16[2,40,960]{2,1,0:T(8,128)(2,1)S(1)}, bf16[2,40,960]{2,1,0:T(8,128)(2,1)S(1)}, u32[]{:S(2)}, u32[]{:S(2)}) collective-permute-start(bf16[2,40,960]{2,1,0:T(8,128)(2,1)S(1)} %collective-permute-done.20.next_ref), channel_id=1, source_target_pairs={{0,1},{1,0},{2,3},{3,2},{4,5},{5,4},{6,7},{7,6},{8,9},{9,8},{10,11... | collective-permute-start | bytes 460808 | tf_op jit(solution)/shard_map/ppermute | solution.py:73
  (6 other events, 18.6 us)

commit v4 on v3

--- a/solution.py
+++ b/solution.py
@@ -13,7 +13,7 @@
 NT = (((1,), (1,)), ((), ()))
 
 
-def call(body, outs, scratch, flops, *args, far=(), sent=(), light=False):
+def call(body, outs, scratch, flops, *args, far=(), sent=(), weight=10):
     def spec(i):
         return pl.BlockSpec(memory_space=pltpu.HBM if i in far else pltpu.VMEM)
 
@@ -21,7 +21,6 @@
         pltpu.with_memory_space_constraint(arg, pltpu.HBM) if i in far else arg
         for i, arg in enumerate(args)
     ]
-    factor = 0 if light else 10
     moved = sum(x.size * x.dtype.itemsize for x in (*args, *outs))
     return pl.pallas_call(
         body,
@@ -33,7 +32,7 @@
         out_specs=tuple(spec(len(args) + i) for i in range(len(outs))),
         scratch_shapes=scratch,
         compiler_params=pltpu.CompilerParams(vmem_limit_bytes=VMEM_LIMIT),
-        cost_estimate=pl.CostEstimate(flops=factor * flops + 1, bytes_accessed=factor * moved + 1, transcendentals=0),
+        cost_estimate=pl.CostEstimate(flops=weight * flops + 1, bytes_accessed=weight * moved + 1, transcendentals=0),
     )(*args)
 
 
@@ -117,7 +116,7 @@
     return lax.dot_general(one.astype(BF), block, NT, preferred_element_type=F32).astype(BF)
 
 
-def window_taps(frames, light=False):
+def window_taps(frames, weight=10):
     rows, chans, width = frames.shape
     dims = (3 * chans, (rows + 2) * width)
 
@@ -134,7 +133,7 @@
         frames.size,
         frames,
         far=(1,),
-        light=light,
+        weight=weight,
     )[0]
 
 
@@ -215,7 +214,8 @@
     frames, rows, chans, width = cot_rows.shape
     span = rows * width
 
-    def body(cot_ref, far_ref, out_ref, weights_ref, taps_ref, done):
+    def body(cot_ref, far_ref, *refs):
+        outs, (weights_ref, taps_ref, done) = refs[:frames], refs[frames:]
         load = pltpu.make_async_copy(far_ref, weights_ref, done)
         load.start()
         edge = jnp.zeros((chans, span), BF)
@@ -229,18 +229,18 @@
                         to = at * span + y * width
                         taps_ref[k * chans : (k + 1) * chans, to : to + width] = cot_ref[f, y]
         load.wait()
-        for f in range(frames):
+        for j in range(frames):
             total = jnp.dot(
                 weights_ref[...],
-                taps_ref[:, f * span : (f + 1) * span],
+                taps_ref[:, columns(place(j), 1, span)],
                 preferred_element_type=F32,
             ).astype(BF)
             for y in range(rows):
-                out_ref[f, y] = total[:, y * width : (y + 1) * width]
-
-    return call(
-        body,
-        [shape(cot_rows.shape)],
+                outs[j][y] = total[:, y * width : (y + 1) * width]
+
+    return call(
+        body,
+        [shape((rows, chans, width))] * frames,
         [
             pltpu.VMEM(weights_t.shape, BF),
             pltpu.VMEM((3 * chans, frames * span), BF),
@@ -250,8 +250,8 @@
         cot_rows,
         weights_t,
         far=(1,),
-        sent=(2,),
-    )[0]
+        sent=tuple(range(2, 2 + frames)),
+    )
 
 
 def spatial_forward(taps, own, middle, pieces, rows):
@@ -358,14 +358,22 @@
         own,
         *pieces,
         far=(*range(3 + count), 4 + count, 5 + count),
-    )
-
-
-def activation_grad(pre_act, act_grad, shard):
+        weight=10,
+    )
+
+
+def activation_grad(pre_act, grads, shard):
     rows, chans, width = pre_act.shape
     half = shard // 2
 
-    def body(pre_ref, act_ref, mine_ref, theirs_ref, far_ref, pg_ref, done):
+    block = rows // len(grads)
+
+    def body(pre_ref, *refs):
+        grad_refs, refs = refs[: len(grads)], refs[len(grads) :]
+        mine_ref, theirs_ref, far_ref, pg_ref, act_ref, done = refs
+        for j, ref in enumerate(grad_refs):
+            act_ref[pl.ds(place(j) * block, block)] = ref[...]
+
         def row(y, carry):
             wide = pre_ref[y].astype(F32)
             s = 1.0 / (1.0 + jnp.exp(-wide))
@@ -392,11 +400,15 @@
     return call(
         body,
         [shape((chans // 2, rows * width))] * 2 + [shape(pre_act.shape)],
-        [pltpu.VMEM(pre_act.shape, BF), pltpu.SemaphoreType.DMA((2,))],
+        [
+            pltpu.VMEM(pre_act.shape, BF),
+            pltpu.VMEM(pre_act.shape, BF),
+            pltpu.SemaphoreType.DMA((2,)),
+        ],
         20 * pre_act.size,
         pre_act,
-        act_grad,
-        far=(4,),
+        *grads,
+        far=(3 + len(grads),),
     )
 
 
@@ -462,7 +474,7 @@
         other_half,
         far=(0, 1),
         sent=tuple(range(5, 4 + owners)),
-        light=True,
+        weight=0,
     )
 
 
@@ -522,15 +534,13 @@
     )[0]
 
 
-def temporal_forward(acts, cot_rows, weights, shard, scale):
+def temporal_weight_grad(acts, cot_rows, shard, scale):
     frames, rows, chans, width = cot_rows.shape
     span = rows * width
     half = shard // 2
-
-    def body(act_ref, cot_ref, far_ref, out_ref, keep_ref, send_ref, *refs):
-        weights_ref, taps_ref, cots_ref, done = refs
-        load = pltpu.make_async_copy(far_ref, weights_ref, done)
-        load.start()
+    owners = chans // shard
+
+    def body(act_ref, cot_ref, keep_ref, send_ref, taps_ref, cots_ref):
         edge = jnp.zeros((chans, span), BF)
         taps_ref[:chans, :span] = edge
         taps_ref[2 * chans :, (frames - 1) * span :] = edge
@@ -542,6 +552,45 @@
                     if 0 <= f - k + 1 < frames:
                         to = at + (1 - k) * span
                         taps_ref[k * chans : (k + 1) * chans, to : to + width] = act_ref[f, y]
+        total = (
+            lax.dot_general(cots_ref[...], taps_ref[...], NT, preferred_element_type=F32) * scale
+        )
+        first = core() == 0
+        for s in range(owners):
+            low = total[s * shard : s * shard + half]
+            high = total[s * shard + half : (s + 1) * shard]
+            keep_ref[s] = jnp.where(first, low, high)
+            send_ref[s] = jnp.where(first, high, low).astype(BF)
+
+    return call(
+        body,
+        [shape((owners, half, 3 * chans), F32), shape((owners, half, 3 * chans))],
+        [
+            pltpu.VMEM((3 * chans, frames * span), BF),
+            pltpu.VMEM((chans, frames * span), BF),
+        ],
+        6 * chans * cot_rows.size,
+        acts,
+        cot_rows,
+    )
+
+
+def temporal_forward(acts, weights):
+    frames, rows, chans, width = acts.shape
+    span = rows * width
+
+    def body(act_ref, far_ref, out_ref, weights_ref, taps_ref, done):
+        load = pltpu.make_async_copy(far_ref, weights_ref, done)
+        load.start()
+        edge = jnp.zeros((chans, span), BF)
+        taps_ref[:chans, :span] = edge
+        taps_ref[2 * chans :, (frames - 1) * span :] = edge
+        for f in range(frames):
+            for k in range(3):
+                if 0 <= f - k + 1 < frames:
+                    for y in range(rows):
+                        to = (f - k + 1) * span + y * width
+                        taps_ref[k * chans : (k + 1) * chans, to : to + width] = act_ref[f, y]
         load.wait()
         for f in range(frames):
             total = jnp.dot(
@@ -551,37 +600,21 @@
             ).astype(BF)
             for y in range(rows):
                 out_ref[f, y] = total[:, y * width : (y + 1) * width]
-        total = (
-            lax.dot_general(cots_ref[...], taps_ref[...], NT, preferred_element_type=F32) * scale
-        )
-        first = core() == 0
-        for s in range(chans // shard):
-            low = total[s * shard : s * shard + half]
-            high = total[s * shard + half : (s + 1) * shard]
-            keep_ref[s] = jnp.where(first, low, high)
-            send_ref[s] = jnp.where(first, high, low).astype(BF)
-
-    owners = chans // shard
-    return call(
-        body,
-        [
-            shape(cot_rows.shape),
-            shape((owners, half, 3 * chans), F32),
-            shape((owners, half, 3 * chans)),
-        ],
+
+    return call(
+        body,
+        [shape(acts.shape)],
         [
             pltpu.VMEM(weights.shape, BF),
             pltpu.VMEM((3 * chans, frames * span), BF),
-            pltpu.VMEM((chans, frames * span), BF),
             pltpu.SemaphoreType.DMA,
         ],
-        12 * chans * cot_rows.size,
+        6 * chans * acts.size,
         acts,
-        cot_rows,
         weights,
-        far=(2,),
-        sent=(3,),
-    )
+        far=(1,),
+        sent=(2,),
+    )[0]
 
 
 def owner_sum(spatial, others, temporal):
@@ -680,8 +713,8 @@
     taps = window_taps(frames)
     temporal_t, taps = lax.optimization_barrier((temporal_t, taps))
     grad_rows = temporal_backward(cot_rows, temporal_t)
-    act_grad = exchange(grad_rows).reshape(frames.shape)
-    grad_rows, *got_b = lax.optimization_barrier((grad_rows, *got_b))
+    act_grad = [grad_rows[0], *spread(grad_rows[1:])]
+    temporal_w, *got_b = lax.optimization_barrier((after(temporal_w, grad_rows[0]), *got_b))
     pair_b = [swap(piece, "dp", 1) for piece in got_b]
     other_frames = swap(after(frames, middle), "dp", 1)
     pre_act, activated, weights = spatial_forward(
@@ -689,17 +722,20 @@
     )
     half_mine, half_theirs, pre_grad = activation_grad(pre_act, act_grad, shard)
     half_other = swap(half_theirs, "dp", 1)
-    other_taps = window_taps(after(other_frames, half_theirs), light=True)
+    other_taps = window_taps(after(other_frames, half_theirs), weight=0)
     act_rows = exchange(activated.reshape(cot_rows.shape))
     spatial_keep, *spatial_send = spatial_weight_grad(
         taps, other_taps, half_mine, half_other, seq, scale, rows
     )
     spatial_got = spread(spatial_send)
-    temporal_rows, temporal_keep, temporal_send = temporal_forward(
-        act_rows, cot_rows, after(temporal_w, spatial_keep), shard, scale
-    )
-    temporal_part = exchange(add_rounded(temporal_keep, swap(temporal_send, "dp", 1)))
-    keep, send = owner_sum(spatial_keep, spatial_got, temporal_part)
+    temporal_keep, temporal_send = temporal_weight_grad(
+        act_rows, after(cot_rows, spatial_keep), shard, scale
+    )
+    temporal_part = add_rounded(temporal_keep, swap(temporal_send, "dp", 1))
+    temporal_rows = temporal_forward(act_rows, after(temporal_w, temporal_part))
+    keep, send = owner_sum(
+        after(spatial_keep, temporal_rows), spatial_got, exchange(temporal_part)
+    )
     temporal_rows = exchange(after(temporal_rows, keep)).reshape(frames.shape)
     total = add_rounded(keep, swap(send, "dp", 2))
     input_grad = spatial_backward(after(pre_grad, keep), cotangent, weights)

time: 105 us -> 100 us (0.952)
  waiting for transfers between devices: 25.7 us -> 20.4 us
    ppermute x23 -> x26, starting transfers between devices: 19.2 us -> 22.8 us  [swap(): return lax.ppermute(values, axis, [(i, i ^ bit) for i in range(size)])]
    all_to_all x5 -> x4, starting transfers between devices: 19 us -> 15.5 us  [exchange(): return lax.all_to_all(blocks, 'seq', 0, 0, tiled=True)]
    ppermute x23 -> x26, waiting for transfers between devices: 21.3 us -> 18.4 us  [swap(): return lax.ppermute(values, axis, [(i, i ^ bit) for i in range(size)])]
    all_to_all x5 -> x4, waiting for transfers between devices: 4.38 us -> 1.9 us  [exchange(): return lax.all_to_all(blocks, 'seq', 0, 0, tiled=True)]
    pallas_call x15 -> x16, Pallas kernels: 37.2 us -> 38 us  [call(): pl.pallas_call(body, out_shape=tuple((pltpu.HBM(out.shape, out.dtype) if...]
  transfers between devices with their start and end apart: 28 -> 30, of which waited for: 12 -> 10; matrix products, arithmetic and copies ran while one was open for 0% -> 0% of each run, Pallas kernels for 31% -> 36%
where the time goes in v4:
time: 100 us; the launch traced here: 99.6 us
  starting transfers between devices  38.3 us (38%)
  Pallas kernels  38 us (38%)
  waiting for transfers between devices  20.4 us (20%)
  other arithmetic  1.3 us (1%)
    pallas_call x16, Pallas kernels, call(): pl.pallas_call(body, out_shape=tuple((pltpu.HBM(out.shape, out.dtype) if...  38 us
    ppermute x26, starting transfers between devices, swap(): return lax.ppermute(values, axis, [(i, i ^ bit) for i in range(size)])  22.8 us
    ppermute x26, waiting for transfers between devices, swap(): return lax.ppermute(values, axis, [(i, i ^ bit) for i in range(size)])  18.4 us
    all_to_all x4, starting transfers between devices, exchange(): return lax.all_to_all(blocks, 'seq', 0, 0, tiled=True)  15.5 us
  transfers between devices with their start and end apart: 30, of which 10 were waited for; matrix products, arithmetic and copies ran while one was open for 0% of the time, Pallas kernels for 36%

profile of v4, /device:TPU:0, one launch (start us, length us, event | category | flops | bytes accessed | tf_op | source)
XLA Modules:
  0.0 99.6 jit_solution(17083292516882793861)
XLA Ops:
  0.6 1.3 %slice_select_fusion = (bf16[3,80,320]{2,1,0:T(8,128)(2,1)S(1)}, bf16[3,80,320]{2,1,0:T(8,128)(2,1)S(1)}) fusion(bf16[9,80,320]{2,1,0:T(8,128)(2,1)} %refs_2_.1, pred[]{:T(512)S(6)} %eq.3, bf16[3,80,320]{2,1,0:T(8,128)(2,1)} %refs_0_.1), kind=kLoop, calls=%fused_computation | loop fusion | flops 153600 | bytes 921601 | tf_op jit(solution)/shard_map/jit(_where)/select_n | solution.py:705
  2.0 4.0 %collective-permute-start.2 = (bf16[3,80,320]{2,1,0:T(8,128)(2,1)S(1)}, bf16[3,80,320]{2,1,0:T(8,128)(2,1)S(1)}, u32[]{:S(2)}, u32[]{:S(2)}) collective-permute-start(bf16[3,80,320]{2,1,0:T(8,128)(2,1)S(1)} %get-tuple-element.85), channel_id=1, source_target_pairs={{0,24},{8,16},{16,8},{24,0},{1,25},{9,17},{17,9},{25,1},{2,26},{10... | collective-permute-start | bytes 460808 | tf_op jit(solution)/shard_map/ppermute | solution.py:72
  6.6 4.1 %all-to-all-start = ((bf16[4,2,320,128]{3,2,1,0:T(8,128)(2,1)}), bf16[4,2,320,128]{3,2,1,0:T(8,128)(2,1)S(1)}, u32[]{:S(2)}, u32[]{:S(2)}) async-start(bf16[4,2,320,128]{3,2,1,0:T(8,128)(2,1)} %bitcast.11), calls=%async_computation | async-start | bytes 1310720 | tf_op jit(solution)/shard_map/all_to_all | solution.py:80
  11.4 4.0 %collective-permute-done.1.refs_3_ = bf16[3,80,320]{2,1,0:T(8,128)(2,1)S(1)} collective-permute-done((bf16[3,80,320]{2,1,0:T(8,128)(2,1)S(1)}, bf16[3,80,320]{2,1,0:T(8,128)(2,1)S(1)}, u32[]{:S(2)}, u32[]{:S(2)}) %collective-permute-start.1) | collective-permute-done | bytes 153632 | tf_op jit(solution)/shard_map/ppermute | solution.py:72
  16.0 1.7 %collective-permute-start.9 = (bf16[3,80,320]{2,1,0:T(8,128)(2,1)S(1)}, bf16[3,80,320]{2,1,0:T(8,128)(2,1)S(1)}, u32[]{:S(2)}, u32[]{:S(2)}) collective-permute-start(bf16[3,80,320]{2,1,0:T(8,128)(2,1)S(1)} %get-tuple-element.84), channel_id=1, source_target_pairs={{0,24},{8,16},{16,8},{24,0},{1,25},{9,17},{17,9},{25,1},{2,26},{10... | collective-permute-start | bytes 460808 | tf_op jit(solution)/shard_map/ppermute | solution.py:72
  17.7 1.2 %collective-permute-start.8 = (bf16[3,80,320]{2,1,0:T(8,128)(2,1)S(1)}, bf16[3,80,320]{2,1,0:T(8,128)(2,1)S(1)}, u32[]{:S(2)}, u32[]{:S(2)}) collective-permute-start(bf16[3,80,320]{2,1,0:T(8,128)(2,1)S(1)} %get-tuple-element.84), channel_id=1, source_target_pairs={{0,16},{8,24},{16,0},{24,8},{1,17},{9,25},{17,1},{25,9},{2,18},{10... | collective-permute-start | bytes 460808 | tf_op jit(solution)/shard_map/ppermute | solution.py:72
  18.9 2.4 %shard_map.76.refs_0_.far_taps = bf16[960,1280]{1,0:T(8,128)(2,1)} custom-call(bf16[8,320,128]{2,1,0:T(8,128)(2,1)S(1)} %bitcast.8), custom_call_target="tpu_custom_call" | custom-call | flops 3276801 | bytes 31129600 | tf_op jit(solution)/shard_map/pallas_call | solution.py:25
  22.0 2.1 %shard_map.75 = (bf16[320,960]{1,0:T(8,128)(2,1)}, bf16[320,960]{1,0:T(8,128)(2,1)}, bf16[320,960]{1,0:T(8,128)(2,1)}) custom-call(bf16[3,80,320]{2,1,0:T(8,128)(2,1)S(1)} %copy-done.2, bf16[9,80,320]{2,1,0:T(8,128)(2,1)S(1)} %copy-done.1, bf16[3,80,320]{2,1,0:T(8,128)(2,1)S(1)} %collective-permute-done.refs_2_, ...), custom_call_target="tpu_custom_call" | custom-call | flops 1966080000 | bytes 33792000 | tf_op jit(solution)/shard_map/pallas_call | solution.py:25
  24.1 2.7 %shard_map.77 = (bf16[2,320,128]{2,1,0:T(8,128)(2,1)}, bf16[2,320,128]{2,1,0:T(8,128)(2,1)}, bf16[2,320,128]{2,1,0:T(8,128)(2,1)}, bf16[2,320,128]{2,1,0:T(8,128)(2,1)}) custom-call(bf16[4,2,320,128]{3,2,1,0:T(8,128)(2,1)S(1)} %all-to-all-done.cot_ref, bf16[320,960]{1,0:T(8,128)(2,1)} %get-tuple-element.49.far_ref), custom_call_target="tpu_custom_call" | custom-call | flops 6291456000 | bytes 19251200 | tf_op jit(solution)/shard_map/pallas_call | solution.py:25
  26.9 2.5 %collective-permute-done.8.refs_4_ = bf16[3,80,320]{2,1,0:T(8,128)(2,1)S(1)} collective-permute-done((bf16[3,80,320]{2,1,0:T(8,128)(2,1)S(1)}, bf16[3,80,320]{2,1,0:T(8,128)(2,1)S(1)}, u32[]{:S(2)}, u32[]{:S(2)}) %collective-permute-start.8) | collective-permute-done | bytes 153632 | tf_op jit(solution)/shard_map/ppermute | solution.py:72
  30.8 1.5 %collective-permute-start.13 = (bf16[2,320,128]{2,1,0:T(8,128)(2,1)}, bf16[2,320,128]{2,1,0:T(8,128)(2,1)}, u32[]{:S(2)}, u32[]{:S(2)}) collective-permute-start(bf16[2,320,128]{2,1,0:T(8,128)(2,1)} %get-tuple-element.56), channel_id=1, source_target_pairs={{0,8},{8,0},{16,24},{24,16},{1,9},{9,1},{17,25},{25,17},{2,10},{10... | collective-permute-start | bytes 491528 | tf_op jit(solution)/shard_map/ppermute | solution.py:72
  32.2 1.4 %collective-permute-start.14 = (bf16[2,320,128]{2,1,0:T(8,128)(2,1)}, bf16[2,320,128]{2,1,0:T(8,128)(2,1)}, u32[]{:S(2)}, u32[]{:S(2)}) collective-permute-start(bf16[2,320,128]{2,1,0:T(8,128)(2,1)} %get-tuple-element.57), channel_id=1, source_target_pairs={{0,16},{8,24},{16,0},{24,8},{1,17},{9,25},{17,1},{25,9},{2,18},{10... | collective-permute-start | bytes 491528 | tf_op jit(solution)/shard_map/ppermute | solution.py:72
  35.0 5.7 %shard_map.78 = (bf16[8,320,128]{2,1,0:T(8,128)(2,1)S(1)}, bf16[8,320,128]{2,1,0:T(8,128)(2,1)}, bf16[3,320,960]{2,1,0:T(8,128)(2,1)}) custom-call(bf16[960,1280]{1,0:T(8,128)(2,1)} %shard_map.76.refs_0_.far_taps, bf16[320,960]{1,0:T(8,128)(2,1)} %get-tuple-element.46.refs_1_, bf16[9,80,320]{2,1,0:T(8,128)(2,1)} %refs_2_.1, bf16[3,80,320]{2,1,0:T(8,128)(2,1)} %copy-done.8, ...), custom_call_target="tpu_custom_call" | custom-call | flops 18874368000 | bytes 76083200 | tf_op jit(solution)/shard_map/pallas_call | solution.py:25
  40.7 3.6 %all-to-all-start.1 = ((bf16[4,2,320,128]{3,2,1,0:T(8,128)(2,1)}), bf16[4,2,320,128]{3,2,1,0:T(8,128)(2,1)S(1)}, u32[]{:S(2)}, u32[]{:S(2)}) async-start(bf16[4,2,320,128]{3,2,1,0:T(8,128)(2,1)} %bitcast.13), calls=%async_computation.1 | async-start | bytes 1310720 | tf_op jit(solution)/shard_map/all_to_all | solution.py:80
  44.2 2.6 %shard_map.79 = (bf16[160,1024]{1,0:T(8,128)(2,1)S(1)}, bf16[160,1024]{1,0:T(8,128)(2,1)S(1)}, bf16[8,320,128]{2,1,0:T(8,128)(2,1)}) custom-call(bf16[8,320,128]{2,1,0:T(8,128)(2,1)S(1)} %get-tuple-element.55.pre_ref, bf16[2,320,128]{2,1,0:T(8,128)(2,1)S(1)} %copy-done.3, bf16[2,320,128]{2,1,0:T(8,128)(2,1)} %collective-permute-done.13.refs_1_, ...), custom_call_target="tpu_custom_call" | custom-call | flops 65536000 | bytes 26214400 | tf_op jit(solution)/shard_map/pallas_call | solution.py:25
  46.9 2.5 %shard_map.80.far_other = bf16[960,1280]{1,0:T(8,128)(2,1)} custom-call(bf16[8,320,128]{2,1,0:T(8,128)(2,1)S(1)} %collective-permute-done.6.frames_ref), custom_call_target="tpu_custom_call" | custom-call | flops 1 | bytes 1 | tf_op jit(solution)/shard_map/pallas_call | solution.py:25
  49.4 5.6 %shard_map.81 = (f32[3,40,960]{2,1,0:T(8,128)S(1)}, bf16[3,40,960]{2,1,0:T(8,128)(2,1)}, bf16[3,40,960]{2,1,0:T(8,128)(2,1)}, bf16[3,40,960]{2,1,0:T(8,128)(2,1)}) custom-call(bf16[960,1280]{1,0:T(8,128)(2,1)} %shard_map.76.refs_0_.far_taps, bf16[960,1280]{1,0:T(8,128)(2,1)} %shard_map.80.far_other, bf16[160,1024]{1,0:T(8,128)(2,1)S(1)} %get-tuple-element.61.mine_ref, ...), custom_call_target="tpu_custom_call" | custom-call | flops 1 | bytes 1 | tf_op jit(solution)/shard_map/pallas_call | solution.py:25
  56.6 2.0 %collective-permute-start.18 = (bf16[3,40,960]{2,1,0:T(8,128)(2,1)}, bf16[3,40,960]{2,1,0:T(8,128)(2,1)S(1)}, u32[]{:S(2)}, u32[]{:S(2)}) collective-permute-start(bf16[3,40,960]{2,1,0:T(8,128)(2,1)} %get-tuple-element.70), channel_id=1, source_target_pairs={{0,8},{8,0},{16,24},{24,16},{1,9},{9,1},{17,25},{25,17},{2,10},{10... | collective-permute-start | bytes 691208 | tf_op jit(solution)/shard_map/ppermute | solution.py:72
  58.6 1.5 %collective-permute-start.19 = (bf16[3,40,960]{2,1,0:T(8,128)(2,1)S(1)}, bf16[3,40,960]{2,1,0:T(8,128)(2,1)S(1)}, u32[]{:S(2)}, u32[]{:S(2)}) collective-permute-start(bf16[3,40,960]{2,1,0:T(8,128)(2,1)S(1)} %copy-done.5), channel_id=1, source_target_pairs={{0,16},{8,24},{16,0},{24,8},{1,17},{9,25},{17,1},{25,9},{2,18},{10... | collective-permute-start | bytes 691208 | tf_op jit(solution)/shard_map/ppermute | solution.py:72
  60.9 4.1 %all-to-all-start.2 = ((bf16[4,40,960]{2,1,0:T(8,128)(2,1)}), bf16[4,40,960]{2,1,0:T(8,128)(2,1)S(1)}, u32[]{:S(2)}, u32[]{:S(2)}) async-start(bf16[4,40,960]{2,1,0:T(8,128)(2,1)} %shard_map.83), calls=%async_computation.2 | async-start | bytes 655360 | tf_op jit(solution)/shard_map/all_to_all | solution.py:80
  65.1 2.8 %shard_map.84 = bf16[4,2,320,128]{3,2,1,0:T(8,128)(2,1)} custom-call(bf16[4,2,320,128]{3,2,1,0:T(8,128)(2,1)S(1)} %all-to-all-done.1.act_ref, bf16[320,960]{1,0:T(8,128)(2,1)} %get-tuple-element.68.far_ref), custom_call_target="tpu_custom_call" | custom-call | flops 6291456000 | bytes 19251200 | tf_op jit(solution)/shard_map/pallas_call | solution.py:25
  67.9 5.3 %collective-permute-done.19.refs_1_ = bf16[3,40,960]{2,1,0:T(8,128)(2,1)S(1)} collective-permute-done((bf16[3,40,960]{2,1,0:T(8,128)(2,1)S(1)}, bf16[3,40,960]{2,1,0:T(8,128)(2,1)S(1)}, u32[]{:S(2)}, u32[]{:S(2)}) %collective-permute-start.19) | collective-permute-done | bytes 230432 | tf_op jit(solution)/shard_map/ppermute | solution.py:72
  73.2 1.9 %all-to-all-done.2.temporal_ref = bf16[4,40,960]{2,1,0:T(8,128)(2,1)S(1)} async-done(((bf16[4,40,960]{2,1,0:T(8,128)(2,1)}), bf16[4,40,960]{2,1,0:T(8,128)(2,1)S(1)}, u32[]{:S(2)}, u32[]{:S(2)}) %all-to-all-start.2) | async-done | bytes 307232 | tf_op jit(solution)/shard_map/all_to_all | solution.py:80
  75.3 1.6 %collective-permute-start.21 = (bf16[2,40,960]{2,1,0:T(8,128)(2,1)S(1)}, bf16[2,40,960]{2,1,0:T(8,128)(2,1)S(1)}, u32[]{:S(2)}, u32[]{:S(2)}) collective-permute-start(bf16[2,40,960]{2,1,0:T(8,128)(2,1)S(1)} %get-tuple-element.74), channel_id=1, source_target_pairs={{0,2},{1,3},{2,0},{3,1},{4,6},{5,7},{6,4},{7,5},{8,10},{9,11},{10,... | collective-permute-start | bytes 460808 | tf_op jit(solution)/shard_map/ppermute | solution.py:72
  76.9 3.7 %all-to-all-start.3 = ((bf16[4,2,320,128]{3,2,1,0:T(8,128)(2,1)}), bf16[4,2,320,128]{3,2,1,0:T(8,128)(2,1)S(1)}, u32[]{:S(2)}, u32[]{:S(2)}) async-start(bf16[4,2,320,128]{3,2,1,0:T(8,128)(2,1)} %shard_map.84), calls=%async_computation.3 | async-start | bytes 1310720 | tf_op jit(solution)/shard_map/all_to_all | solution.py:80
  81.4 2.7 %collective-permute-start.22 = (bf16[2,40,960]{2,1,0:T(8,128)(2,1)S(1)}, bf16[2,40,960]{2,1,0:T(8,128)(2,1)S(1)}, u32[]{:S(2)}, u32[]{:S(2)}) collective-permute-start(bf16[2,40,960]{2,1,0:T(8,128)(2,1)S(1)} %shard_map.86.keep_ref), channel_id=1, source_target_pairs={{0,4},{1,5},{2,6},{3,7},{4,0},{5,1},{6,2},{7,3},{8,12},{9,13},{10,... | collective-permute-start | bytes 460808 | tf_op jit(solution)/shard_map/ppermute | solution.py:72
  84.1 7.3 %shard_map.87 = bf16[8,320,128]{2,1,0:T(8,128)(2,1)} custom-call(bf16[8,320,128]{2,1,0:T(8,128)(2,1)} %get-tuple-element.76.far_pg, bf16[8,320,128]{2,1,0:T(8,128)(2,1)} %bitcast.12, bf16[3,320,960]{2,1,0:T(8,128)(2,1)} %get-tuple-element.77.far_weights), custom_call_target="tpu_custom_call" | custom-call | flops 18874368000 | bytes 38092800 | tf_op jit(solution)/shard_map/pallas_call | solution.py:25
  91.5 1.6 %collective-permute-start.23 = (bf16[2,40,960]{2,1,0:T(8,128)(2,1)S(1)}, bf16[2,40,960]{2,1,0:T(8,128)(2,1)S(1)}, u32[]{:S(2)}, u32[]{:S(2)}) collective-permute-start(bf16[2,40,960]{2,1,0:T(8,128)(2,1)S(1)} %shard_map.88.own_ref), channel_id=1, source_target_pairs={{0,2},{1,3},{2,0},{3,1},{4,6},{5,7},{6,4},{7,5},{8,10},{9,11},{10,... | collective-permute-start | bytes 460808 | tf_op jit(solution)/shard_map/ppermute | solution.py:72
  93.1 1.0 shard_map.89
  94.1 2.7 %collective-permute-done.23.next_ref = bf16[2,40,960]{2,1,0:T(8,128)(2,1)S(1)} collective-permute-done((bf16[2,40,960]{2,1,0:T(8,128)(2,1)S(1)}, bf16[2,40,960]{2,1,0:T(8,128)(2,1)S(1)}, u32[]{:S(2)}, u32[]{:S(2)}) %collective-permute-start.23) | collective-permute-done | bytes 153632 | tf_op jit(solution)/shard_map/ppermute | solution.py:72
  96.9 1.4 %collective-permute-done.25.both_ref = bf16[2,40,960]{2,1,0:T(8,128)(2,1)S(1)} collective-permute-done((bf16[2,40,960]{2,1,0:T(8,128)(2,1)S(1)}, bf16[2,40,960]{2,1,0:T(8,128)(2,1)S(1)}, u32[]{:S(2)}, u32[]{:S(2)}) %collective-permute-start.25) | collective-permute-done | bytes 153632 | tf_op jit(solution)/shard_map/ppermute | solution.py:72
  98.2 1.4 %shard_map.90 = (f32[9,80,320]{2,1,0:T(8,128)}, f32[3,80,320]{2,1,0:T(8,128)}) custom-call(bf16[2,40,960]{2,1,0:T(8,128)(2,1)S(1)} %shard_map.88.own_ref, bf16[2,40,960]{2,1,0:T(8,128)(2,1)S(1)} %collective-permute-done.23.next_ref, bf16[2,40,960]{2,1,0:T(8,128)(2,1)S(1)} %collective-permute-done.24.core_ref, ...), custom_call_target="tpu_custom_call" | custom-call | flops 6144001 | bytes 18432000 | tf_op jit(solution)/shard_map/pallas_call | solution.py:25
  (69 shorter events, 8.9 us)
Async XLA Ops:
  1.9 20.0 %copy-start.1 = (bf16[9,80,320]{2,1,0:T(8,128)(2,1)S(1)}, bf16[9,80,320]{2,1,0:T(8,128)(2,1)}, u32[]{:S(2)}) copy-start(bf16[9,80,320]{2,1,0:T(8,128)(2,1)} %refs_2_.1) | copy-start | bytes 1382404
  2.0 20.0 %copy-start.2 = (bf16[3,80,320]{2,1,0:T(8,128)(2,1)S(1)}, bf16[3,80,320]{2,1,0:T(8,128)(2,1)}, u32[]{:S(2)}) copy-start(bf16[3,80,320]{2,1,0:T(8,128)(2,1)} %refs_0_.1) | copy-start | bytes 460804
  2.0 9.4 %collective-permute-start.2 = (bf16[3,80,320]{2,1,0:T(8,128)(2,1)S(1)}, bf16[3,80,320]{2,1,0:T(8,128)(2,1)S(1)}, u32[]{:S(2)}, u32[]{:S(2)}) collective-permute-start(bf16[3,80,320]{2,1,0:T(8,128)(2,1)S(1)} %get-tuple-element.85), channel_id=1, source_target_pairs={{0,24},{8,16},{16,8},{24,0},{1,25},{9,17},{17,9},{25,1},{2,26},{10... | collective-permute-start | bytes 460808 | tf_op jit(solution)/shard_map/ppermute | solution.py:72
  5.9 9.5 %collective-permute-start.1 = (bf16[3,80,320]{2,1,0:T(8,128)(2,1)S(1)}, bf16[3,80,320]{2,1,0:T(8,128)(2,1)S(1)}, u32[]{:S(2)}, u32[]{:S(2)}) collective-permute-start(bf16[3,80,320]{2,1,0:T(8,128)(2,1)S(1)} %get-tuple-element.85), channel_id=1, source_target_pairs={{0,16},{8,24},{16,0},{24,8},{1,17},{9,25},{17,1},{25,9},{2,18},{10... | collective-permute-start | bytes 460808 | tf_op jit(solution)/shard_map/ppermute | solution.py:72
  6.4 9.5 %collective-permute-start = (bf16[3,80,320]{2,1,0:T(8,128)(2,1)S(1)}, bf16[3,80,320]{2,1,0:T(8,128)(2,1)S(1)}, u32[]{:S(2)}, u32[]{:S(2)}) collective-permute-start(bf16[3,80,320]{2,1,0:T(8,128)(2,1)S(1)} %get-tuple-element.85), channel_id=1, source_target_pairs={{0,8},{8,0},{16,24},{24,16},{1,9},{9,1},{17,25},{25,17},{2,10},{10... | collective-permute-start | bytes 460808 | tf_op jit(solution)/shard_map/ppermute | solution.py:72
  6.6 17.5 %all-to-all-start = ((bf16[4,2,320,128]{3,2,1,0:T(8,128)(2,1)}), bf16[4,2,320,128]{3,2,1,0:T(8,128)(2,1)S(1)}, u32[]{:S(2)}, u32[]{:S(2)}) async-start(bf16[4,2,320,128]{3,2,1,0:T(8,128)(2,1)} %bitcast.11), calls=%async_computation | async-start | bytes 1310720 | tf_op jit(solution)/shard_map/all_to_all | solution.py:80
  11.4 9.9 %collective-permute-start.5 = (bf16[3,80,320]{2,1,0:T(8,128)(2,1)S(1)}, bf16[3,80,320]{2,1,0:T(8,128)(2,1)S(1)}, u32[]{:S(2)}, u32[]{:S(2)}) collective-permute-start(bf16[3,80,320]{2,1,0:T(8,128)(2,1)S(1)} %collective-permute-done.2.refs_4_), channel_id=1, source_target_pairs={{0,1},{1,0},{2,3},{3,2},{4,5},{5,4},{6,7},{7,6},{8,9},{9,8},{10,11... | collective-permute-start | bytes 460808 | tf_op jit(solution)/shard_map/ppermute | solution.py:72
  15.5 6.5 %collective-permute-start.4 = (bf16[3,80,320]{2,1,0:T(8,128)(2,1)S(1)}, bf16[3,80,320]{2,1,0:T(8,128)(2,1)S(1)}, u32[]{:S(2)}, u32[]{:S(2)}) collective-permute-start(bf16[3,80,320]{2,1,0:T(8,128)(2,1)S(1)} %collective-permute-done.1.refs_3_), channel_id=1, source_target_pairs={{0,1},{1,0},{2,3},{3,2},{4,5},{5,4},{6,7},{7,6},{8,9},{9,8},{10,11... | collective-permute-start | bytes 460808 | tf_op jit(solution)/shard_map/ppermute | solution.py:72
  16.0 6.0 %collective-permute-start.3 = (bf16[3,80,320]{2,1,0:T(8,128)(2,1)S(1)}, bf16[3,80,320]{2,1,0:T(8,128)(2,1)S(1)}, u32[]{:S(2)}, u32[]{:S(2)}) collective-permute-start(bf16[3,80,320]{2,1,0:T(8,128)(2,1)S(1)} %collective-permute-done.refs_2_), channel_id=1, source_target_pairs={{0,1},{1,0},{2,3},{3,2},{4,5},{5,4},{6,7},{7,6},{8,9},{9,8},{10,11... | collective-permute-start | bytes 460808 | tf_op jit(solution)/shard_map/ppermute | solution.py:72
  16.0 10.9 %collective-permute-start.9 = (bf16[3,80,320]{2,1,0:T(8,128)(2,1)S(1)}, bf16[3,80,320]{2,1,0:T(8,128)(2,1)S(1)}, u32[]{:S(2)}, u32[]{:S(2)}) collective-permute-start(bf16[3,80,320]{2,1,0:T(8,128)(2,1)S(1)} %get-tuple-element.84), channel_id=1, source_target_pairs={{0,24},{8,16},{16,8},{24,0},{1,25},{9,17},{17,9},{25,1},{2,26},{10... | collective-permute-start | bytes 460808 | tf_op jit(solution)/shard_map/ppermute | solution.py:72
  17.7 11.6 %collective-permute-start.8 = (bf16[3,80,320]{2,1,0:T(8,128)(2,1)S(1)}, bf16[3,80,320]{2,1,0:T(8,128)(2,1)S(1)}, u32[]{:S(2)}, u32[]{:S(2)}) collective-permute-start(bf16[3,80,320]{2,1,0:T(8,128)(2,1)S(1)} %get-tuple-element.84), channel_id=1, source_target_pairs={{0,16},{8,24},{16,0},{24,8},{1,17},{9,25},{17,1},{25,9},{2,18},{10... | collective-permute-start | bytes 460808 | tf_op jit(solution)/shard_map/ppermute | solution.py:72
  21.3 8.4 %collective-permute-start.7 = (bf16[3,80,320]{2,1,0:T(8,128)(2,1)S(1)}, bf16[3,80,320]{2,1,0:T(8,128)(2,1)S(1)}, u32[]{:S(2)}, u32[]{:S(2)}) collective-permute-start(bf16[3,80,320]{2,1,0:T(8,128)(2,1)S(1)} %get-tuple-element.84), channel_id=1, source_target_pairs={{0,8},{8,0},{16,24},{24,16},{1,9},{9,1},{17,25},{25,17},{2,10},{10... | collective-permute-start | bytes 460808 | tf_op jit(solution)/shard_map/ppermute | solution.py:72
  29.7 2.5 %collective-permute-start.10 = (bf16[3,80,320]{2,1,0:T(8,128)(2,1)S(1)}, bf16[3,80,320]{2,1,0:T(8,128)(2,1)S(1)}, u32[]{:S(2)}, u32[]{:S(2)}) collective-permute-start(bf16[3,80,320]{2,1,0:T(8,128)(2,1)S(1)} %collective-permute-done.7.refs_3_), channel_id=1, source_target_pairs={{0,1},{1,0},{2,3},{3,2},{4,5},{5,4},{6,7},{7,6},{8,9},{9,8},{10,11... | collective-permute-start | bytes 460808 | tf_op jit(solution)/shard_map/ppermute | solution.py:72
  29.7 3.9 %collective-permute-start.11 = (bf16[3,80,320]{2,1,0:T(8,128)(2,1)S(1)}, bf16[3,80,320]{2,1,0:T(8,128)(2,1)S(1)}, u32[]{:S(2)}, u32[]{:S(2)}) collective-permute-start(bf16[3,80,320]{2,1,0:T(8,128)(2,1)S(1)} %collective-permute-done.8.refs_4_), channel_id=1, source_target_pairs={{0,1},{1,0},{2,3},{3,2},{4,5},{5,4},{6,7},{7,6},{8,9},{9,8},{10,11... | collective-permute-start | bytes 460808 | tf_op jit(solution)/shard_map/ppermute | solution.py:72
  30.2 4.0 %collective-permute-start.12 = (bf16[3,80,320]{2,1,0:T(8,128)(2,1)S(1)}, bf16[3,80,320]{2,1,0:T(8,128)(2,1)S(1)}, u32[]{:S(2)}, u32[]{:S(2)}) collective-permute-start(bf16[3,80,320]{2,1,0:T(8,128)(2,1)S(1)} %collective-permute-done.9.refs_5_), channel_id=1, source_target_pairs={{0,1},{1,0},{2,3},{3,2},{4,5},{5,4},{6,7},{7,6},{8,9},{9,8},{10,11... | collective-permute-start | bytes 460808 | tf_op jit(solution)/shard_map/ppermute | solution.py:72
  30.3 16.7 %collective-permute-start.6 = (bf16[8,320,128]{2,1,0:T(8,128)(2,1)S(1)}, bf16[8,320,128]{2,1,0:T(8,128)(2,1)S(1)}, u32[]{:S(2)}, u32[]{:S(2)}) collective-permute-start(bf16[8,320,128]{2,1,0:T(8,128)(2,1)S(1)} %bitcast.9), channel_id=1, source_target_pairs={{0,1},{1,0},{2,3},{3,2},{4,5},{5,4},{6,7},{7,6},{8,9},{9,8},{10,11... | collective-permute-start | bytes 1966088 | tf_op jit(solution)/shard_map/ppermute | solution.py:72
  30.8 13.5 %collective-permute-start.13 = (bf16[2,320,128]{2,1,0:T(8,128)(2,1)}, bf16[2,320,128]{2,1,0:T(8,128)(2,1)}, u32[]{:S(2)}, u32[]{:S(2)}) collective-permute-start(bf16[2,320,128]{2,1,0:T(8,128)(2,1)} %get-tuple-element.56), channel_id=1, source_target_pairs={{0,8},{8,0},{16,24},{24,16},{1,9},{9,1},{17,25},{25,17},{2,10},{10... | collective-permute-start | bytes 491528 | tf_op jit(solution)/shard_map/ppermute | solution.py:72
  32.2 12.0 %collective-permute-start.14 = (bf16[2,320,128]{2,1,0:T(8,128)(2,1)}, bf16[2,320,128]{2,1,0:T(8,128)(2,1)}, u32[]{:S(2)}, u32[]{:S(2)}) collective-permute-start(bf16[2,320,128]{2,1,0:T(8,128)(2,1)} %get-tuple-element.57), channel_id=1, source_target_pairs={{0,16},{8,24},{16,0},{24,8},{1,17},{9,25},{17,1},{25,9},{2,18},{10... | collective-permute-start | bytes 491528 | tf_op jit(solution)/shard_map/ppermute | solution.py:72
  33.7 10.6 %collective-permute-start.15 = (bf16[2,320,128]{2,1,0:T(8,128)(2,1)}, bf16[2,320,128]{2,1,0:T(8,128)(2,1)}, u32[]{:S(2)}, u32[]{:S(2)}) collective-permute-start(bf16[2,320,128]{2,1,0:T(8,128)(2,1)} %get-tuple-element.58), channel_id=1, source_target_pairs={{0,24},{8,16},{16,8},{24,0},{1,25},{9,17},{17,9},{25,1},{2,26},{10... | collective-permute-start | bytes 491528 | tf_op jit(solution)/shard_map/ppermute | solution.py:72
  40.7 14.4 %all-to-all-start.1 = ((bf16[4,2,320,128]{3,2,1,0:T(8,128)(2,1)}), bf16[4,2,320,128]{3,2,1,0:T(8,128)(2,1)S(1)}, u32[]{:S(2)}, u32[]{:S(2)}) async-start(bf16[4,2,320,128]{3,2,1,0:T(8,128)(2,1)} %bitcast.13), calls=%async_computation.1 | async-start | bytes 1310720 | tf_op jit(solution)/shard_map/all_to_all | solution.py:80
  46.8 2.6 %collective-permute-start.16 = (bf16[160,1024]{1,0:T(8,128)(2,1)S(1)}, bf16[160,1024]{1,0:T(8,128)(2,1)S(1)}, u32[]{:S(2)}, u32[]{:S(2)}) collective-permute-start(bf16[160,1024]{1,0:T(8,128)(2,1)S(1)} %get-tuple-element.59), channel_id=1, source_target_pairs={{0,1},{1,0},{2,3},{3,2},{4,5},{5,4},{6,7},{7,6},{8,9},{9,8},{10,11... | collective-permute-start | bytes 983048 | tf_op jit(solution)/shard_map/ppermute | solution.py:72
  56.0 4.1 %collective-permute-start.17 = (bf16[4,40,960]{2,1,0:T(8,128)(2,1)S(1)}, bf16[4,40,960]{2,1,0:T(8,128)(2,1)S(1)}, u32[]{:S(2)}, u32[]{:S(2)}) collective-permute-start(bf16[4,40,960]{2,1,0:T(8,128)(2,1)S(1)} %get-tuple-element.67), channel_id=1, source_target_pairs={{0,1},{1,0},{2,3},{3,2},{4,5},{5,4},{6,7},{7,6},{8,9},{9,8},{10,11... | collective-permute-start | bytes 921608 | tf_op jit(solution)/shard_map/ppermute | solution.py:72
  56.6 11.3 %collective-permute-start.18 = (bf16[3,40,960]{2,1,0:T(8,128)(2,1)}, bf16[3,40,960]{2,1,0:T(8,128)(2,1)S(1)}, u32[]{:S(2)}, u32[]{:S(2)}) collective-permute-start(bf16[3,40,960]{2,1,0:T(8,128)(2,1)} %get-tuple-element.70), channel_id=1, source_target_pairs={{0,8},{8,0},{16,24},{24,16},{1,9},{9,1},{17,25},{25,17},{2,10},{10... | collective-permute-start | bytes 691208 | tf_op jit(solution)/shard_map/ppermute | solution.py:72
  58.6 14.5 %collective-permute-start.19 = (bf16[3,40,960]{2,1,0:T(8,128)(2,1)S(1)}, bf16[3,40,960]{2,1,0:T(8,128)(2,1)S(1)}, u32[]{:S(2)}, u32[]{:S(2)}) collective-permute-start(bf16[3,40,960]{2,1,0:T(8,128)(2,1)S(1)} %copy-done.5), channel_id=1, source_target_pairs={{0,16},{8,24},{16,0},{24,8},{1,17},{9,25},{17,1},{25,9},{2,18},{10... | collective-permute-start | bytes 691208 | tf_op jit(solution)/shard_map/ppermute | solution.py:72
  60.1 13.1 %collective-permute-start.20 = (bf16[3,40,960]{2,1,0:T(8,128)(2,1)S(1)}, bf16[3,40,960]{2,1,0:T(8,128)(2,1)S(1)}, u32[]{:S(2)}, u32[]{:S(2)}) collective-permute-start(bf16[3,40,960]{2,1,0:T(8,128)(2,1)S(1)} %copy-done.4), channel_id=1, source_target_pairs={{0,24},{8,16},{16,8},{24,0},{1,25},{9,17},{17,9},{25,1},{2,26},{10... | collective-permute-start | bytes 691208 | tf_op jit(solution)/shard_map/ppermute | solution.py:72
  60.9 14.1 %all-to-all-start.2 = ((bf16[4,40,960]{2,1,0:T(8,128)(2,1)}), bf16[4,40,960]{2,1,0:T(8,128)(2,1)S(1)}, u32[]{:S(2)}, u32[]{:S(2)}) async-start(bf16[4,40,960]{2,1,0:T(8,128)(2,1)} %shard_map.83), calls=%async_computation.2 | async-start | bytes 655360 | tf_op jit(solution)/shard_map/all_to_all | solution.py:80
  75.3 6.1 %collective-permute-start.21 = (bf16[2,40,960]{2,1,0:T(8,128)(2,1)S(1)}, bf16[2,40,960]{2,1,0:T(8,128)(2,1)S(1)}, u32[]{:S(2)}, u32[]{:S(2)}) collective-permute-start(bf16[2,40,960]{2,1,0:T(8,128)(2,1)S(1)} %get-tuple-element.74), channel_id=1, source_target_pairs={{0,2},{1,3},{2,0},{3,1},{4,6},{5,7},{6,4},{7,5},{8,10},{9,11},{10,... | collective-permute-start | bytes 460808 | tf_op jit(solution)/shard_map/ppermute | solution.py:72
  76.9 16.2 %all-to-all-start.3 = ((bf16[4,2,320,128]{3,2,1,0:T(8,128)(2,1)}), bf16[4,2,320,128]{3,2,1,0:T(8,128)(2,1)S(1)}, u32[]{:S(2)}, u32[]{:S(2)}) async-start(bf16[4,2,320,128]{3,2,1,0:T(8,128)(2,1)} %shard_map.84), calls=%async_computation.3 | async-start | bytes 1310720 | tf_op jit(solution)/shard_map/all_to_all | solution.py:80
  81.4 10.0 %collective-permute-start.22 = (bf16[2,40,960]{2,1,0:T(8,128)(2,1)S(1)}, bf16[2,40,960]{2,1,0:T(8,128)(2,1)S(1)}, u32[]{:S(2)}, u32[]{:S(2)}) collective-permute-start(bf16[2,40,960]{2,1,0:T(8,128)(2,1)S(1)} %shard_map.86.keep_ref), channel_id=1, source_target_pairs={{0,4},{1,5},{2,6},{3,7},{4,0},{5,1},{6,2},{7,3},{8,12},{9,13},{10,... | collective-permute-start | bytes 460808 | tf_op jit(solution)/shard_map/ppermute | solution.py:72
  91.5 5.4 %collective-permute-start.23 = (bf16[2,40,960]{2,1,0:T(8,128)(2,1)S(1)}, bf16[2,40,960]{2,1,0:T(8,128)(2,1)S(1)}, u32[]{:S(2)}, u32[]{:S(2)}) collective-permute-start(bf16[2,40,960]{2,1,0:T(8,128)(2,1)S(1)} %shard_map.88.own_ref), channel_id=1, source_target_pairs={{0,2},{1,3},{2,0},{3,1},{4,6},{5,7},{6,4},{7,5},{8,10},{9,11},{10,... | collective-permute-start | bytes 460808 | tf_op jit(solution)/shard_map/ppermute | solution.py:72
  93.1 3.7 %collective-permute-start.24 = (bf16[2,40,960]{2,1,0:T(8,128)(2,1)S(1)}, bf16[2,40,960]{2,1,0:T(8,128)(2,1)S(1)}, u32[]{:S(2)}, u32[]{:S(2)}) collective-permute-start(bf16[2,40,960]{2,1,0:T(8,128)(2,1)S(1)} %shard_map.88.own_ref), channel_id=1, source_target_pairs={{0,1},{1,0},{2,3},{3,2},{4,5},{5,4},{6,7},{7,6},{8,9},{9,8},{10,11... | collective-permute-start | bytes 460808 | tf_op jit(solution)/shard_map/ppermute | solution.py:72
  96.9 1.4 %collective-permute-start.25 = (bf16[2,40,960]{2,1,0:T(8,128)(2,1)S(1)}, bf16[2,40,960]{2,1,0:T(8,128)(2,1)S(1)}, u32[]{:S(2)}, u32[]{:S(2)}) collective-permute-start(bf16[2,40,960]{2,1,0:T(8,128)(2,1)S(1)} %collective-permute-done.23.next_ref), channel_id=1, source_target_pairs={{0,1},{1,0},{2,3},{3,2},{4,5},{5,4},{6,7},{7,6},{8,9},{9,8},{10,11... | collective-permute-start | bytes 460808 | tf_op jit(solution)/shard_map/ppermute | solution.py:72
  (10 other events, 57.7 us)

commit v5 on v4

--- a/solution.py
+++ b/solution.py
@@ -706,23 +706,22 @@
     got_a = spread([mine_a] * (seq - 1))
     cot_rows = exchange(cotangent.reshape(seq, rows // seq, chans, width))
     got_b = spread([mine_b] * (seq - 1))
+    taps = window_taps(frames)
+    other_taps = window_taps(swap(after(frames, mine_a), "dp", 1))
+    taps, other_taps, *got_a = lax.optimization_barrier((taps, other_taps, *got_a))
     pair_a = [swap(piece, "dp", 1) for piece in got_a]
     temporal_t, temporal_w, middle = kernel_maps(
         temporal_kernel, spatial_kernel, got_a, pair_a
     )
-    taps = window_taps(frames)
-    temporal_t, taps = lax.optimization_barrier((temporal_t, taps))
     grad_rows = temporal_backward(cot_rows, temporal_t)
     act_grad = [grad_rows[0], *spread(grad_rows[1:])]
     temporal_w, *got_b = lax.optimization_barrier((after(temporal_w, grad_rows[0]), *got_b))
     pair_b = [swap(piece, "dp", 1) for piece in got_b]
-    other_frames = swap(after(frames, middle), "dp", 1)
     pre_act, activated, weights = spatial_forward(
         taps, spatial_kernel, middle, (*got_b, *pair_b), rows
     )
     half_mine, half_theirs, pre_grad = activation_grad(pre_act, act_grad, shard)
     half_other = swap(half_theirs, "dp", 1)
-    other_taps = window_taps(after(other_frames, half_theirs), weight=0)
     act_rows = exchange(activated.reshape(cot_rows.shape))
     spatial_keep, *spatial_send = spatial_weight_grad(
         taps, other_taps, half_mine, half_other, seq, scale, rows

time: 100 us -> 98.7 us (0.987)
  Pallas kernels: 38 us -> 37 us
    all_to_all x4, waiting for transfers between devices: 1.9 us -> 3.15 us  [exchange(): return lax.all_to_all(blocks, 'seq', 0, 0, tiled=True)]
    ppermute x26, waiting for transfers between devices: 18.4 us -> 17.3 us  [swap(): return lax.ppermute(values, axis, [(i, i ^ bit) for i in range(size)])]
    pallas_call x16, Pallas kernels: 38 us -> 37 us  [call(): pl.pallas_call(body, out_shape=tuple((pltpu.HBM(out.shape, out.dtype) if...]
  transfers between devices with their start and end apart: 30 -> 30, of which waited for: 10 -> 12; matrix products, arithmetic and copies ran while one was open for 0% -> 0% of each run, Pallas kernels for 36% -> 35%
where the time goes in v5:
time: 98.7 us; the launch traced here: 98.3 us
  starting transfers between devices  37.8 us (38%)
  Pallas kernels  37 us (37%)
  waiting for transfers between devices  20.5 us (21%)
  other arithmetic  1.3 us (1%)
    pallas_call x16, Pallas kernels, call(): pl.pallas_call(body, out_shape=tuple((pltpu.HBM(out.shape, out.dtype) if...  37 us
    ppermute x26, starting transfers between devices, swap(): return lax.ppermute(values, axis, [(i, i ^ bit) for i in range(size)])  22.4 us
    ppermute x26, waiting for transfers between devices, swap(): return lax.ppermute(values, axis, [(i, i ^ bit) for i in range(size)])  17.3 us
    all_to_all x4, starting transfers between devices, exchange(): return lax.all_to_all(blocks, 'seq', 0, 0, tiled=True)  15.4 us
    all_to_all x4, waiting for transfers between devices, exchange(): return lax.all_to_all(blocks, 'seq', 0, 0, tiled=True)  3.15 us
  transfers between devices with their start and end apart: 30, of which 12 were waited for; matrix products, arithmetic and copies ran while one was open for 0% of the time, Pallas kernels for 35%

profile of v5, /device:TPU:0, one launch (start us, length us, event | category | flops | bytes accessed | tf_op | source)
XLA Modules:
  0.0 98.3 jit_solution(1113697835774621347)
XLA Ops:
  0.6 1.3 %slice_select_fusion = (bf16[3,80,320]{2,1,0:T(8,128)(2,1)S(1)}, bf16[3,80,320]{2,1,0:T(8,128)(2,1)S(1)}) fusion(bf16[9,80,320]{2,1,0:T(8,128)(2,1)} %refs_2_.1, pred[]{:T(512)S(6)} %eq.3, bf16[3,80,320]{2,1,0:T(8,128)(2,1)} %refs_0_.1), kind=kLoop, calls=%fused_computation | loop fusion | flops 153600 | bytes 921601 | tf_op jit(solution)/shard_map/jit(_where)/select_n | solution.py:705
  2.4 3.6 %collective-permute-start.3 = (bf16[3,80,320]{2,1,0:T(8,128)(2,1)S(1)}, bf16[3,80,320]{2,1,0:T(8,128)(2,1)S(1)}, u32[]{:S(2)}, u32[]{:S(2)}) collective-permute-start(bf16[3,80,320]{2,1,0:T(8,128)(2,1)S(1)} %get-tuple-element.89), channel_id=1, source_target_pairs={{0,24},{8,16},{16,8},{24,0},{1,25},{9,17},{17,9},{25,1},{2,26},{10... | collective-permute-start | bytes 460808 | tf_op jit(solution)/shard_map/ppermute | solution.py:72
  6.6 4.1 %all-to-all-start = ((bf16[4,2,320,128]{3,2,1,0:T(8,128)(2,1)}), bf16[4,2,320,128]{3,2,1,0:T(8,128)(2,1)S(1)}, u32[]{:S(2)}, u32[]{:S(2)}) async-start(bf16[4,2,320,128]{3,2,1,0:T(8,128)(2,1)} %bitcast.11), calls=%async_computation | async-start | bytes 1310720 | tf_op jit(solution)/shard_map/all_to_all | solution.py:80
  10.8 2.4 %shard_map.75.refs_0_.far_taps = bf16[960,1280]{1,0:T(8,128)(2,1)} custom-call(bf16[8,320,128]{2,1,0:T(8,128)(2,1)S(1)} %bitcast.9), custom_call_target="tpu_custom_call" | custom-call | flops 3276801 | bytes 31129600 | tf_op jit(solution)/shard_map/pallas_call | solution.py:25
  13.2 2.5 %shard_map.76.far_other = bf16[960,1280]{1,0:T(8,128)(2,1)} custom-call(bf16[8,320,128]{2,1,0:T(8,128)(2,1)S(1)} %collective-permute-done.frames_ref), custom_call_target="tpu_custom_call" | custom-call | flops 3276801 | bytes 31129600 | tf_op jit(solution)/shard_map/pallas_call | solution.py:25
  16.4 2.8 %collective-permute-start.9 = (bf16[3,80,320]{2,1,0:T(8,128)(2,1)S(1)}, bf16[3,80,320]{2,1,0:T(8,128)(2,1)S(1)}, u32[]{:S(2)}, u32[]{:S(2)}) collective-permute-start(bf16[3,80,320]{2,1,0:T(8,128)(2,1)S(1)} %get-tuple-element.88), channel_id=1, source_target_pairs={{0,24},{8,16},{16,8},{24,0},{1,25},{9,17},{17,9},{25,1},{2,26},{10... | collective-permute-start | bytes 460808 | tf_op jit(solution)/shard_map/ppermute | solution.py:72
  20.0 2.1 %shard_map.77 = (bf16[320,960]{1,0:T(8,128)(2,1)}, bf16[320,960]{1,0:T(8,128)(2,1)}, bf16[320,960]{1,0:T(8,128)(2,1)}) custom-call(bf16[3,80,320]{2,1,0:T(8,128)(2,1)S(1)} %copy-done.2, bf16[9,80,320]{2,1,0:T(8,128)(2,1)S(1)} %copy-done.1, bf16[3,80,320]{2,1,0:T(8,128)(2,1)S(1)} %collective-permute-done.1.refs_2_, ...), custom_call_target="tpu_custom_call" | custom-call | flops 1966080000 | bytes 33792000 | tf_op jit(solution)/shard_map/pallas_call | solution.py:25
  23.0 2.7 %shard_map.78 = (bf16[2,320,128]{2,1,0:T(8,128)(2,1)}, bf16[2,320,128]{2,1,0:T(8,128)(2,1)}, bf16[2,320,128]{2,1,0:T(8,128)(2,1)}, bf16[2,320,128]{2,1,0:T(8,128)(2,1)}) custom-call(bf16[4,2,320,128]{3,2,1,0:T(8,128)(2,1)S(1)} %all-to-all-done.cot_ref, bf16[320,960]{1,0:T(8,128)(2,1)} %get-tuple-element.54.far_ref), custom_call_target="tpu_custom_call" | custom-call | flops 6291456000 | bytes 19251200 | tf_op jit(solution)/shard_map/pallas_call | solution.py:25
  26.5 3.6 %collective-permute-done.8.refs_4_ = bf16[3,80,320]{2,1,0:T(8,128)(2,1)S(1)} collective-permute-done((bf16[3,80,320]{2,1,0:T(8,128)(2,1)S(1)}, bf16[3,80,320]{2,1,0:T(8,128)(2,1)S(1)}, u32[]{:S(2)}, u32[]{:S(2)}) %collective-permute-start.8) | collective-permute-done | bytes 153632 | tf_op jit(solution)/shard_map/ppermute | solution.py:72
  31.0 1.5 %collective-permute-start.13 = (bf16[2,320,128]{2,1,0:T(8,128)(2,1)}, bf16[2,320,128]{2,1,0:T(8,128)(2,1)S(1)}, u32[]{:S(2)}, u32[]{:S(2)}) collective-permute-start(bf16[2,320,128]{2,1,0:T(8,128)(2,1)} %get-tuple-element.61), channel_id=1, source_target_pairs={{0,8},{8,0},{16,24},{24,16},{1,9},{9,1},{17,25},{25,17},{2,10},{10... | collective-permute-start | bytes 491528 | tf_op jit(solution)/shard_map/ppermute | solution.py:72
  32.5 1.5 %collective-permute-start.14 = (bf16[2,320,128]{2,1,0:T(8,128)(2,1)}, bf16[2,320,128]{2,1,0:T(8,128)(2,1)S(1)}, u32[]{:S(2)}, u32[]{:S(2)}) collective-permute-start(bf16[2,320,128]{2,1,0:T(8,128)(2,1)} %get-tuple-element.62), channel_id=1, source_target_pairs={{0,16},{8,24},{16,0},{24,8},{1,17},{9,25},{17,1},{25,9},{2,18},{10... | collective-permute-start | bytes 491528 | tf_op jit(solution)/shard_map/ppermute | solution.py:72
  35.4 5.7 %shard_map.79 = (bf16[8,320,128]{2,1,0:T(8,128)(2,1)S(1)}, bf16[8,320,128]{2,1,0:T(8,128)(2,1)}, bf16[3,320,960]{2,1,0:T(8,128)(2,1)}) custom-call(bf16[960,1280]{1,0:T(8,128)(2,1)} %shard_map.75.refs_0_.far_taps, bf16[320,960]{1,0:T(8,128)(2,1)} %get-tuple-element.52.refs_1_, bf16[9,80,320]{2,1,0:T(8,128)(2,1)} %refs_2_.1, bf16[3,80,320]{2,1,0:T(8,128)(2,1)} %copy-done.8, ...), custom_call_target="tpu_custom_call" | custom-call | flops 18874368000 | bytes 76083200 | tf_op jit(solution)/shard_map/pallas_call | solution.py:25
  41.0 3.7 %all-to-all-start.1 = ((bf16[4,2,320,128]{3,2,1,0:T(8,128)(2,1)}), bf16[4,2,320,128]{3,2,1,0:T(8,128)(2,1)S(1)}, u32[]{:S(2)}, u32[]{:S(2)}) async-start(bf16[4,2,320,128]{3,2,1,0:T(8,128)(2,1)} %bitcast.13), calls=%async_computation.1 | async-start | bytes 1310720 | tf_op jit(solution)/shard_map/all_to_all | solution.py:80
  44.8 1.5 %shard_map.80 = (bf16[160,1024]{1,0:T(8,128)(2,1)S(1)}, bf16[160,1024]{1,0:T(8,128)(2,1)S(1)}, bf16[8,320,128]{2,1,0:T(8,128)(2,1)}) custom-call(bf16[8,320,128]{2,1,0:T(8,128)(2,1)S(1)} %get-tuple-element.60.pre_ref, bf16[2,320,128]{2,1,0:T(8,128)(2,1)S(1)} %copy-done.3, bf16[2,320,128]{2,1,0:T(8,128)(2,1)S(1)} %collective-permute-done.13.refs_1_, ...), custom_call_target="tpu_custom_call" | custom-call | flops 65536000 | bytes 26214400 | tf_op jit(solution)/shard_map/pallas_call | solution.py:25
  46.4 1.6 %collective-permute-done.16.theirs_ref = bf16[160,1024]{1,0:T(8,128)(2,1)S(1)} collective-permute-done((bf16[160,1024]{1,0:T(8,128)(2,1)S(1)}, bf16[160,1024]{1,0:T(8,128)(2,1)S(1)}, u32[]{:S(2)}, u32[]{:S(2)}) %collective-permute-start.16) | collective-permute-done | bytes 327712 | tf_op jit(solution)/shard_map/ppermute | solution.py:72
  48.0 5.6 %shard_map.81 = (f32[3,40,960]{2,1,0:T(8,128)S(1)}, bf16[3,40,960]{2,1,0:T(8,128)(2,1)}, bf16[3,40,960]{2,1,0:T(8,128)(2,1)}, bf16[3,40,960]{2,1,0:T(8,128)(2,1)}) custom-call(bf16[960,1280]{1,0:T(8,128)(2,1)} %shard_map.75.refs_0_.far_taps, bf16[960,1280]{1,0:T(8,128)(2,1)} %shard_map.76.far_other, bf16[160,1024]{1,0:T(8,128)(2,1)S(1)} %get-tuple-element.64.mine_ref, ...), custom_call_target="tpu_custom_call" | custom-call | flops 1 | bytes 1 | tf_op jit(solution)/shard_map/pallas_call | solution.py:25
  55.1 1.8 %collective-permute-start.18 = (bf16[3,40,960]{2,1,0:T(8,128)(2,1)}, bf16[3,40,960]{2,1,0:T(8,128)(2,1)S(1)}, u32[]{:S(2)}, u32[]{:S(2)}) collective-permute-start(bf16[3,40,960]{2,1,0:T(8,128)(2,1)} %get-tuple-element.74), channel_id=1, source_target_pairs={{0,8},{8,0},{16,24},{24,16},{1,9},{9,1},{17,25},{25,17},{2,10},{10... | collective-permute-start | bytes 691208 | tf_op jit(solution)/shard_map/ppermute | solution.py:72
  56.9 1.5 %collective-permute-start.19 = (bf16[3,40,960]{2,1,0:T(8,128)(2,1)S(1)}, bf16[3,40,960]{2,1,0:T(8,128)(2,1)S(1)}, u32[]{:S(2)}, u32[]{:S(2)}) collective-permute-start(bf16[3,40,960]{2,1,0:T(8,128)(2,1)S(1)} %copy-done.5), channel_id=1, source_target_pairs={{0,16},{8,24},{16,0},{24,8},{1,17},{9,25},{17,1},{25,9},{2,18},{10... | collective-permute-start | bytes 691208 | tf_op jit(solution)/shard_map/ppermute | solution.py:72
  59.4 3.9 %all-to-all-start.2 = ((bf16[4,40,960]{2,1,0:T(8,128)(2,1)}), bf16[4,40,960]{2,1,0:T(8,128)(2,1)S(1)}, u32[]{:S(2)}, u32[]{:S(2)}) async-start(bf16[4,40,960]{2,1,0:T(8,128)(2,1)} %shard_map.83), calls=%async_computation.2 | async-start | bytes 655360 | tf_op jit(solution)/shard_map/all_to_all | solution.py:80
  63.3 2.8 %shard_map.84 = bf16[4,2,320,128]{3,2,1,0:T(8,128)(2,1)} custom-call(bf16[4,2,320,128]{3,2,1,0:T(8,128)(2,1)S(1)} %all-to-all-done.1.act_ref, bf16[320,960]{1,0:T(8,128)(2,1)} %get-tuple-element.72.far_ref), custom_call_target="tpu_custom_call" | custom-call | flops 6291456000 | bytes 19251200 | tf_op jit(solution)/shard_map/pallas_call | solution.py:25
  66.1 5.6 %collective-permute-done.19.refs_1_ = bf16[3,40,960]{2,1,0:T(8,128)(2,1)S(1)} collective-permute-done((bf16[3,40,960]{2,1,0:T(8,128)(2,1)S(1)}, bf16[3,40,960]{2,1,0:T(8,128)(2,1)S(1)}, u32[]{:S(2)}, u32[]{:S(2)}) %collective-permute-start.19) | collective-permute-done | bytes 230432 | tf_op jit(solution)/shard_map/ppermute | solution.py:72
  71.7 1.9 %all-to-all-done.2.temporal_ref = bf16[4,40,960]{2,1,0:T(8,128)(2,1)S(1)} async-done(((bf16[4,40,960]{2,1,0:T(8,128)(2,1)}), bf16[4,40,960]{2,1,0:T(8,128)(2,1)S(1)}, u32[]{:S(2)}, u32[]{:S(2)}) %all-to-all-start.2) | async-done | bytes 307232 | tf_op jit(solution)/shard_map/all_to_all | solution.py:80
  73.8 1.6 %collective-permute-start.21 = (bf16[2,40,960]{2,1,0:T(8,128)(2,1)S(1)}, bf16[2,40,960]{2,1,0:T(8,128)(2,1)S(1)}, u32[]{:S(2)}, u32[]{:S(2)}) collective-permute-start(bf16[2,40,960]{2,1,0:T(8,128)(2,1)S(1)} %get-tuple-element.78), channel_id=1, source_target_pairs={{0,2},{1,3},{2,0},{3,1},{4,6},{5,7},{6,4},{7,5},{8,10},{9,11},{10,... | collective-permute-start | bytes 460808 | tf_op jit(solution)/shard_map/ppermute | solution.py:72
  75.4 3.7 %all-to-all-start.3 = ((bf16[4,2,320,128]{3,2,1,0:T(8,128)(2,1)}), bf16[4,2,320,128]{3,2,1,0:T(8,128)(2,1)S(1)}, u32[]{:S(2)}, u32[]{:S(2)}) async-start(bf16[4,2,320,128]{3,2,1,0:T(8,128)(2,1)} %shard_map.84), calls=%async_computation.3 | async-start | bytes 1310720 | tf_op jit(solution)/shard_map/all_to_all | solution.py:80
  79.1 0.9 collective-permute-done.21.other_ref
  80.1 2.7 %collective-permute-start.22 = (bf16[2,40,960]{2,1,0:T(8,128)(2,1)S(1)}, bf16[2,40,960]{2,1,0:T(8,128)(2,1)S(1)}, u32[]{:S(2)}, u32[]{:S(2)}) collective-permute-start(bf16[2,40,960]{2,1,0:T(8,128)(2,1)S(1)} %shard_map.86.keep_ref), channel_id=1, source_target_pairs={{0,4},{1,5},{2,6},{3,7},{4,0},{5,1},{6,2},{7,3},{8,12},{9,13},{10,... | collective-permute-start | bytes 460808 | tf_op jit(solution)/shard_map/ppermute | solution.py:72
  82.7 7.3 %shard_map.87 = bf16[8,320,128]{2,1,0:T(8,128)(2,1)} custom-call(bf16[8,320,128]{2,1,0:T(8,128)(2,1)} %get-tuple-element.80.far_pg, bf16[8,320,128]{2,1,0:T(8,128)(2,1)} %bitcast.12, bf16[3,320,960]{2,1,0:T(8,128)(2,1)} %get-tuple-element.81.far_weights), custom_call_target="tpu_custom_call" | custom-call | flops 18874368000 | bytes 38092800 | tf_op jit(solution)/shard_map/pallas_call | solution.py:25
  90.1 1.6 %collective-permute-start.23 = (bf16[2,40,960]{2,1,0:T(8,128)(2,1)S(1)}, bf16[2,40,960]{2,1,0:T(8,128)(2,1)S(1)}, u32[]{:S(2)}, u32[]{:S(2)}) collective-permute-start(bf16[2,40,960]{2,1,0:T(8,128)(2,1)S(1)} %shard_map.88.own_ref), channel_id=1, source_target_pairs={{0,2},{1,3},{2,0},{3,1},{4,6},{5,7},{6,4},{7,5},{8,10},{9,11},{10,... | collective-permute-start | bytes 460808 | tf_op jit(solution)/shard_map/ppermute | solution.py:72
  91.8 1.0 %shard_map.89 = bf16[8,320,128]{2,1,0:T(8,128)(2,1)} custom-call(bf16[8,320,128]{2,1,0:T(8,128)(2,1)S(1)} %bitcast.10, bf16[8,320,128]{2,1,0:T(8,128)(2,1)S(1)} %bitcast.7), custom_call_target="tpu_custom_call" | custom-call | flops 3276801 | bytes 19660800 | tf_op jit(solution)/shard_map/pallas_call | solution.py:25
  92.7 2.7 %collective-permute-done.23.next_ref = bf16[2,40,960]{2,1,0:T(8,128)(2,1)S(1)} collective-permute-done((bf16[2,40,960]{2,1,0:T(8,128)(2,1)S(1)}, bf16[2,40,960]{2,1,0:T(8,128)(2,1)S(1)}, u32[]{:S(2)}, u32[]{:S(2)}) %collective-permute-start.23) | collective-permute-done | bytes 153632 | tf_op jit(solution)/shard_map/ppermute | solution.py:72
  95.5 1.4 %collective-permute-done.25.both_ref = bf16[2,40,960]{2,1,0:T(8,128)(2,1)S(1)} collective-permute-done((bf16[2,40,960]{2,1,0:T(8,128)(2,1)S(1)}, bf16[2,40,960]{2,1,0:T(8,128)(2,1)S(1)}, u32[]{:S(2)}, u32[]{:S(2)}) %collective-permute-start.25) | collective-permute-done | bytes 153632 | tf_op jit(solution)/shard_map/ppermute | solution.py:72
  96.9 1.4 %shard_map.90 = (f32[9,80,320]{2,1,0:T(8,128)}, f32[3,80,320]{2,1,0:T(8,128)}) custom-call(bf16[2,40,960]{2,1,0:T(8,128)(2,1)S(1)} %shard_map.88.own_ref, bf16[2,40,960]{2,1,0:T(8,128)(2,1)S(1)} %collective-permute-done.23.next_ref, bf16[2,40,960]{2,1,0:T(8,128)(2,1)S(1)} %collective-permute-done.24.core_ref, ...), custom_call_target="tpu_custom_call" | custom-call | flops 6144001 | bytes 18432000 | tf_op jit(solution)/shard_map/pallas_call | solution.py:25
  (69 shorter events, 9.3 us)
Async XLA Ops:
  0.6 10.1 %copy-start = (bf16[1,1,8,320,128]{4,3,2,1,0:T(8,128)(2,1)S(1)}, bf16[1,1,8,320,128]{4,3,2,1,0:T(8,128)(2,1)}, u32[]{:S(2)}) copy-start(bf16[1,1,8,320,128]{4,3,2,1,0:T(8,128)(2,1)} %param.4) | copy-start | bytes 1966084
  1.9 11.2 %collective-permute-start = (bf16[8,320,128]{2,1,0:T(8,128)(2,1)}, bf16[8,320,128]{2,1,0:T(8,128)(2,1)S(1)}, u32[]{:S(2)}, u32[]{:S(2)}) collective-permute-start(bf16[8,320,128]{2,1,0:T(8,128)(2,1)} %bitcast.8), channel_id=1, source_target_pairs={{0,1},{1,0},{2,3},{3,2},{4,5},{5,4},{6,7},{7,6},{8,9},{9,8},{10,11... | collective-permute-start | bytes 1966088 | tf_op jit(solution)/shard_map/ppermute | solution.py:72
  2.4 13.3 %collective-permute-start.3 = (bf16[3,80,320]{2,1,0:T(8,128)(2,1)S(1)}, bf16[3,80,320]{2,1,0:T(8,128)(2,1)S(1)}, u32[]{:S(2)}, u32[]{:S(2)}) collective-permute-start(bf16[3,80,320]{2,1,0:T(8,128)(2,1)S(1)} %get-tuple-element.89), channel_id=1, source_target_pairs={{0,24},{8,16},{16,8},{24,0},{1,25},{9,17},{17,9},{25,1},{2,26},{10... | collective-permute-start | bytes 460808 | tf_op jit(solution)/shard_map/ppermute | solution.py:72
  6.0 9.7 %collective-permute-start.2 = (bf16[3,80,320]{2,1,0:T(8,128)(2,1)S(1)}, bf16[3,80,320]{2,1,0:T(8,128)(2,1)S(1)}, u32[]{:S(2)}, u32[]{:S(2)}) collective-permute-start(bf16[3,80,320]{2,1,0:T(8,128)(2,1)S(1)} %get-tuple-element.89), channel_id=1, source_target_pairs={{0,16},{8,24},{16,0},{24,8},{1,17},{9,25},{17,1},{25,9},{2,18},{10... | collective-permute-start | bytes 460808 | tf_op jit(solution)/shard_map/ppermute | solution.py:72
  6.5 9.4 %collective-permute-start.1 = (bf16[3,80,320]{2,1,0:T(8,128)(2,1)S(1)}, bf16[3,80,320]{2,1,0:T(8,128)(2,1)S(1)}, u32[]{:S(2)}, u32[]{:S(2)}) collective-permute-start(bf16[3,80,320]{2,1,0:T(8,128)(2,1)S(1)} %get-tuple-element.89), channel_id=1, source_target_pairs={{0,8},{8,0},{16,24},{24,16},{1,9},{9,1},{17,25},{25,17},{2,10},{10... | collective-permute-start | bytes 460808 | tf_op jit(solution)/shard_map/ppermute | solution.py:72
  6.6 16.4 %all-to-all-start = ((bf16[4,2,320,128]{3,2,1,0:T(8,128)(2,1)}), bf16[4,2,320,128]{3,2,1,0:T(8,128)(2,1)S(1)}, u32[]{:S(2)}, u32[]{:S(2)}) async-start(bf16[4,2,320,128]{3,2,1,0:T(8,128)(2,1)} %bitcast.11), calls=%async_computation | async-start | bytes 1310720 | tf_op jit(solution)/shard_map/all_to_all | solution.py:80
  15.9 3.9 %collective-permute-start.4 = (bf16[3,80,320]{2,1,0:T(8,128)(2,1)S(1)}, bf16[3,80,320]{2,1,0:T(8,128)(2,1)S(1)}, u32[]{:S(2)}, u32[]{:S(2)}) collective-permute-start(bf16[3,80,320]{2,1,0:T(8,128)(2,1)S(1)} %collective-permute-done.1.refs_2_), channel_id=1, source_target_pairs={{0,1},{1,0},{2,3},{3,2},{4,5},{5,4},{6,7},{7,6},{8,9},{9,8},{10,11... | collective-permute-start | bytes 460808 | tf_op jit(solution)/shard_map/ppermute | solution.py:72
  15.9 4.0 %collective-permute-start.5 = (bf16[3,80,320]{2,1,0:T(8,128)(2,1)S(1)}, bf16[3,80,320]{2,1,0:T(8,128)(2,1)S(1)}, u32[]{:S(2)}, u32[]{:S(2)}) collective-permute-start(bf16[3,80,320]{2,1,0:T(8,128)(2,1)S(1)} %collective-permute-done.2.refs_3_), channel_id=1, source_target_pairs={{0,1},{1,0},{2,3},{3,2},{4,5},{5,4},{6,7},{7,6},{8,9},{9,8},{10,11... | collective-permute-start | bytes 460808 | tf_op jit(solution)/shard_map/ppermute | solution.py:72
  16.4 3.5 %collective-permute-start.6 = (bf16[3,80,320]{2,1,0:T(8,128)(2,1)S(1)}, bf16[3,80,320]{2,1,0:T(8,128)(2,1)S(1)}, u32[]{:S(2)}, u32[]{:S(2)}) collective-permute-start(bf16[3,80,320]{2,1,0:T(8,128)(2,1)S(1)} %collective-permute-done.3.refs_4_), channel_id=1, source_target_pairs={{0,1},{1,0},{2,3},{3,2},{4,5},{5,4},{6,7},{7,6},{8,9},{9,8},{10,11... | collective-permute-start | bytes 460808 | tf_op jit(solution)/shard_map/ppermute | solution.py:72
  16.4 10.1 %collective-permute-start.9 = (bf16[3,80,320]{2,1,0:T(8,128)(2,1)S(1)}, bf16[3,80,320]{2,1,0:T(8,128)(2,1)S(1)}, u32[]{:S(2)}, u32[]{:S(2)}) collective-permute-start(bf16[3,80,320]{2,1,0:T(8,128)(2,1)S(1)} %get-tuple-element.88), channel_id=1, source_target_pairs={{0,24},{8,16},{16,8},{24,0},{1,25},{9,17},{17,9},{25,1},{2,26},{10... | collective-permute-start | bytes 460808 | tf_op jit(solution)/shard_map/ppermute | solution.py:72
  19.3 10.8 %collective-permute-start.8 = (bf16[3,80,320]{2,1,0:T(8,128)(2,1)S(1)}, bf16[3,80,320]{2,1,0:T(8,128)(2,1)S(1)}, u32[]{:S(2)}, u32[]{:S(2)}) collective-permute-start(bf16[3,80,320]{2,1,0:T(8,128)(2,1)S(1)} %get-tuple-element.88), channel_id=1, source_target_pairs={{0,16},{8,24},{16,0},{24,8},{1,17},{9,25},{17,1},{25,9},{2,18},{10... | collective-permute-start | bytes 460808 | tf_op jit(solution)/shard_map/ppermute | solution.py:72
  19.8 10.7 %collective-permute-start.7 = (bf16[3,80,320]{2,1,0:T(8,128)(2,1)S(1)}, bf16[3,80,320]{2,1,0:T(8,128)(2,1)S(1)}, u32[]{:S(2)}, u32[]{:S(2)}) collective-permute-start(bf16[3,80,320]{2,1,0:T(8,128)(2,1)S(1)} %get-tuple-element.88), channel_id=1, source_target_pairs={{0,8},{8,0},{16,24},{24,16},{1,9},{9,1},{17,25},{25,17},{2,10},{10... | collective-permute-start | bytes 460808 | tf_op jit(solution)/shard_map/ppermute | solution.py:72
  30.5 3.5 %collective-permute-start.10 = (bf16[3,80,320]{2,1,0:T(8,128)(2,1)S(1)}, bf16[3,80,320]{2,1,0:T(8,128)(2,1)S(1)}, u32[]{:S(2)}, u32[]{:S(2)}) collective-permute-start(bf16[3,80,320]{2,1,0:T(8,128)(2,1)S(1)} %collective-permute-done.7.refs_3_), channel_id=1, source_target_pairs={{0,1},{1,0},{2,3},{3,2},{4,5},{5,4},{6,7},{7,6},{8,9},{9,8},{10,11... | collective-permute-start | bytes 460808 | tf_op jit(solution)/shard_map/ppermute | solution.py:72
  30.5 4.1 %collective-permute-start.11 = (bf16[3,80,320]{2,1,0:T(8,128)(2,1)S(1)}, bf16[3,80,320]{2,1,0:T(8,128)(2,1)S(1)}, u32[]{:S(2)}, u32[]{:S(2)}) collective-permute-start(bf16[3,80,320]{2,1,0:T(8,128)(2,1)S(1)} %collective-permute-done.8.refs_4_), channel_id=1, source_target_pairs={{0,1},{1,0},{2,3},{3,2},{4,5},{5,4},{6,7},{7,6},{8,9},{9,8},{10,11... | collective-permute-start | bytes 460808 | tf_op jit(solution)/shard_map/ppermute | solution.py:72
  31.0 3.6 %collective-permute-start.12 = (bf16[3,80,320]{2,1,0:T(8,128)(2,1)S(1)}, bf16[3,80,320]{2,1,0:T(8,128)(2,1)S(1)}, u32[]{:S(2)}, u32[]{:S(2)}) collective-permute-start(bf16[3,80,320]{2,1,0:T(8,128)(2,1)S(1)} %collective-permute-done.9.refs_5_), channel_id=1, source_target_pairs={{0,1},{1,0},{2,3},{3,2},{4,5},{5,4},{6,7},{7,6},{8,9},{9,8},{10,11... | collective-permute-start | bytes 460808 | tf_op jit(solution)/shard_map/ppermute | solution.py:72
  31.0 13.8 %collective-permute-start.13 = (bf16[2,320,128]{2,1,0:T(8,128)(2,1)}, bf16[2,320,128]{2,1,0:T(8,128)(2,1)S(1)}, u32[]{:S(2)}, u32[]{:S(2)}) collective-permute-start(bf16[2,320,128]{2,1,0:T(8,128)(2,1)} %get-tuple-element.61), channel_id=1, source_target_pairs={{0,8},{8,0},{16,24},{24,16},{1,9},{9,1},{17,25},{25,17},{2,10},{10... | collective-permute-start | bytes 491528 | tf_op jit(solution)/shard_map/ppermute | solution.py:72
  32.5 12.3 %collective-permute-start.14 = (bf16[2,320,128]{2,1,0:T(8,128)(2,1)}, bf16[2,320,128]{2,1,0:T(8,128)(2,1)S(1)}, u32[]{:S(2)}, u32[]{:S(2)}) collective-permute-start(bf16[2,320,128]{2,1,0:T(8,128)(2,1)} %get-tuple-element.62), channel_id=1, source_target_pairs={{0,16},{8,24},{16,0},{24,8},{1,17},{9,25},{17,1},{25,9},{2,18},{10... | collective-permute-start | bytes 491528 | tf_op jit(solution)/shard_map/ppermute | solution.py:72
  34.0 10.8 %collective-permute-start.15 = (bf16[2,320,128]{2,1,0:T(8,128)(2,1)}, bf16[2,320,128]{2,1,0:T(8,128)(2,1)S(1)}, u32[]{:S(2)}, u32[]{:S(2)}) collective-permute-start(bf16[2,320,128]{2,1,0:T(8,128)(2,1)} %get-tuple-element.63), channel_id=1, source_target_pairs={{0,24},{8,16},{16,8},{24,0},{1,25},{9,17},{17,9},{25,1},{2,26},{10... | collective-permute-start | bytes 491528 | tf_op jit(solution)/shard_map/ppermute | solution.py:72
  35.4 9.4 %copy-start.3 = (bf16[2,320,128]{2,1,0:T(8,128)(2,1)S(1)}, bf16[2,320,128]{2,1,0:T(8,128)(2,1)}, u32[]{:S(2)}) copy-start(bf16[2,320,128]{2,1,0:T(8,128)(2,1)} %get-tuple-element.55.refs_0_) | copy-start | bytes 491524
  41.0 13.0 %all-to-all-start.1 = ((bf16[4,2,320,128]{3,2,1,0:T(8,128)(2,1)}), bf16[4,2,320,128]{3,2,1,0:T(8,128)(2,1)S(1)}, u32[]{:S(2)}, u32[]{:S(2)}) async-start(bf16[4,2,320,128]{3,2,1,0:T(8,128)(2,1)} %bitcast.13), calls=%async_computation.1 | async-start | bytes 1310720 | tf_op jit(solution)/shard_map/all_to_all | solution.py:80
  46.3 1.7 %collective-permute-start.16 = (bf16[160,1024]{1,0:T(8,128)(2,1)S(1)}, bf16[160,1024]{1,0:T(8,128)(2,1)S(1)}, u32[]{:S(2)}, u32[]{:S(2)}) collective-permute-start(bf16[160,1024]{1,0:T(8,128)(2,1)S(1)} %get-tuple-element.65), channel_id=1, source_target_pairs={{0,1},{1,0},{2,3},{3,2},{4,5},{5,4},{6,7},{7,6},{8,9},{9,8},{10,11... | collective-permute-start | bytes 983048 | tf_op jit(solution)/shard_map/ppermute | solution.py:72
  55.0 3.6 %collective-permute-start.17 = (bf16[4,40,960]{2,1,0:T(8,128)(2,1)S(1)}, bf16[4,40,960]{2,1,0:T(8,128)(2,1)S(1)}, u32[]{:S(2)}, u32[]{:S(2)}) collective-permute-start(bf16[4,40,960]{2,1,0:T(8,128)(2,1)S(1)} %get-tuple-element.71), channel_id=1, source_target_pairs={{0,1},{1,0},{2,3},{3,2},{4,5},{5,4},{6,7},{7,6},{8,9},{9,8},{10,11... | collective-permute-start | bytes 921608 | tf_op jit(solution)/shard_map/ppermute | solution.py:72
  55.1 11.0 %collective-permute-start.18 = (bf16[3,40,960]{2,1,0:T(8,128)(2,1)}, bf16[3,40,960]{2,1,0:T(8,128)(2,1)S(1)}, u32[]{:S(2)}, u32[]{:S(2)}) collective-permute-start(bf16[3,40,960]{2,1,0:T(8,128)(2,1)} %get-tuple-element.74), channel_id=1, source_target_pairs={{0,8},{8,0},{16,24},{24,16},{1,9},{9,1},{17,25},{25,17},{2,10},{10... | collective-permute-start | bytes 691208 | tf_op jit(solution)/shard_map/ppermute | solution.py:72
  56.9 14.8 %collective-permute-start.19 = (bf16[3,40,960]{2,1,0:T(8,128)(2,1)S(1)}, bf16[3,40,960]{2,1,0:T(8,128)(2,1)S(1)}, u32[]{:S(2)}, u32[]{:S(2)}) collective-permute-start(bf16[3,40,960]{2,1,0:T(8,128)(2,1)S(1)} %copy-done.5), channel_id=1, source_target_pairs={{0,16},{8,24},{16,0},{24,8},{1,17},{9,25},{17,1},{25,9},{2,18},{10... | collective-permute-start | bytes 691208 | tf_op jit(solution)/shard_map/ppermute | solution.py:72
  58.3 13.4 %collective-permute-start.20 = (bf16[3,40,960]{2,1,0:T(8,128)(2,1)S(1)}, bf16[3,40,960]{2,1,0:T(8,128)(2,1)S(1)}, u32[]{:S(2)}, u32[]{:S(2)}) collective-permute-start(bf16[3,40,960]{2,1,0:T(8,128)(2,1)S(1)} %copy-done.4), channel_id=1, source_target_pairs={{0,24},{8,16},{16,8},{24,0},{1,25},{9,17},{17,9},{25,1},{2,26},{10... | collective-permute-start | bytes 691208 | tf_op jit(solution)/shard_map/ppermute | solution.py:72
  59.4 14.2 %all-to-all-start.2 = ((bf16[4,40,960]{2,1,0:T(8,128)(2,1)}), bf16[4,40,960]{2,1,0:T(8,128)(2,1)S(1)}, u32[]{:S(2)}, u32[]{:S(2)}) async-start(bf16[4,40,960]{2,1,0:T(8,128)(2,1)} %shard_map.83), calls=%async_computation.2 | async-start | bytes 655360 | tf_op jit(solution)/shard_map/all_to_all | solution.py:80
  73.8 6.3 %collective-permute-start.21 = (bf16[2,40,960]{2,1,0:T(8,128)(2,1)S(1)}, bf16[2,40,960]{2,1,0:T(8,128)(2,1)S(1)}, u32[]{:S(2)}, u32[]{:S(2)}) collective-permute-start(bf16[2,40,960]{2,1,0:T(8,128)(2,1)S(1)} %get-tuple-element.78), channel_id=1, source_target_pairs={{0,2},{1,3},{2,0},{3,1},{4,6},{5,7},{6,4},{7,5},{8,10},{9,11},{10,... | collective-permute-start | bytes 460808 | tf_op jit(solution)/shard_map/ppermute | solution.py:72
  75.4 16.3 %all-to-all-start.3 = ((bf16[4,2,320,128]{3,2,1,0:T(8,128)(2,1)}), bf16[4,2,320,128]{3,2,1,0:T(8,128)(2,1)S(1)}, u32[]{:S(2)}, u32[]{:S(2)}) async-start(bf16[4,2,320,128]{3,2,1,0:T(8,128)(2,1)} %shard_map.84), calls=%async_computation.3 | async-start | bytes 1310720 | tf_op jit(solution)/shard_map/all_to_all | solution.py:80
  80.1 10.0 %collective-permute-start.22 = (bf16[2,40,960]{2,1,0:T(8,128)(2,1)S(1)}, bf16[2,40,960]{2,1,0:T(8,128)(2,1)S(1)}, u32[]{:S(2)}, u32[]{:S(2)}) collective-permute-start(bf16[2,40,960]{2,1,0:T(8,128)(2,1)S(1)} %shard_map.86.keep_ref), channel_id=1, source_target_pairs={{0,4},{1,5},{2,6},{3,7},{4,0},{5,1},{6,2},{7,3},{8,12},{9,13},{10,... | collective-permute-start | bytes 460808 | tf_op jit(solution)/shard_map/ppermute | solution.py:72
  90.1 5.4 %collective-permute-start.23 = (bf16[2,40,960]{2,1,0:T(8,128)(2,1)S(1)}, bf16[2,40,960]{2,1,0:T(8,128)(2,1)S(1)}, u32[]{:S(2)}, u32[]{:S(2)}) collective-permute-start(bf16[2,40,960]{2,1,0:T(8,128)(2,1)S(1)} %shard_map.88.own_ref), channel_id=1, source_target_pairs={{0,2},{1,3},{2,0},{3,1},{4,6},{5,7},{6,4},{7,5},{8,10},{9,11},{10,... | collective-permute-start | bytes 460808 | tf_op jit(solution)/shard_map/ppermute | solution.py:72
  91.8 3.7 %collective-permute-start.24 = (bf16[2,40,960]{2,1,0:T(8,128)(2,1)S(1)}, bf16[2,40,960]{2,1,0:T(8,128)(2,1)S(1)}, u32[]{:S(2)}, u32[]{:S(2)}) collective-permute-start(bf16[2,40,960]{2,1,0:T(8,128)(2,1)S(1)} %shard_map.88.own_ref), channel_id=1, source_target_pairs={{0,1},{1,0},{2,3},{3,2},{4,5},{5,4},{6,7},{7,6},{8,9},{9,8},{10,11... | collective-permute-start | bytes 460808 | tf_op jit(solution)/shard_map/ppermute | solution.py:72
  95.5 1.4 %collective-permute-start.25 = (bf16[2,40,960]{2,1,0:T(8,128)(2,1)S(1)}, bf16[2,40,960]{2,1,0:T(8,128)(2,1)S(1)}, u32[]{:S(2)}, u32[]{:S(2)}) collective-permute-start(bf16[2,40,960]{2,1,0:T(8,128)(2,1)S(1)} %collective-permute-done.23.next_ref), channel_id=1, source_target_pairs={{0,1},{1,0},{2,3},{3,2},{4,5},{5,4},{6,7},{7,6},{8,9},{9,8},{10,11... | collective-permute-start | bytes 460808 | tf_op jit(solution)/shard_map/ppermute | solution.py:72
  (10 other events, 44.5 us)

commit v6 on v5

--- a/solution.py
+++ b/solution.py
@@ -473,7 +473,6 @@
         half_grad,
         other_half,
         far=(0, 1),
-        sent=tuple(range(5, 4 + owners)),
         weight=0,
     )
 

time: 98.7 us -> 98.6 us (level)
  no operation moved by 1% of the time
where the time goes in v6:
time: 98.6 us; the launch traced here: 98.1 us
  starting transfers between devices  37.7 us (38%)
  Pallas kernels  36.9 us (37%)
  waiting for transfers between devices  20.6 us (21%)
  other arithmetic  1.3 us (1%)
    pallas_call x16, Pallas kernels, call(): pl.pallas_call(body, out_shape=tuple((pltpu.HBM(out.shape, out.dtype) if...  36.9 us
    ppermute x26, starting transfers between devices, swap(): return lax.ppermute(values, axis, [(i, i ^ bit) for i in range(size)])  22.4 us
    ppermute x26, waiting for transfers between devices, swap(): return lax.ppermute(values, axis, [(i, i ^ bit) for i in range(size)])  17.3 us
    all_to_all x4, starting transfers between devices, exchange(): return lax.all_to_all(blocks, 'seq', 0, 0, tiled=True)  15.3 us
    all_to_all x4, waiting for transfers between devices, exchange(): return lax.all_to_all(blocks, 'seq', 0, 0, tiled=True)  3.3 us
  transfers between devices with their start and end apart: 30, of which 12 were waited for; matrix products, arithmetic and copies ran while one was open for 0% of the time, Pallas kernels for 35%

profile of v6, /device:TPU:0, one launch (start us, length us, event | category | flops | bytes accessed | tf_op | source)
XLA Modules:
  0.0 98.1 jit_solution(1136012682466225846)
XLA Ops:
  0.6 1.3 %slice_select_fusion = (bf16[3,80,320]{2,1,0:T(8,128)(2,1)S(1)}, bf16[3,80,320]{2,1,0:T(8,128)(2,1)S(1)}) fusion(bf16[9,80,320]{2,1,0:T(8,128)(2,1)} %refs_2_.1, pred[]{:T(512)S(6)} %eq.3, bf16[3,80,320]{2,1,0:T(8,128)(2,1)} %refs_0_.1), kind=kLoop, calls=%fused_computation | loop fusion | flops 153600 | bytes 921601 | tf_op jit(solution)/shard_map/jit(_where)/select_n | solution.py:704
  2.4 3.6 %collective-permute-start.3 = (bf16[3,80,320]{2,1,0:T(8,128)(2,1)S(1)}, bf16[3,80,320]{2,1,0:T(8,128)(2,1)S(1)}, u32[]{:S(2)}, u32[]{:S(2)}) collective-permute-start(bf16[3,80,320]{2,1,0:T(8,128)(2,1)S(1)} %get-tuple-element.89), channel_id=1, source_target_pairs={{0,24},{8,16},{16,8},{24,0},{1,25},{9,17},{17,9},{25,1},{2,26},{10... | collective-permute-start | bytes 460808 | tf_op jit(solution)/shard_map/ppermute | solution.py:72
  6.6 4.1 %all-to-all-start = ((bf16[4,2,320,128]{3,2,1,0:T(8,128)(2,1)}), bf16[4,2,320,128]{3,2,1,0:T(8,128)(2,1)S(1)}, u32[]{:S(2)}, u32[]{:S(2)}) async-start(bf16[4,2,320,128]{3,2,1,0:T(8,128)(2,1)} %bitcast.11), calls=%async_computation | async-start | bytes 1310720 | tf_op jit(solution)/shard_map/all_to_all | solution.py:80
  10.8 2.4 %shard_map.75.refs_0_.far_taps = bf16[960,1280]{1,0:T(8,128)(2,1)} custom-call(bf16[8,320,128]{2,1,0:T(8,128)(2,1)S(1)} %bitcast.9), custom_call_target="tpu_custom_call" | custom-call | flops 3276801 | bytes 31129600 | tf_op jit(solution)/shard_map/pallas_call | solution.py:25
  13.2 2.5 %shard_map.76.far_other = bf16[960,1280]{1,0:T(8,128)(2,1)} custom-call(bf16[8,320,128]{2,1,0:T(8,128)(2,1)S(1)} %collective-permute-done.frames_ref), custom_call_target="tpu_custom_call" | custom-call | flops 3276801 | bytes 31129600 | tf_op jit(solution)/shard_map/pallas_call | solution.py:25
  16.4 2.8 %collective-permute-start.9 = (bf16[3,80,320]{2,1,0:T(8,128)(2,1)S(1)}, bf16[3,80,320]{2,1,0:T(8,128)(2,1)S(1)}, u32[]{:S(2)}, u32[]{:S(2)}) collective-permute-start(bf16[3,80,320]{2,1,0:T(8,128)(2,1)S(1)} %get-tuple-element.88), channel_id=1, source_target_pairs={{0,24},{8,16},{16,8},{24,0},{1,25},{9,17},{17,9},{25,1},{2,26},{10... | collective-permute-start | bytes 460808 | tf_op jit(solution)/shard_map/ppermute | solution.py:72
  20.0 2.1 %shard_map.77 = (bf16[320,960]{1,0:T(8,128)(2,1)}, bf16[320,960]{1,0:T(8,128)(2,1)}, bf16[320,960]{1,0:T(8,128)(2,1)}) custom-call(bf16[3,80,320]{2,1,0:T(8,128)(2,1)S(1)} %copy-done.2, bf16[9,80,320]{2,1,0:T(8,128)(2,1)S(1)} %copy-done.1, bf16[3,80,320]{2,1,0:T(8,128)(2,1)S(1)} %collective-permute-done.1.refs_2_, ...), custom_call_target="tpu_custom_call" | custom-call | flops 1966080000 | bytes 33792000 | tf_op jit(solution)/shard_map/pallas_call | solution.py:25
  23.0 2.7 %shard_map.78 = (bf16[2,320,128]{2,1,0:T(8,128)(2,1)}, bf16[2,320,128]{2,1,0:T(8,128)(2,1)}, bf16[2,320,128]{2,1,0:T(8,128)(2,1)}, bf16[2,320,128]{2,1,0:T(8,128)(2,1)}) custom-call(bf16[4,2,320,128]{3,2,1,0:T(8,128)(2,1)S(1)} %all-to-all-done.cot_ref, bf16[320,960]{1,0:T(8,128)(2,1)} %get-tuple-element.54.far_ref), custom_call_target="tpu_custom_call" | custom-call | flops 6291456000 | bytes 19251200 | tf_op jit(solution)/shard_map/pallas_call | solution.py:25
  26.5 3.6 %collective-permute-done.8.refs_4_ = bf16[3,80,320]{2,1,0:T(8,128)(2,1)S(1)} collective-permute-done((bf16[3,80,320]{2,1,0:T(8,128)(2,1)S(1)}, bf16[3,80,320]{2,1,0:T(8,128)(2,1)S(1)}, u32[]{:S(2)}, u32[]{:S(2)}) %collective-permute-start.8) | collective-permute-done | bytes 153632 | tf_op jit(solution)/shard_map/ppermute | solution.py:72
  31.0 1.5 %collective-permute-start.13 = (bf16[2,320,128]{2,1,0:T(8,128)(2,1)}, bf16[2,320,128]{2,1,0:T(8,128)(2,1)S(1)}, u32[]{:S(2)}, u32[]{:S(2)}) collective-permute-start(bf16[2,320,128]{2,1,0:T(8,128)(2,1)} %get-tuple-element.61), channel_id=1, source_target_pairs={{0,8},{8,0},{16,24},{24,16},{1,9},{9,1},{17,25},{25,17},{2,10},{10... | collective-permute-start | bytes 491528 | tf_op jit(solution)/shard_map/ppermute | solution.py:72
  32.5 1.5 %collective-permute-start.14 = (bf16[2,320,128]{2,1,0:T(8,128)(2,1)}, bf16[2,320,128]{2,1,0:T(8,128)(2,1)S(1)}, u32[]{:S(2)}, u32[]{:S(2)}) collective-permute-start(bf16[2,320,128]{2,1,0:T(8,128)(2,1)} %get-tuple-element.62), channel_id=1, source_target_pairs={{0,16},{8,24},{16,0},{24,8},{1,17},{9,25},{17,1},{25,9},{2,18},{10... | collective-permute-start | bytes 491528 | tf_op jit(solution)/shard_map/ppermute | solution.py:72
  35.3 5.7 %shard_map.79 = (bf16[8,320,128]{2,1,0:T(8,128)(2,1)S(1)}, bf16[8,320,128]{2,1,0:T(8,128)(2,1)}, bf16[3,320,960]{2,1,0:T(8,128)(2,1)}) custom-call(bf16[960,1280]{1,0:T(8,128)(2,1)} %shard_map.75.refs_0_.far_taps, bf16[320,960]{1,0:T(8,128)(2,1)} %get-tuple-element.52.refs_1_, bf16[9,80,320]{2,1,0:T(8,128)(2,1)} %refs_2_.1, bf16[3,80,320]{2,1,0:T(8,128)(2,1)} %copy-done.6, ...), custom_call_target="tpu_custom_call" | custom-call | flops 18874368000 | bytes 76083200 | tf_op jit(solution)/shard_map/pallas_call | solution.py:25
  41.0 3.7 %all-to-all-start.1 = ((bf16[4,2,320,128]{3,2,1,0:T(8,128)(2,1)}), bf16[4,2,320,128]{3,2,1,0:T(8,128)(2,1)S(1)}, u32[]{:S(2)}, u32[]{:S(2)}) async-start(bf16[4,2,320,128]{3,2,1,0:T(8,128)(2,1)} %bitcast.13), calls=%async_computation.1 | async-start | bytes 1310720 | tf_op jit(solution)/shard_map/all_to_all | solution.py:80
  44.8 1.5 %shard_map.80 = (bf16[160,1024]{1,0:T(8,128)(2,1)S(1)}, bf16[160,1024]{1,0:T(8,128)(2,1)S(1)}, bf16[8,320,128]{2,1,0:T(8,128)(2,1)}) custom-call(bf16[8,320,128]{2,1,0:T(8,128)(2,1)S(1)} %get-tuple-element.60.pre_ref, bf16[2,320,128]{2,1,0:T(8,128)(2,1)S(1)} %copy-done.3, bf16[2,320,128]{2,1,0:T(8,128)(2,1)S(1)} %collective-permute-done.13.refs_1_, ...), custom_call_target="tpu_custom_call" | custom-call | flops 65536000 | bytes 26214400 | tf_op jit(solution)/shard_map/pallas_call | solution.py:25
  46.4 1.6 %collective-permute-done.16.theirs_ref = bf16[160,1024]{1,0:T(8,128)(2,1)S(1)} collective-permute-done((bf16[160,1024]{1,0:T(8,128)(2,1)S(1)}, bf16[160,1024]{1,0:T(8,128)(2,1)S(1)}, u32[]{:S(2)}, u32[]{:S(2)}) %collective-permute-start.16) | collective-permute-done | bytes 327712 | tf_op jit(solution)/shard_map/ppermute | solution.py:72
  48.0 5.5 %shard_map.81 = (f32[3,40,960]{2,1,0:T(8,128)S(1)}, bf16[3,40,960]{2,1,0:T(8,128)(2,1)}, bf16[3,40,960]{2,1,0:T(8,128)(2,1)S(1)}, bf16[3,40,960]{2,1,0:T(8,128)(2,1)S(1)}) custom-call(bf16[960,1280]{1,0:T(8,128)(2,1)} %shard_map.75.refs_0_.far_taps, bf16[960,1280]{1,0:T(8,128)(2,1)} %shard_map.76.far_other, ...), custom_call_target="tpu_custom_call" | custom-call | flops 1 | bytes 1 | tf_op jit(solution)/shard_map/pallas_call | solution.py:25
  55.1 1.7 %collective-permute-start.18 = (bf16[3,40,960]{2,1,0:T(8,128)(2,1)}, bf16[3,40,960]{2,1,0:T(8,128)(2,1)S(1)}, u32[]{:S(2)}, u32[]{:S(2)}) collective-permute-start(bf16[3,40,960]{2,1,0:T(8,128)(2,1)} %get-tuple-element.74), channel_id=1, source_target_pairs={{0,8},{8,0},{16,24},{24,16},{1,9},{9,1},{17,25},{25,17},{2,10},{10... | collective-permute-start | bytes 691208 | tf_op jit(solution)/shard_map/ppermute | solution.py:72
  56.7 1.5 %collective-permute-start.19 = (bf16[3,40,960]{2,1,0:T(8,128)(2,1)S(1)}, bf16[3,40,960]{2,1,0:T(8,128)(2,1)S(1)}, u32[]{:S(2)}, u32[]{:S(2)}) collective-permute-start(bf16[3,40,960]{2,1,0:T(8,128)(2,1)S(1)} %get-tuple-element.75), channel_id=1, source_target_pairs={{0,16},{8,24},{16,0},{24,8},{1,17},{9,25},{17,1},{25,9},{2,18},{10... | collective-permute-start | bytes 691208 | tf_op jit(solution)/shard_map/ppermute | solution.py:72
  59.4 3.8 %all-to-all-start.2 = ((bf16[4,40,960]{2,1,0:T(8,128)(2,1)}), bf16[4,40,960]{2,1,0:T(8,128)(2,1)S(1)}, u32[]{:S(2)}, u32[]{:S(2)}) async-start(bf16[4,40,960]{2,1,0:T(8,128)(2,1)} %shard_map.83), calls=%async_computation.2 | async-start | bytes 655360 | tf_op jit(solution)/shard_map/all_to_all | solution.py:80
  63.2 2.8 %shard_map.84 = bf16[4,2,320,128]{3,2,1,0:T(8,128)(2,1)} custom-call(bf16[4,2,320,128]{3,2,1,0:T(8,128)(2,1)S(1)} %all-to-all-done.1.act_ref, bf16[320,960]{1,0:T(8,128)(2,1)} %get-tuple-element.72.far_ref), custom_call_target="tpu_custom_call" | custom-call | flops 6291456000 | bytes 19251200 | tf_op jit(solution)/shard_map/pallas_call | solution.py:25
  66.0 5.6 %collective-permute-done.19.refs_1_ = bf16[3,40,960]{2,1,0:T(8,128)(2,1)S(1)} collective-permute-done((bf16[3,40,960]{2,1,0:T(8,128)(2,1)S(1)}, bf16[3,40,960]{2,1,0:T(8,128)(2,1)S(1)}, u32[]{:S(2)}, u32[]{:S(2)}) %collective-permute-start.19) | collective-permute-done | bytes 230432 | tf_op jit(solution)/shard_map/ppermute | solution.py:72
  71.6 1.9 %all-to-all-done.2.temporal_ref = bf16[4,40,960]{2,1,0:T(8,128)(2,1)S(1)} async-done(((bf16[4,40,960]{2,1,0:T(8,128)(2,1)}), bf16[4,40,960]{2,1,0:T(8,128)(2,1)S(1)}, u32[]{:S(2)}, u32[]{:S(2)}) %all-to-all-start.2) | async-done | bytes 307232 | tf_op jit(solution)/shard_map/all_to_all | solution.py:80
  73.7 1.6 %collective-permute-start.21 = (bf16[2,40,960]{2,1,0:T(8,128)(2,1)S(1)}, bf16[2,40,960]{2,1,0:T(8,128)(2,1)S(1)}, u32[]{:S(2)}, u32[]{:S(2)}) collective-permute-start(bf16[2,40,960]{2,1,0:T(8,128)(2,1)S(1)} %get-tuple-element.78), channel_id=1, source_target_pairs={{0,2},{1,3},{2,0},{3,1},{4,6},{5,7},{6,4},{7,5},{8,10},{9,11},{10,... | collective-permute-start | bytes 460808 | tf_op jit(solution)/shard_map/ppermute | solution.py:72
  75.3 3.7 %all-to-all-start.3 = ((bf16[4,2,320,128]{3,2,1,0:T(8,128)(2,1)}), bf16[4,2,320,128]{3,2,1,0:T(8,128)(2,1)S(1)}, u32[]{:S(2)}, u32[]{:S(2)}) async-start(bf16[4,2,320,128]{3,2,1,0:T(8,128)(2,1)} %shard_map.84), calls=%async_computation.3 | async-start | bytes 1310720 | tf_op jit(solution)/shard_map/all_to_all | solution.py:80
  79.0 0.9 collective-permute-done.21.other_ref
  80.0 2.7 %collective-permute-start.22 = (bf16[2,40,960]{2,1,0:T(8,128)(2,1)S(1)}, bf16[2,40,960]{2,1,0:T(8,128)(2,1)S(1)}, u32[]{:S(2)}, u32[]{:S(2)}) collective-permute-start(bf16[2,40,960]{2,1,0:T(8,128)(2,1)S(1)} %shard_map.86.keep_ref), channel_id=1, source_target_pairs={{0,4},{1,5},{2,6},{3,7},{4,0},{5,1},{6,2},{7,3},{8,12},{9,13},{10,... | collective-permute-start | bytes 460808 | tf_op jit(solution)/shard_map/ppermute | solution.py:72
  82.6 7.3 %shard_map.87 = bf16[8,320,128]{2,1,0:T(8,128)(2,1)} custom-call(bf16[8,320,128]{2,1,0:T(8,128)(2,1)} %get-tuple-element.80.far_pg, bf16[8,320,128]{2,1,0:T(8,128)(2,1)} %bitcast.12, bf16[3,320,960]{2,1,0:T(8,128)(2,1)} %get-tuple-element.81.far_weights), custom_call_target="tpu_custom_call" | custom-call | flops 18874368000 | bytes 38092800 | tf_op jit(solution)/shard_map/pallas_call | solution.py:25
  90.0 1.6 %collective-permute-start.23 = (bf16[2,40,960]{2,1,0:T(8,128)(2,1)S(1)}, bf16[2,40,960]{2,1,0:T(8,128)(2,1)S(1)}, u32[]{:S(2)}, u32[]{:S(2)}) collective-permute-start(bf16[2,40,960]{2,1,0:T(8,128)(2,1)S(1)} %shard_map.88.own_ref), channel_id=1, source_target_pairs={{0,2},{1,3},{2,0},{3,1},{4,6},{5,7},{6,4},{7,5},{8,10},{9,11},{10,... | collective-permute-start | bytes 460808 | tf_op jit(solution)/shard_map/ppermute | solution.py:72
  91.6 1.0 %shard_map.89 = bf16[8,320,128]{2,1,0:T(8,128)(2,1)} custom-call(bf16[8,320,128]{2,1,0:T(8,128)(2,1)S(1)} %bitcast.10, bf16[8,320,128]{2,1,0:T(8,128)(2,1)S(1)} %bitcast.7), custom_call_target="tpu_custom_call" | custom-call | flops 3276801 | bytes 19660800 | tf_op jit(solution)/shard_map/pallas_call | solution.py:25
  92.6 2.8 %collective-permute-done.23.next_ref = bf16[2,40,960]{2,1,0:T(8,128)(2,1)S(1)} collective-permute-done((bf16[2,40,960]{2,1,0:T(8,128)(2,1)S(1)}, bf16[2,40,960]{2,1,0:T(8,128)(2,1)S(1)}, u32[]{:S(2)}, u32[]{:S(2)}) %collective-permute-start.23) | collective-permute-done | bytes 153632 | tf_op jit(solution)/shard_map/ppermute | solution.py:72
  95.4 1.4 %collective-permute-done.25.both_ref = bf16[2,40,960]{2,1,0:T(8,128)(2,1)S(1)} collective-permute-done((bf16[2,40,960]{2,1,0:T(8,128)(2,1)S(1)}, bf16[2,40,960]{2,1,0:T(8,128)(2,1)S(1)}, u32[]{:S(2)}, u32[]{:S(2)}) %collective-permute-start.25) | collective-permute-done | bytes 153632 | tf_op jit(solution)/shard_map/ppermute | solution.py:72
  96.8 1.4 %shard_map.90 = (f32[9,80,320]{2,1,0:T(8,128)}, f32[3,80,320]{2,1,0:T(8,128)}) custom-call(bf16[2,40,960]{2,1,0:T(8,128)(2,1)S(1)} %shard_map.88.own_ref, bf16[2,40,960]{2,1,0:T(8,128)(2,1)S(1)} %collective-permute-done.23.next_ref, bf16[2,40,960]{2,1,0:T(8,128)(2,1)S(1)} %collective-permute-done.24.core_ref, ...), custom_call_target="tpu_custom_call" | custom-call | flops 6144001 | bytes 18432000 | tf_op jit(solution)/shard_map/pallas_call | solution.py:25
  (65 shorter events, 9.5 us)
Async XLA Ops:
  0.6 10.1 %copy-start = (bf16[1,1,8,320,128]{4,3,2,1,0:T(8,128)(2,1)S(1)}, bf16[1,1,8,320,128]{4,3,2,1,0:T(8,128)(2,1)}, u32[]{:S(2)}) copy-start(bf16[1,1,8,320,128]{4,3,2,1,0:T(8,128)(2,1)} %param.4) | copy-start | bytes 1966084
  1.9 11.2 %collective-permute-start = (bf16[8,320,128]{2,1,0:T(8,128)(2,1)}, bf16[8,320,128]{2,1,0:T(8,128)(2,1)S(1)}, u32[]{:S(2)}, u32[]{:S(2)}) collective-permute-start(bf16[8,320,128]{2,1,0:T(8,128)(2,1)} %bitcast.8), channel_id=1, source_target_pairs={{0,1},{1,0},{2,3},{3,2},{4,5},{5,4},{6,7},{7,6},{8,9},{9,8},{10,11... | collective-permute-start | bytes 1966088 | tf_op jit(solution)/shard_map/ppermute | solution.py:72
  2.4 13.3 %collective-permute-start.3 = (bf16[3,80,320]{2,1,0:T(8,128)(2,1)S(1)}, bf16[3,80,320]{2,1,0:T(8,128)(2,1)S(1)}, u32[]{:S(2)}, u32[]{:S(2)}) collective-permute-start(bf16[3,80,320]{2,1,0:T(8,128)(2,1)S(1)} %get-tuple-element.89), channel_id=1, source_target_pairs={{0,24},{8,16},{16,8},{24,0},{1,25},{9,17},{17,9},{25,1},{2,26},{10... | collective-permute-start | bytes 460808 | tf_op jit(solution)/shard_map/ppermute | solution.py:72
  6.0 9.7 %collective-permute-start.2 = (bf16[3,80,320]{2,1,0:T(8,128)(2,1)S(1)}, bf16[3,80,320]{2,1,0:T(8,128)(2,1)S(1)}, u32[]{:S(2)}, u32[]{:S(2)}) collective-permute-start(bf16[3,80,320]{2,1,0:T(8,128)(2,1)S(1)} %get-tuple-element.89), channel_id=1, source_target_pairs={{0,16},{8,24},{16,0},{24,8},{1,17},{9,25},{17,1},{25,9},{2,18},{10... | collective-permute-start | bytes 460808 | tf_op jit(solution)/shard_map/ppermute | solution.py:72
  6.5 9.4 %collective-permute-start.1 = (bf16[3,80,320]{2,1,0:T(8,128)(2,1)S(1)}, bf16[3,80,320]{2,1,0:T(8,128)(2,1)S(1)}, u32[]{:S(2)}, u32[]{:S(2)}) collective-permute-start(bf16[3,80,320]{2,1,0:T(8,128)(2,1)S(1)} %get-tuple-element.89), channel_id=1, source_target_pairs={{0,8},{8,0},{16,24},{24,16},{1,9},{9,1},{17,25},{25,17},{2,10},{10... | collective-permute-start | bytes 460808 | tf_op jit(solution)/shard_map/ppermute | solution.py:72
  6.6 16.4 %all-to-all-start = ((bf16[4,2,320,128]{3,2,1,0:T(8,128)(2,1)}), bf16[4,2,320,128]{3,2,1,0:T(8,128)(2,1)S(1)}, u32[]{:S(2)}, u32[]{:S(2)}) async-start(bf16[4,2,320,128]{3,2,1,0:T(8,128)(2,1)} %bitcast.11), calls=%async_computation | async-start | bytes 1310720 | tf_op jit(solution)/shard_map/all_to_all | solution.py:80
  15.9 3.9 %collective-permute-start.4 = (bf16[3,80,320]{2,1,0:T(8,128)(2,1)S(1)}, bf16[3,80,320]{2,1,0:T(8,128)(2,1)S(1)}, u32[]{:S(2)}, u32[]{:S(2)}) collective-permute-start(bf16[3,80,320]{2,1,0:T(8,128)(2,1)S(1)} %collective-permute-done.1.refs_2_), channel_id=1, source_target_pairs={{0,1},{1,0},{2,3},{3,2},{4,5},{5,4},{6,7},{7,6},{8,9},{9,8},{10,11... | collective-permute-start | bytes 460808 | tf_op jit(solution)/shard_map/ppermute | solution.py:72
  15.9 4.0 %collective-permute-start.5 = (bf16[3,80,320]{2,1,0:T(8,128)(2,1)S(1)}, bf16[3,80,320]{2,1,0:T(8,128)(2,1)S(1)}, u32[]{:S(2)}, u32[]{:S(2)}) collective-permute-start(bf16[3,80,320]{2,1,0:T(8,128)(2,1)S(1)} %collective-permute-done.2.refs_3_), channel_id=1, source_target_pairs={{0,1},{1,0},{2,3},{3,2},{4,5},{5,4},{6,7},{7,6},{8,9},{9,8},{10,11... | collective-permute-start | bytes 460808 | tf_op jit(solution)/shard_map/ppermute | solution.py:72
  16.4 3.5 %collective-permute-start.6 = (bf16[3,80,320]{2,1,0:T(8,128)(2,1)S(1)}, bf16[3,80,320]{2,1,0:T(8,128)(2,1)S(1)}, u32[]{:S(2)}, u32[]{:S(2)}) collective-permute-start(bf16[3,80,320]{2,1,0:T(8,128)(2,1)S(1)} %collective-permute-done.3.refs_4_), channel_id=1, source_target_pairs={{0,1},{1,0},{2,3},{3,2},{4,5},{5,4},{6,7},{7,6},{8,9},{9,8},{10,11... | collective-permute-start | bytes 460808 | tf_op jit(solution)/shard_map/ppermute | solution.py:72
  16.4 10.1 %collective-permute-start.9 = (bf16[3,80,320]{2,1,0:T(8,128)(2,1)S(1)}, bf16[3,80,320]{2,1,0:T(8,128)(2,1)S(1)}, u32[]{:S(2)}, u32[]{:S(2)}) collective-permute-start(bf16[3,80,320]{2,1,0:T(8,128)(2,1)S(1)} %get-tuple-element.88), channel_id=1, source_target_pairs={{0,24},{8,16},{16,8},{24,0},{1,25},{9,17},{17,9},{25,1},{2,26},{10... | collective-permute-start | bytes 460808 | tf_op jit(solution)/shard_map/ppermute | solution.py:72
  19.3 10.8 %collective-permute-start.8 = (bf16[3,80,320]{2,1,0:T(8,128)(2,1)S(1)}, bf16[3,80,320]{2,1,0:T(8,128)(2,1)S(1)}, u32[]{:S(2)}, u32[]{:S(2)}) collective-permute-start(bf16[3,80,320]{2,1,0:T(8,128)(2,1)S(1)} %get-tuple-element.88), channel_id=1, source_target_pairs={{0,16},{8,24},{16,0},{24,8},{1,17},{9,25},{17,1},{25,9},{2,18},{10... | collective-permute-start | bytes 460808 | tf_op jit(solution)/shard_map/ppermute | solution.py:72
  19.8 10.6 %collective-permute-start.7 = (bf16[3,80,320]{2,1,0:T(8,128)(2,1)S(1)}, bf16[3,80,320]{2,1,0:T(8,128)(2,1)S(1)}, u32[]{:S(2)}, u32[]{:S(2)}) collective-permute-start(bf16[3,80,320]{2,1,0:T(8,128)(2,1)S(1)} %get-tuple-element.88), channel_id=1, source_target_pairs={{0,8},{8,0},{16,24},{24,16},{1,9},{9,1},{17,25},{25,17},{2,10},{10... | collective-permute-start | bytes 460808 | tf_op jit(solution)/shard_map/ppermute | solution.py:72
  30.5 3.5 %collective-permute-start.10 = (bf16[3,80,320]{2,1,0:T(8,128)(2,1)S(1)}, bf16[3,80,320]{2,1,0:T(8,128)(2,1)S(1)}, u32[]{:S(2)}, u32[]{:S(2)}) collective-permute-start(bf16[3,80,320]{2,1,0:T(8,128)(2,1)S(1)} %collective-permute-done.7.refs_3_), channel_id=1, source_target_pairs={{0,1},{1,0},{2,3},{3,2},{4,5},{5,4},{6,7},{7,6},{8,9},{9,8},{10,11... | collective-permute-start | bytes 460808 | tf_op jit(solution)/shard_map/ppermute | solution.py:72
  30.5 4.1 %collective-permute-start.11 = (bf16[3,80,320]{2,1,0:T(8,128)(2,1)S(1)}, bf16[3,80,320]{2,1,0:T(8,128)(2,1)S(1)}, u32[]{:S(2)}, u32[]{:S(2)}) collective-permute-start(bf16[3,80,320]{2,1,0:T(8,128)(2,1)S(1)} %collective-permute-done.8.refs_4_), channel_id=1, source_target_pairs={{0,1},{1,0},{2,3},{3,2},{4,5},{5,4},{6,7},{7,6},{8,9},{9,8},{10,11... | collective-permute-start | bytes 460808 | tf_op jit(solution)/shard_map/ppermute | solution.py:72
  31.0 3.6 %collective-permute-start.12 = (bf16[3,80,320]{2,1,0:T(8,128)(2,1)S(1)}, bf16[3,80,320]{2,1,0:T(8,128)(2,1)S(1)}, u32[]{:S(2)}, u32[]{:S(2)}) collective-permute-start(bf16[3,80,320]{2,1,0:T(8,128)(2,1)S(1)} %collective-permute-done.9.refs_5_), channel_id=1, source_target_pairs={{0,1},{1,0},{2,3},{3,2},{4,5},{5,4},{6,7},{7,6},{8,9},{9,8},{10,11... | collective-permute-start | bytes 460808 | tf_op jit(solution)/shard_map/ppermute | solution.py:72
  31.0 13.8 %collective-permute-start.13 = (bf16[2,320,128]{2,1,0:T(8,128)(2,1)}, bf16[2,320,128]{2,1,0:T(8,128)(2,1)S(1)}, u32[]{:S(2)}, u32[]{:S(2)}) collective-permute-start(bf16[2,320,128]{2,1,0:T(8,128)(2,1)} %get-tuple-element.61), channel_id=1, source_target_pairs={{0,8},{8,0},{16,24},{24,16},{1,9},{9,1},{17,25},{25,17},{2,10},{10... | collective-permute-start | bytes 491528 | tf_op jit(solution)/shard_map/ppermute | solution.py:72
  32.5 12.3 %collective-permute-start.14 = (bf16[2,320,128]{2,1,0:T(8,128)(2,1)}, bf16[2,320,128]{2,1,0:T(8,128)(2,1)S(1)}, u32[]{:S(2)}, u32[]{:S(2)}) collective-permute-start(bf16[2,320,128]{2,1,0:T(8,128)(2,1)} %get-tuple-element.62), channel_id=1, source_target_pairs={{0,16},{8,24},{16,0},{24,8},{1,17},{9,25},{17,1},{25,9},{2,18},{10... | collective-permute-start | bytes 491528 | tf_op jit(solution)/shard_map/ppermute | solution.py:72
  34.0 10.8 %collective-permute-start.15 = (bf16[2,320,128]{2,1,0:T(8,128)(2,1)}, bf16[2,320,128]{2,1,0:T(8,128)(2,1)S(1)}, u32[]{:S(2)}, u32[]{:S(2)}) collective-permute-start(bf16[2,320,128]{2,1,0:T(8,128)(2,1)} %get-tuple-element.63), channel_id=1, source_target_pairs={{0,24},{8,16},{16,8},{24,0},{1,25},{9,17},{17,9},{25,1},{2,26},{10... | collective-permute-start | bytes 491528 | tf_op jit(solution)/shard_map/ppermute | solution.py:72
  35.3 9.4 %copy-start.3 = (bf16[2,320,128]{2,1,0:T(8,128)(2,1)S(1)}, bf16[2,320,128]{2,1,0:T(8,128)(2,1)}, u32[]{:S(2)}) copy-start(bf16[2,320,128]{2,1,0:T(8,128)(2,1)} %get-tuple-element.55.refs_0_) | copy-start | bytes 491524
  41.0 13.0 %all-to-all-start.1 = ((bf16[4,2,320,128]{3,2,1,0:T(8,128)(2,1)}), bf16[4,2,320,128]{3,2,1,0:T(8,128)(2,1)S(1)}, u32[]{:S(2)}, u32[]{:S(2)}) async-start(bf16[4,2,320,128]{3,2,1,0:T(8,128)(2,1)} %bitcast.13), calls=%async_computation.1 | async-start | bytes 1310720 | tf_op jit(solution)/shard_map/all_to_all | solution.py:80
  46.3 1.7 %collective-permute-start.16 = (bf16[160,1024]{1,0:T(8,128)(2,1)S(1)}, bf16[160,1024]{1,0:T(8,128)(2,1)S(1)}, u32[]{:S(2)}, u32[]{:S(2)}) collective-permute-start(bf16[160,1024]{1,0:T(8,128)(2,1)S(1)} %get-tuple-element.65), channel_id=1, source_target_pairs={{0,1},{1,0},{2,3},{3,2},{4,5},{5,4},{6,7},{7,6},{8,9},{9,8},{10,11... | collective-permute-start | bytes 983048 | tf_op jit(solution)/shard_map/ppermute | solution.py:72
  55.0 3.6 %collective-permute-start.17 = (bf16[4,40,960]{2,1,0:T(8,128)(2,1)S(1)}, bf16[4,40,960]{2,1,0:T(8,128)(2,1)S(1)}, u32[]{:S(2)}, u32[]{:S(2)}) collective-permute-start(bf16[4,40,960]{2,1,0:T(8,128)(2,1)S(1)} %get-tuple-element.71), channel_id=1, source_target_pairs={{0,1},{1,0},{2,3},{3,2},{4,5},{5,4},{6,7},{7,6},{8,9},{9,8},{10,11... | collective-permute-start | bytes 921608 | tf_op jit(solution)/shard_map/ppermute | solution.py:72
  55.1 10.9 %collective-permute-start.18 = (bf16[3,40,960]{2,1,0:T(8,128)(2,1)}, bf16[3,40,960]{2,1,0:T(8,128)(2,1)S(1)}, u32[]{:S(2)}, u32[]{:S(2)}) collective-permute-start(bf16[3,40,960]{2,1,0:T(8,128)(2,1)} %get-tuple-element.74), channel_id=1, source_target_pairs={{0,8},{8,0},{16,24},{24,16},{1,9},{9,1},{17,25},{25,17},{2,10},{10... | collective-permute-start | bytes 691208 | tf_op jit(solution)/shard_map/ppermute | solution.py:72
  56.7 14.8 %collective-permute-start.19 = (bf16[3,40,960]{2,1,0:T(8,128)(2,1)S(1)}, bf16[3,40,960]{2,1,0:T(8,128)(2,1)S(1)}, u32[]{:S(2)}, u32[]{:S(2)}) collective-permute-start(bf16[3,40,960]{2,1,0:T(8,128)(2,1)S(1)} %get-tuple-element.75), channel_id=1, source_target_pairs={{0,16},{8,24},{16,0},{24,8},{1,17},{9,25},{17,1},{25,9},{2,18},{10... | collective-permute-start | bytes 691208 | tf_op jit(solution)/shard_map/ppermute | solution.py:72
  58.2 13.4 %collective-permute-start.20 = (bf16[3,40,960]{2,1,0:T(8,128)(2,1)S(1)}, bf16[3,40,960]{2,1,0:T(8,128)(2,1)S(1)}, u32[]{:S(2)}, u32[]{:S(2)}) collective-permute-start(bf16[3,40,960]{2,1,0:T(8,128)(2,1)S(1)} %get-tuple-element.76), channel_id=1, source_target_pairs={{0,24},{8,16},{16,8},{24,0},{1,25},{9,17},{17,9},{25,1},{2,26},{10... | collective-permute-start | bytes 691208 | tf_op jit(solution)/shard_map/ppermute | solution.py:72
  59.4 14.0 %all-to-all-start.2 = ((bf16[4,40,960]{2,1,0:T(8,128)(2,1)}), bf16[4,40,960]{2,1,0:T(8,128)(2,1)S(1)}, u32[]{:S(2)}, u32[]{:S(2)}) async-start(bf16[4,40,960]{2,1,0:T(8,128)(2,1)} %shard_map.83), calls=%async_computation.2 | async-start | bytes 655360 | tf_op jit(solution)/shard_map/all_to_all | solution.py:80
  73.7 6.3 %collective-permute-start.21 = (bf16[2,40,960]{2,1,0:T(8,128)(2,1)S(1)}, bf16[2,40,960]{2,1,0:T(8,128)(2,1)S(1)}, u32[]{:S(2)}, u32[]{:S(2)}) collective-permute-start(bf16[2,40,960]{2,1,0:T(8,128)(2,1)S(1)} %get-tuple-element.78), channel_id=1, source_target_pairs={{0,2},{1,3},{2,0},{3,1},{4,6},{5,7},{6,4},{7,5},{8,10},{9,11},{10,... | collective-permute-start | bytes 460808 | tf_op jit(solution)/shard_map/ppermute | solution.py:72
  75.3 16.3 %all-to-all-start.3 = ((bf16[4,2,320,128]{3,2,1,0:T(8,128)(2,1)}), bf16[4,2,320,128]{3,2,1,0:T(8,128)(2,1)S(1)}, u32[]{:S(2)}, u32[]{:S(2)}) async-start(bf16[4,2,320,128]{3,2,1,0:T(8,128)(2,1)} %shard_map.84), calls=%async_computation.3 | async-start | bytes 1310720 | tf_op jit(solution)/shard_map/all_to_all | solution.py:80
  80.0 10.0 %collective-permute-start.22 = (bf16[2,40,960]{2,1,0:T(8,128)(2,1)S(1)}, bf16[2,40,960]{2,1,0:T(8,128)(2,1)S(1)}, u32[]{:S(2)}, u32[]{:S(2)}) collective-permute-start(bf16[2,40,960]{2,1,0:T(8,128)(2,1)S(1)} %shard_map.86.keep_ref), channel_id=1, source_target_pairs={{0,4},{1,5},{2,6},{3,7},{4,0},{5,1},{6,2},{7,3},{8,12},{9,13},{10,... | collective-permute-start | bytes 460808 | tf_op jit(solution)/shard_map/ppermute | solution.py:72
  90.0 5.4 %collective-permute-start.23 = (bf16[2,40,960]{2,1,0:T(8,128)(2,1)S(1)}, bf16[2,40,960]{2,1,0:T(8,128)(2,1)S(1)}, u32[]{:S(2)}, u32[]{:S(2)}) collective-permute-start(bf16[2,40,960]{2,1,0:T(8,128)(2,1)S(1)} %shard_map.88.own_ref), channel_id=1, source_target_pairs={{0,2},{1,3},{2,0},{3,1},{4,6},{5,7},{6,4},{7,5},{8,10},{9,11},{10,... | collective-permute-start | bytes 460808 | tf_op jit(solution)/shard_map/ppermute | solution.py:72
  91.6 3.8 %collective-permute-start.24 = (bf16[2,40,960]{2,1,0:T(8,128)(2,1)S(1)}, bf16[2,40,960]{2,1,0:T(8,128)(2,1)S(1)}, u32[]{:S(2)}, u32[]{:S(2)}) collective-permute-start(bf16[2,40,960]{2,1,0:T(8,128)(2,1)S(1)} %shard_map.88.own_ref), channel_id=1, source_target_pairs={{0,1},{1,0},{2,3},{3,2},{4,5},{5,4},{6,7},{7,6},{8,9},{9,8},{10,11... | collective-permute-start | bytes 460808 | tf_op jit(solution)/shard_map/ppermute | solution.py:72
  95.4 1.4 %collective-permute-start.25 = (bf16[2,40,960]{2,1,0:T(8,128)(2,1)S(1)}, bf16[2,40,960]{2,1,0:T(8,128)(2,1)S(1)}, u32[]{:S(2)}, u32[]{:S(2)}) collective-permute-start(bf16[2,40,960]{2,1,0:T(8,128)(2,1)S(1)} %collective-permute-done.23.next_ref), channel_id=1, source_target_pairs={{0,1},{1,0},{2,3},{3,2},{4,5},{5,4},{6,7},{7,6},{8,9},{9,8},{10,11... | collective-permute-start | bytes 460808 | tf_op jit(solution)/shard_map/ppermute | solution.py:72
  (8 other events, 36.6 us)

commit v7 on v6

--- a/solution.py
+++ b/solution.py
@@ -262,16 +262,8 @@
     tiles = rows // 2
 
     def body(*refs):
-        far_taps, far_middle, far_sources = refs[0], refs[1], refs[2 : 3 + count]
-        pre_ref, far_act, far_weights, taps_ref, act_ref, weights_ref, done = refs[3 + count : -2]
-        own_ref, pieces_ref = refs[-2:]
-        sources = [own_ref] + [pieces_ref.at[i] for i in range(count)]
-        fetched = [
-            pltpu.make_async_copy(far, near, done.at[tiles + 2 + i])
-            for i, (far, near) in enumerate(zip(far_sources, sources))
-        ]
-        for copy in fetched:
-            copy.start()
+        far_taps, far_middle, sources = refs[0], refs[1], refs[2 : 3 + count]
+        pre_ref, far_act, far_weights, taps_ref, act_ref, weights_ref, done = refs[3 + count :]
         middle_load = pltpu.make_async_copy(far_middle, weights_ref.at[1], done.at[tiles + 1])
         middle_load.start()
 
@@ -285,8 +277,6 @@
 
         lax.fori_loop(0, tiles + 1, start, 0)
 
-        for copy in fetched:
-            copy.wait()
         lists = [sources[1 + i * (owners - 1) : 1 + (i + 1) * (owners - 1)] for i in range(2)]
         for side, order in enumerate(((0, 1), (1, 0))):
 
@@ -348,16 +338,14 @@
             pltpu.VMEM(taps.shape, BF),
             pltpu.VMEM((rows, chans, width), BF),
             pltpu.VMEM((3, chans, 3 * chans), BF),
-            pltpu.SemaphoreType.DMA((tiles + 3 + count,)),
-            pltpu.VMEM(own.shape, BF),
-            pltpu.VMEM((count, 3, shard, chans), BF),
+            pltpu.SemaphoreType.DMA((tiles + 2,)),
         ],
         18 * chans * chans * rows * width,
         taps,
         middle,
         own,
         *pieces,
-        far=(*range(3 + count), 4 + count, 5 + count),
+        far=(0, 1, 4 + count, 5 + count),
         weight=10,
     )
 

time: 98.6 us -> 98.9 us (level)
  transfers between devices with their start and end apart: 30 -> 30, of which waited for: 12 -> 11; matrix products, arithmetic and copies ran while one was open for 0% -> 0% of each run, Pallas kernels for 35% -> 35%
where the time goes in v7:
time: 98.9 us; the launch traced here: 98.4 us
  starting transfers between devices  37.9 us (38%)
  Pallas kernels  37.3 us (38%)
  waiting for transfers between devices  20.4 us (21%)
  other arithmetic  1.97 us (2%)
    pallas_call x16, Pallas kernels, call(): pl.pallas_call(body, out_shape=tuple((pltpu.HBM(out.shape, out.dtype) if...  37.3 us
    ppermute x26, starting transfers between devices, swap(): return lax.ppermute(values, axis, [(i, i ^ bit) for i in range(size)])  22.2 us
    ppermute x26, waiting for transfers between devices, swap(): return lax.ppermute(values, axis, [(i, i ^ bit) for i in range(size)])  17.6 us
    all_to_all x4, starting transfers between devices, exchange(): return lax.all_to_all(blocks, 'seq', 0, 0, tiled=True)  15.6 us
    all_to_all x4, waiting for transfers between devices, exchange(): return lax.all_to_all(blocks, 'seq', 0, 0, tiled=True)  2.8 us
  transfers between devices with their start and end apart: 30, of which 11 were waited for; matrix products, arithmetic and copies ran while one was open for 0% of the time, Pallas kernels for 35%

profile of v7, /device:TPU:0, one launch (start us, length us, event | category | flops | bytes accessed | tf_op | source)
XLA Modules:
  0.0 98.4 jit_solution(450196042882962154)
XLA Ops:
  0.6 2.0 %slice_select_fusion = (bf16[3,80,320]{2,1,0:T(8,128)(2,1)S(1)}, bf16[3,80,320]{2,1,0:T(8,128)(2,1)}) fusion(bf16[9,80,320]{2,1,0:T(8,128)(2,1)} %refs_2_.1, pred[]{:T(512)S(6)} %eq.3, bf16[3,80,320]{2,1,0:T(8,128)(2,1)} %refs_0_.1), kind=kLoop, calls=%fused_computation | loop fusion | flops 153600 | bytes 921601 | tf_op jit(solution)/shard_map/jit(_where)/select_n | solution.py:692
  3.0 3.5 %collective-permute-start.3 = (bf16[3,80,320]{2,1,0:T(8,128)(2,1)}, bf16[3,80,320]{2,1,0:T(8,128)(2,1)S(1)}, u32[]{:S(2)}, u32[]{:S(2)}) collective-permute-start(bf16[3,80,320]{2,1,0:T(8,128)(2,1)} %get-tuple-element.89), channel_id=1, source_target_pairs={{0,24},{8,16},{16,8},{24,0},{1,25},{9,17},{17,9},{25,1},{2,26},{10... | collective-permute-start | bytes 460808 | tf_op jit(solution)/shard_map/ppermute | solution.py:72
  7.1 4.1 %all-to-all-start = ((bf16[4,2,320,128]{3,2,1,0:T(8,128)(2,1)}), bf16[4,2,320,128]{3,2,1,0:T(8,128)(2,1)S(1)}, u32[]{:S(2)}, u32[]{:S(2)}) async-start(bf16[4,2,320,128]{3,2,1,0:T(8,128)(2,1)} %bitcast.11), calls=%async_computation | async-start | bytes 1310720 | tf_op jit(solution)/shard_map/all_to_all | solution.py:80
  11.3 2.4 %shard_map.75.refs_0_.far_taps = bf16[960,1280]{1,0:T(8,128)(2,1)} custom-call(bf16[8,320,128]{2,1,0:T(8,128)(2,1)S(1)} %bitcast.9), custom_call_target="tpu_custom_call" | custom-call | flops 3276801 | bytes 31129600 | tf_op jit(solution)/shard_map/pallas_call | solution.py:25
  13.7 2.5 %shard_map.76.far_other = bf16[960,1280]{1,0:T(8,128)(2,1)} custom-call(bf16[8,320,128]{2,1,0:T(8,128)(2,1)S(1)} %collective-permute-done.frames_ref), custom_call_target="tpu_custom_call" | custom-call | flops 3276801 | bytes 31129600 | tf_op jit(solution)/shard_map/pallas_call | solution.py:25
  17.2 2.6 %collective-permute-start.9 = (bf16[3,80,320]{2,1,0:T(8,128)(2,1)S(1)}, bf16[3,80,320]{2,1,0:T(8,128)(2,1)S(1)}, u32[]{:S(2)}, u32[]{:S(2)}) collective-permute-start(bf16[3,80,320]{2,1,0:T(8,128)(2,1)S(1)} %get-tuple-element.88), channel_id=1, source_target_pairs={{0,24},{8,16},{16,8},{24,0},{1,25},{9,17},{17,9},{25,1},{2,26},{10... | collective-permute-start | bytes 460808 | tf_op jit(solution)/shard_map/ppermute | solution.py:72
  20.7 2.1 %shard_map.77 = (bf16[320,960]{1,0:T(8,128)(2,1)}, bf16[320,960]{1,0:T(8,128)(2,1)}, bf16[320,960]{1,0:T(8,128)(2,1)}) custom-call(bf16[3,80,320]{2,1,0:T(8,128)(2,1)S(1)} %copy-done.2, bf16[9,80,320]{2,1,0:T(8,128)(2,1)S(1)} %copy-done.1, bf16[3,80,320]{2,1,0:T(8,128)(2,1)S(1)} %collective-permute-done.1.refs_2_, ...), custom_call_target="tpu_custom_call" | custom-call | flops 1966080000 | bytes 33792000 | tf_op jit(solution)/shard_map/pallas_call | solution.py:25
  23.7 2.7 %shard_map.78 = (bf16[2,320,128]{2,1,0:T(8,128)(2,1)}, bf16[2,320,128]{2,1,0:T(8,128)(2,1)}, bf16[2,320,128]{2,1,0:T(8,128)(2,1)}, bf16[2,320,128]{2,1,0:T(8,128)(2,1)}) custom-call(bf16[4,2,320,128]{3,2,1,0:T(8,128)(2,1)S(1)} %all-to-all-done.cot_ref, bf16[320,960]{1,0:T(8,128)(2,1)} %get-tuple-element.54.far_ref), custom_call_target="tpu_custom_call" | custom-call | flops 6291456000 | bytes 19251200 | tf_op jit(solution)/shard_map/pallas_call | solution.py:25
  27.3 3.6 %collective-permute-done.8.refs_4_ = bf16[3,80,320]{2,1,0:T(8,128)(2,1)S(1)} collective-permute-done((bf16[3,80,320]{2,1,0:T(8,128)(2,1)S(1)}, bf16[3,80,320]{2,1,0:T(8,128)(2,1)S(1)}, u32[]{:S(2)}, u32[]{:S(2)}) %collective-permute-start.8) | collective-permute-done | bytes 153632 | tf_op jit(solution)/shard_map/ppermute | solution.py:72
  31.8 1.4 %collective-permute-start.13 = (bf16[2,320,128]{2,1,0:T(8,128)(2,1)}, bf16[2,320,128]{2,1,0:T(8,128)(2,1)S(1)}, u32[]{:S(2)}, u32[]{:S(2)}) collective-permute-start(bf16[2,320,128]{2,1,0:T(8,128)(2,1)} %get-tuple-element.61), channel_id=1, source_target_pairs={{0,8},{8,0},{16,24},{24,16},{1,9},{9,1},{17,25},{25,17},{2,10},{10... | collective-permute-start | bytes 491528 | tf_op jit(solution)/shard_map/ppermute | solution.py:72
  33.3 1.5 %collective-permute-start.14 = (bf16[2,320,128]{2,1,0:T(8,128)(2,1)}, bf16[2,320,128]{2,1,0:T(8,128)(2,1)}, u32[]{:S(2)}, u32[]{:S(2)}) collective-permute-start(bf16[2,320,128]{2,1,0:T(8,128)(2,1)} %get-tuple-element.62), channel_id=1, source_target_pairs={{0,16},{8,24},{16,0},{24,8},{1,17},{9,25},{17,1},{25,9},{2,18},{10... | collective-permute-start | bytes 491528 | tf_op jit(solution)/shard_map/ppermute | solution.py:72
  35.3 5.1 %shard_map.79 = (bf16[8,320,128]{2,1,0:T(8,128)(2,1)S(1)}, bf16[8,320,128]{2,1,0:T(8,128)(2,1)}, bf16[3,320,960]{2,1,0:T(8,128)(2,1)}) custom-call(bf16[960,1280]{1,0:T(8,128)(2,1)} %shard_map.75.refs_0_.far_taps, bf16[320,960]{1,0:T(8,128)(2,1)} %get-tuple-element.52.refs_1_, bf16[9,80,320]{2,1,0:T(8,128)(2,1)S(1)} %copy-done.1, ...), custom_call_target="tpu_custom_call" | custom-call | flops 18874368000 | bytes 76083200 | tf_op jit(solution)/shard_map/pallas_call | solution.py:25
  40.4 3.6 %all-to-all-start.1 = ((bf16[4,2,320,128]{3,2,1,0:T(8,128)(2,1)}), bf16[4,2,320,128]{3,2,1,0:T(8,128)(2,1)S(1)}, u32[]{:S(2)}, u32[]{:S(2)}) async-start(bf16[4,2,320,128]{3,2,1,0:T(8,128)(2,1)} %bitcast.13), calls=%async_computation.1 | async-start | bytes 1310720 | tf_op jit(solution)/shard_map/all_to_all | solution.py:80
  44.1 2.5 %shard_map.80 = (bf16[160,1024]{1,0:T(8,128)(2,1)S(1)}, bf16[160,1024]{1,0:T(8,128)(2,1)S(1)}, bf16[8,320,128]{2,1,0:T(8,128)(2,1)}) custom-call(bf16[8,320,128]{2,1,0:T(8,128)(2,1)S(1)} %get-tuple-element.60.pre_ref, bf16[2,320,128]{2,1,0:T(8,128)(2,1)S(1)} %copy-done.3, bf16[2,320,128]{2,1,0:T(8,128)(2,1)S(1)} %collective-permute-done.13.refs_1_, ...), custom_call_target="tpu_custom_call" | custom-call | flops 65536000 | bytes 26214400 | tf_op jit(solution)/shard_map/pallas_call | solution.py:25
  46.7 1.6 %collective-permute-done.16.theirs_ref = bf16[160,1024]{1,0:T(8,128)(2,1)S(1)} collective-permute-done((bf16[160,1024]{1,0:T(8,128)(2,1)S(1)}, bf16[160,1024]{1,0:T(8,128)(2,1)S(1)}, u32[]{:S(2)}, u32[]{:S(2)}) %collective-permute-start.16) | collective-permute-done | bytes 327712 | tf_op jit(solution)/shard_map/ppermute | solution.py:72
  48.3 5.5 %shard_map.81 = (f32[3,40,960]{2,1,0:T(8,128)S(1)}, bf16[3,40,960]{2,1,0:T(8,128)(2,1)}, bf16[3,40,960]{2,1,0:T(8,128)(2,1)S(1)}, bf16[3,40,960]{2,1,0:T(8,128)(2,1)S(1)}) custom-call(bf16[960,1280]{1,0:T(8,128)(2,1)} %shard_map.75.refs_0_.far_taps, bf16[960,1280]{1,0:T(8,128)(2,1)} %shard_map.76.far_other, ...), custom_call_target="tpu_custom_call" | custom-call | flops 1 | bytes 1 | tf_op jit(solution)/shard_map/pallas_call | solution.py:25
  55.0 2.0 %collective-permute-start.18 = (bf16[3,40,960]{2,1,0:T(8,128)(2,1)}, bf16[3,40,960]{2,1,0:T(8,128)(2,1)S(1)}, u32[]{:S(2)}, u32[]{:S(2)}) collective-permute-start(bf16[3,40,960]{2,1,0:T(8,128)(2,1)} %get-tuple-element.74), channel_id=1, source_target_pairs={{0,8},{8,0},{16,24},{24,16},{1,9},{9,1},{17,25},{25,17},{2,10},{10... | collective-permute-start | bytes 691208 | tf_op jit(solution)/shard_map/ppermute | solution.py:72
  57.0 1.5 %collective-permute-start.19 = (bf16[3,40,960]{2,1,0:T(8,128)(2,1)S(1)}, bf16[3,40,960]{2,1,0:T(8,128)(2,1)S(1)}, u32[]{:S(2)}, u32[]{:S(2)}) collective-permute-start(bf16[3,40,960]{2,1,0:T(8,128)(2,1)S(1)} %get-tuple-element.75), channel_id=1, source_target_pairs={{0,16},{8,24},{16,0},{24,8},{1,17},{9,25},{17,1},{25,9},{2,18},{10... | collective-permute-start | bytes 691208 | tf_op jit(solution)/shard_map/ppermute | solution.py:72
  59.3 4.2 %all-to-all-start.2 = ((bf16[4,40,960]{2,1,0:T(8,128)(2,1)}), bf16[4,40,960]{2,1,0:T(8,128)(2,1)S(1)}, u32[]{:S(2)}, u32[]{:S(2)}) async-start(bf16[4,40,960]{2,1,0:T(8,128)(2,1)} %shard_map.83), calls=%async_computation.2 | async-start | bytes 655360 | tf_op jit(solution)/shard_map/all_to_all | solution.py:80
  63.5 2.8 %shard_map.84 = bf16[4,2,320,128]{3,2,1,0:T(8,128)(2,1)} custom-call(bf16[4,2,320,128]{3,2,1,0:T(8,128)(2,1)S(1)} %all-to-all-done.1.act_ref, bf16[320,960]{1,0:T(8,128)(2,1)} %get-tuple-element.72.far_ref), custom_call_target="tpu_custom_call" | custom-call | flops 6291456000 | bytes 19251200 | tf_op jit(solution)/shard_map/pallas_call | solution.py:25
  66.3 5.6 %collective-permute-done.19.refs_1_ = bf16[3,40,960]{2,1,0:T(8,128)(2,1)S(1)} collective-permute-done((bf16[3,40,960]{2,1,0:T(8,128)(2,1)S(1)}, bf16[3,40,960]{2,1,0:T(8,128)(2,1)S(1)}, u32[]{:S(2)}, u32[]{:S(2)}) %collective-permute-start.19) | collective-permute-done | bytes 230432 | tf_op jit(solution)/shard_map/ppermute | solution.py:72
  71.9 1.9 %all-to-all-done.2.temporal_ref = bf16[4,40,960]{2,1,0:T(8,128)(2,1)S(1)} async-done(((bf16[4,40,960]{2,1,0:T(8,128)(2,1)}), bf16[4,40,960]{2,1,0:T(8,128)(2,1)S(1)}, u32[]{:S(2)}, u32[]{:S(2)}) %all-to-all-start.2) | async-done | bytes 307232 | tf_op jit(solution)/shard_map/all_to_all | solution.py:80
  74.0 1.6 %collective-permute-start.21 = (bf16[2,40,960]{2,1,0:T(8,128)(2,1)S(1)}, bf16[2,40,960]{2,1,0:T(8,128)(2,1)S(1)}, u32[]{:S(2)}, u32[]{:S(2)}) collective-permute-start(bf16[2,40,960]{2,1,0:T(8,128)(2,1)S(1)} %get-tuple-element.78), channel_id=1, source_target_pairs={{0,2},{1,3},{2,0},{3,1},{4,6},{5,7},{6,4},{7,5},{8,10},{9,11},{10,... | collective-permute-start | bytes 460808 | tf_op jit(solution)/shard_map/ppermute | solution.py:72
  75.6 3.7 %all-to-all-start.3 = ((bf16[4,2,320,128]{3,2,1,0:T(8,128)(2,1)}), bf16[4,2,320,128]{3,2,1,0:T(8,128)(2,1)S(1)}, u32[]{:S(2)}, u32[]{:S(2)}) async-start(bf16[4,2,320,128]{3,2,1,0:T(8,128)(2,1)} %shard_map.84), calls=%async_computation.3 | async-start | bytes 1310720 | tf_op jit(solution)/shard_map/all_to_all | solution.py:80
  79.3 1.0 collective-permute-done.21.other_ref
  80.3 2.6 %collective-permute-start.22 = (bf16[2,40,960]{2,1,0:T(8,128)(2,1)S(1)}, bf16[2,40,960]{2,1,0:T(8,128)(2,1)S(1)}, u32[]{:S(2)}, u32[]{:S(2)}) collective-permute-start(bf16[2,40,960]{2,1,0:T(8,128)(2,1)S(1)} %shard_map.86.keep_ref), channel_id=1, source_target_pairs={{0,4},{1,5},{2,6},{3,7},{4,0},{5,1},{6,2},{7,3},{8,12},{9,13},{10,... | collective-permute-start | bytes 460808 | tf_op jit(solution)/shard_map/ppermute | solution.py:72
  82.9 7.3 %shard_map.87 = bf16[8,320,128]{2,1,0:T(8,128)(2,1)} custom-call(bf16[8,320,128]{2,1,0:T(8,128)(2,1)} %get-tuple-element.80.far_pg, bf16[8,320,128]{2,1,0:T(8,128)(2,1)} %bitcast.12, bf16[3,320,960]{2,1,0:T(8,128)(2,1)} %get-tuple-element.81.far_weights), custom_call_target="tpu_custom_call" | custom-call | flops 18874368000 | bytes 38092800 | tf_op jit(solution)/shard_map/pallas_call | solution.py:25
  90.3 1.6 %collective-permute-start.23 = (bf16[2,40,960]{2,1,0:T(8,128)(2,1)S(1)}, bf16[2,40,960]{2,1,0:T(8,128)(2,1)S(1)}, u32[]{:S(2)}, u32[]{:S(2)}) collective-permute-start(bf16[2,40,960]{2,1,0:T(8,128)(2,1)S(1)} %shard_map.88.own_ref), channel_id=1, source_target_pairs={{0,2},{1,3},{2,0},{3,1},{4,6},{5,7},{6,4},{7,5},{8,10},{9,11},{10,... | collective-permute-start | bytes 460808 | tf_op jit(solution)/shard_map/ppermute | solution.py:72
  91.9 1.0 %shard_map.89 = bf16[8,320,128]{2,1,0:T(8,128)(2,1)} custom-call(bf16[8,320,128]{2,1,0:T(8,128)(2,1)S(1)} %bitcast.10, bf16[8,320,128]{2,1,0:T(8,128)(2,1)S(1)} %bitcast.7), custom_call_target="tpu_custom_call" | custom-call | flops 3276801 | bytes 19660800 | tf_op jit(solution)/shard_map/pallas_call | solution.py:25
  92.9 2.7 %collective-permute-done.23.next_ref = bf16[2,40,960]{2,1,0:T(8,128)(2,1)S(1)} collective-permute-done((bf16[2,40,960]{2,1,0:T(8,128)(2,1)S(1)}, bf16[2,40,960]{2,1,0:T(8,128)(2,1)S(1)}, u32[]{:S(2)}, u32[]{:S(2)}) %collective-permute-start.23) | collective-permute-done | bytes 153632 | tf_op jit(solution)/shard_map/ppermute | solution.py:72
  95.7 1.4 %collective-permute-done.25.both_ref = bf16[2,40,960]{2,1,0:T(8,128)(2,1)S(1)} collective-permute-done((bf16[2,40,960]{2,1,0:T(8,128)(2,1)S(1)}, bf16[2,40,960]{2,1,0:T(8,128)(2,1)S(1)}, u32[]{:S(2)}, u32[]{:S(2)}) %collective-permute-start.25) | collective-permute-done | bytes 153632 | tf_op jit(solution)/shard_map/ppermute | solution.py:72
  97.1 1.4 %shard_map.90 = (f32[9,80,320]{2,1,0:T(8,128)}, f32[3,80,320]{2,1,0:T(8,128)}) custom-call(bf16[2,40,960]{2,1,0:T(8,128)(2,1)S(1)} %shard_map.88.own_ref, bf16[2,40,960]{2,1,0:T(8,128)(2,1)S(1)} %collective-permute-done.23.next_ref, bf16[2,40,960]{2,1,0:T(8,128)(2,1)S(1)} %collective-permute-done.24.core_ref, ...), custom_call_target="tpu_custom_call" | custom-call | flops 6144001 | bytes 18432000 | tf_op jit(solution)/shard_map/pallas_call | solution.py:25
  (53 shorter events, 8.3 us)
Async XLA Ops:
  0.6 10.6 %copy-start = (bf16[1,1,8,320,128]{4,3,2,1,0:T(8,128)(2,1)S(1)}, bf16[1,1,8,320,128]{4,3,2,1,0:T(8,128)(2,1)}, u32[]{:S(2)}) copy-start(bf16[1,1,8,320,128]{4,3,2,1,0:T(8,128)(2,1)} %param.4) | copy-start | bytes 1966084
  2.6 11.1 %collective-permute-start = (bf16[8,320,128]{2,1,0:T(8,128)(2,1)}, bf16[8,320,128]{2,1,0:T(8,128)(2,1)S(1)}, u32[]{:S(2)}, u32[]{:S(2)}) collective-permute-start(bf16[8,320,128]{2,1,0:T(8,128)(2,1)} %bitcast.8), channel_id=1, source_target_pairs={{0,1},{1,0},{2,3},{3,2},{4,5},{5,4},{6,7},{7,6},{8,9},{9,8},{10,11... | collective-permute-start | bytes 1966088 | tf_op jit(solution)/shard_map/ppermute | solution.py:72
  3.0 13.2 %collective-permute-start.3 = (bf16[3,80,320]{2,1,0:T(8,128)(2,1)}, bf16[3,80,320]{2,1,0:T(8,128)(2,1)S(1)}, u32[]{:S(2)}, u32[]{:S(2)}) collective-permute-start(bf16[3,80,320]{2,1,0:T(8,128)(2,1)} %get-tuple-element.89), channel_id=1, source_target_pairs={{0,24},{8,16},{16,8},{24,0},{1,25},{9,17},{17,9},{25,1},{2,26},{10... | collective-permute-start | bytes 460808 | tf_op jit(solution)/shard_map/ppermute | solution.py:72
  6.5 9.7 %collective-permute-start.2 = (bf16[3,80,320]{2,1,0:T(8,128)(2,1)}, bf16[3,80,320]{2,1,0:T(8,128)(2,1)S(1)}, u32[]{:S(2)}, u32[]{:S(2)}) collective-permute-start(bf16[3,80,320]{2,1,0:T(8,128)(2,1)} %get-tuple-element.89), channel_id=1, source_target_pairs={{0,16},{8,24},{16,0},{24,8},{1,17},{9,25},{17,1},{25,9},{2,18},{10... | collective-permute-start | bytes 460808 | tf_op jit(solution)/shard_map/ppermute | solution.py:72
  7.0 9.6 %collective-permute-start.1 = (bf16[3,80,320]{2,1,0:T(8,128)(2,1)}, bf16[3,80,320]{2,1,0:T(8,128)(2,1)S(1)}, u32[]{:S(2)}, u32[]{:S(2)}) collective-permute-start(bf16[3,80,320]{2,1,0:T(8,128)(2,1)} %get-tuple-element.89), channel_id=1, source_target_pairs={{0,8},{8,0},{16,24},{24,16},{1,9},{9,1},{17,25},{25,17},{2,10},{10... | collective-permute-start | bytes 460808 | tf_op jit(solution)/shard_map/ppermute | solution.py:72
  7.1 16.6 %all-to-all-start = ((bf16[4,2,320,128]{3,2,1,0:T(8,128)(2,1)}), bf16[4,2,320,128]{3,2,1,0:T(8,128)(2,1)S(1)}, u32[]{:S(2)}, u32[]{:S(2)}) async-start(bf16[4,2,320,128]{3,2,1,0:T(8,128)(2,1)} %bitcast.11), calls=%async_computation | async-start | bytes 1310720 | tf_op jit(solution)/shard_map/all_to_all | solution.py:80
  11.3 9.4 %copy-start.2 = (bf16[3,80,320]{2,1,0:T(8,128)(2,1)S(1)}, bf16[3,80,320]{2,1,0:T(8,128)(2,1)}, u32[]{:S(2)}) copy-start(bf16[3,80,320]{2,1,0:T(8,128)(2,1)} %refs_0_.1) | copy-start | bytes 460804
  16.7 3.7 %collective-permute-start.4 = (bf16[3,80,320]{2,1,0:T(8,128)(2,1)S(1)}, bf16[3,80,320]{2,1,0:T(8,128)(2,1)S(1)}, u32[]{:S(2)}, u32[]{:S(2)}) collective-permute-start(bf16[3,80,320]{2,1,0:T(8,128)(2,1)S(1)} %collective-permute-done.1.refs_2_), channel_id=1, source_target_pairs={{0,1},{1,0},{2,3},{3,2},{4,5},{5,4},{6,7},{7,6},{8,9},{9,8},{10,11... | collective-permute-start | bytes 460808 | tf_op jit(solution)/shard_map/ppermute | solution.py:72
  16.7 4.0 %collective-permute-start.5 = (bf16[3,80,320]{2,1,0:T(8,128)(2,1)S(1)}, bf16[3,80,320]{2,1,0:T(8,128)(2,1)S(1)}, u32[]{:S(2)}, u32[]{:S(2)}) collective-permute-start(bf16[3,80,320]{2,1,0:T(8,128)(2,1)S(1)} %collective-permute-done.2.refs_3_), channel_id=1, source_target_pairs={{0,1},{1,0},{2,3},{3,2},{4,5},{5,4},{6,7},{7,6},{8,9},{9,8},{10,11... | collective-permute-start | bytes 460808 | tf_op jit(solution)/shard_map/ppermute | solution.py:72
  17.2 3.5 %collective-permute-start.6 = (bf16[3,80,320]{2,1,0:T(8,128)(2,1)S(1)}, bf16[3,80,320]{2,1,0:T(8,128)(2,1)S(1)}, u32[]{:S(2)}, u32[]{:S(2)}) collective-permute-start(bf16[3,80,320]{2,1,0:T(8,128)(2,1)S(1)} %collective-permute-done.3.refs_4_), channel_id=1, source_target_pairs={{0,1},{1,0},{2,3},{3,2},{4,5},{5,4},{6,7},{7,6},{8,9},{9,8},{10,11... | collective-permute-start | bytes 460808 | tf_op jit(solution)/shard_map/ppermute | solution.py:72
  17.2 10.1 %collective-permute-start.9 = (bf16[3,80,320]{2,1,0:T(8,128)(2,1)S(1)}, bf16[3,80,320]{2,1,0:T(8,128)(2,1)S(1)}, u32[]{:S(2)}, u32[]{:S(2)}) collective-permute-start(bf16[3,80,320]{2,1,0:T(8,128)(2,1)S(1)} %get-tuple-element.88), channel_id=1, source_target_pairs={{0,24},{8,16},{16,8},{24,0},{1,25},{9,17},{17,9},{25,1},{2,26},{10... | collective-permute-start | bytes 460808 | tf_op jit(solution)/shard_map/ppermute | solution.py:72
  19.8 11.1 %collective-permute-start.8 = (bf16[3,80,320]{2,1,0:T(8,128)(2,1)S(1)}, bf16[3,80,320]{2,1,0:T(8,128)(2,1)S(1)}, u32[]{:S(2)}, u32[]{:S(2)}) collective-permute-start(bf16[3,80,320]{2,1,0:T(8,128)(2,1)S(1)} %get-tuple-element.88), channel_id=1, source_target_pairs={{0,16},{8,24},{16,0},{24,8},{1,17},{9,25},{17,1},{25,9},{2,18},{10... | collective-permute-start | bytes 460808 | tf_op jit(solution)/shard_map/ppermute | solution.py:72
  20.4 10.9 %collective-permute-start.7 = (bf16[3,80,320]{2,1,0:T(8,128)(2,1)S(1)}, bf16[3,80,320]{2,1,0:T(8,128)(2,1)S(1)}, u32[]{:S(2)}, u32[]{:S(2)}) collective-permute-start(bf16[3,80,320]{2,1,0:T(8,128)(2,1)S(1)} %get-tuple-element.88), channel_id=1, source_target_pairs={{0,8},{8,0},{16,24},{24,16},{1,9},{9,1},{17,25},{25,17},{2,10},{10... | collective-permute-start | bytes 460808 | tf_op jit(solution)/shard_map/ppermute | solution.py:72
  31.3 3.4 %collective-permute-start.10 = (bf16[3,80,320]{2,1,0:T(8,128)(2,1)S(1)}, bf16[3,80,320]{2,1,0:T(8,128)(2,1)S(1)}, u32[]{:S(2)}, u32[]{:S(2)}) collective-permute-start(bf16[3,80,320]{2,1,0:T(8,128)(2,1)S(1)} %collective-permute-done.7.refs_3_), channel_id=1, source_target_pairs={{0,1},{1,0},{2,3},{3,2},{4,5},{5,4},{6,7},{7,6},{8,9},{9,8},{10,11... | collective-permute-start | bytes 460808 | tf_op jit(solution)/shard_map/ppermute | solution.py:72
  31.3 4.0 %collective-permute-start.11 = (bf16[3,80,320]{2,1,0:T(8,128)(2,1)S(1)}, bf16[3,80,320]{2,1,0:T(8,128)(2,1)S(1)}, u32[]{:S(2)}, u32[]{:S(2)}) collective-permute-start(bf16[3,80,320]{2,1,0:T(8,128)(2,1)S(1)} %collective-permute-done.8.refs_4_), channel_id=1, source_target_pairs={{0,1},{1,0},{2,3},{3,2},{4,5},{5,4},{6,7},{7,6},{8,9},{9,8},{10,11... | collective-permute-start | bytes 460808 | tf_op jit(solution)/shard_map/ppermute | solution.py:72
  31.8 3.5 %collective-permute-start.12 = (bf16[3,80,320]{2,1,0:T(8,128)(2,1)S(1)}, bf16[3,80,320]{2,1,0:T(8,128)(2,1)S(1)}, u32[]{:S(2)}, u32[]{:S(2)}) collective-permute-start(bf16[3,80,320]{2,1,0:T(8,128)(2,1)S(1)} %collective-permute-done.9.refs_5_), channel_id=1, source_target_pairs={{0,1},{1,0},{2,3},{3,2},{4,5},{5,4},{6,7},{7,6},{8,9},{9,8},{10,11... | collective-permute-start | bytes 460808 | tf_op jit(solution)/shard_map/ppermute | solution.py:72
  31.8 12.3 %collective-permute-start.13 = (bf16[2,320,128]{2,1,0:T(8,128)(2,1)}, bf16[2,320,128]{2,1,0:T(8,128)(2,1)S(1)}, u32[]{:S(2)}, u32[]{:S(2)}) collective-permute-start(bf16[2,320,128]{2,1,0:T(8,128)(2,1)} %get-tuple-element.61), channel_id=1, source_target_pairs={{0,8},{8,0},{16,24},{24,16},{1,9},{9,1},{17,25},{25,17},{2,10},{10... | collective-permute-start | bytes 491528 | tf_op jit(solution)/shard_map/ppermute | solution.py:72
  33.3 10.8 %collective-permute-start.14 = (bf16[2,320,128]{2,1,0:T(8,128)(2,1)}, bf16[2,320,128]{2,1,0:T(8,128)(2,1)}, u32[]{:S(2)}, u32[]{:S(2)}) collective-permute-start(bf16[2,320,128]{2,1,0:T(8,128)(2,1)} %get-tuple-element.62), channel_id=1, source_target_pairs={{0,16},{8,24},{16,0},{24,8},{1,17},{9,25},{17,1},{25,9},{2,18},{10... | collective-permute-start | bytes 491528 | tf_op jit(solution)/shard_map/ppermute | solution.py:72
  34.7 9.4 %collective-permute-start.15 = (bf16[2,320,128]{2,1,0:T(8,128)(2,1)}, bf16[2,320,128]{2,1,0:T(8,128)(2,1)}, u32[]{:S(2)}, u32[]{:S(2)}) collective-permute-start(bf16[2,320,128]{2,1,0:T(8,128)(2,1)} %get-tuple-element.63), channel_id=1, source_target_pairs={{0,24},{8,16},{16,8},{24,0},{1,25},{9,17},{17,9},{25,1},{2,26},{10... | collective-permute-start | bytes 491528 | tf_op jit(solution)/shard_map/ppermute | solution.py:72
  40.4 13.4 %all-to-all-start.1 = ((bf16[4,2,320,128]{3,2,1,0:T(8,128)(2,1)}), bf16[4,2,320,128]{3,2,1,0:T(8,128)(2,1)S(1)}, u32[]{:S(2)}, u32[]{:S(2)}) async-start(bf16[4,2,320,128]{3,2,1,0:T(8,128)(2,1)} %bitcast.13), calls=%async_computation.1 | async-start | bytes 1310720 | tf_op jit(solution)/shard_map/all_to_all | solution.py:80
  46.6 1.7 %collective-permute-start.16 = (bf16[160,1024]{1,0:T(8,128)(2,1)S(1)}, bf16[160,1024]{1,0:T(8,128)(2,1)S(1)}, u32[]{:S(2)}, u32[]{:S(2)}) collective-permute-start(bf16[160,1024]{1,0:T(8,128)(2,1)S(1)} %get-tuple-element.65), channel_id=1, source_target_pairs={{0,1},{1,0},{2,3},{3,2},{4,5},{5,4},{6,7},{7,6},{8,9},{9,8},{10,11... | collective-permute-start | bytes 983048 | tf_op jit(solution)/shard_map/ppermute | solution.py:72
  54.8 3.7 %collective-permute-start.17 = (bf16[4,40,960]{2,1,0:T(8,128)(2,1)S(1)}, bf16[4,40,960]{2,1,0:T(8,128)(2,1)S(1)}, u32[]{:S(2)}, u32[]{:S(2)}) collective-permute-start(bf16[4,40,960]{2,1,0:T(8,128)(2,1)S(1)} %get-tuple-element.71), channel_id=1, source_target_pairs={{0,1},{1,0},{2,3},{3,2},{4,5},{5,4},{6,7},{7,6},{8,9},{9,8},{10,11... | collective-permute-start | bytes 921608 | tf_op jit(solution)/shard_map/ppermute | solution.py:72
  55.0 11.3 %collective-permute-start.18 = (bf16[3,40,960]{2,1,0:T(8,128)(2,1)}, bf16[3,40,960]{2,1,0:T(8,128)(2,1)S(1)}, u32[]{:S(2)}, u32[]{:S(2)}) collective-permute-start(bf16[3,40,960]{2,1,0:T(8,128)(2,1)} %get-tuple-element.74), channel_id=1, source_target_pairs={{0,8},{8,0},{16,24},{24,16},{1,9},{9,1},{17,25},{25,17},{2,10},{10... | collective-permute-start | bytes 691208 | tf_op jit(solution)/shard_map/ppermute | solution.py:72
  57.0 14.8 %collective-permute-start.19 = (bf16[3,40,960]{2,1,0:T(8,128)(2,1)S(1)}, bf16[3,40,960]{2,1,0:T(8,128)(2,1)S(1)}, u32[]{:S(2)}, u32[]{:S(2)}) collective-permute-start(bf16[3,40,960]{2,1,0:T(8,128)(2,1)S(1)} %get-tuple-element.75), channel_id=1, source_target_pairs={{0,16},{8,24},{16,0},{24,8},{1,17},{9,25},{17,1},{25,9},{2,18},{10... | collective-permute-start | bytes 691208 | tf_op jit(solution)/shard_map/ppermute | solution.py:72
  58.5 13.4 %collective-permute-start.20 = (bf16[3,40,960]{2,1,0:T(8,128)(2,1)S(1)}, bf16[3,40,960]{2,1,0:T(8,128)(2,1)S(1)}, u32[]{:S(2)}, u32[]{:S(2)}) collective-permute-start(bf16[3,40,960]{2,1,0:T(8,128)(2,1)S(1)} %get-tuple-element.76), channel_id=1, source_target_pairs={{0,24},{8,16},{16,8},{24,0},{1,25},{9,17},{17,9},{25,1},{2,26},{10... | collective-permute-start | bytes 691208 | tf_op jit(solution)/shard_map/ppermute | solution.py:72
  59.3 14.5 %all-to-all-start.2 = ((bf16[4,40,960]{2,1,0:T(8,128)(2,1)}), bf16[4,40,960]{2,1,0:T(8,128)(2,1)S(1)}, u32[]{:S(2)}, u32[]{:S(2)}) async-start(bf16[4,40,960]{2,1,0:T(8,128)(2,1)} %shard_map.83), calls=%async_computation.2 | async-start | bytes 655360 | tf_op jit(solution)/shard_map/all_to_all | solution.py:80
  74.0 6.3 %collective-permute-start.21 = (bf16[2,40,960]{2,1,0:T(8,128)(2,1)S(1)}, bf16[2,40,960]{2,1,0:T(8,128)(2,1)S(1)}, u32[]{:S(2)}, u32[]{:S(2)}) collective-permute-start(bf16[2,40,960]{2,1,0:T(8,128)(2,1)S(1)} %get-tuple-element.78), channel_id=1, source_target_pairs={{0,2},{1,3},{2,0},{3,1},{4,6},{5,7},{6,4},{7,5},{8,10},{9,11},{10,... | collective-permute-start | bytes 460808 | tf_op jit(solution)/shard_map/ppermute | solution.py:72
  75.6 16.3 %all-to-all-start.3 = ((bf16[4,2,320,128]{3,2,1,0:T(8,128)(2,1)}), bf16[4,2,320,128]{3,2,1,0:T(8,128)(2,1)S(1)}, u32[]{:S(2)}, u32[]{:S(2)}) async-start(bf16[4,2,320,128]{3,2,1,0:T(8,128)(2,1)} %shard_map.84), calls=%async_computation.3 | async-start | bytes 1310720 | tf_op jit(solution)/shard_map/all_to_all | solution.py:80
  80.3 10.0 %collective-permute-start.22 = (bf16[2,40,960]{2,1,0:T(8,128)(2,1)S(1)}, bf16[2,40,960]{2,1,0:T(8,128)(2,1)S(1)}, u32[]{:S(2)}, u32[]{:S(2)}) collective-permute-start(bf16[2,40,960]{2,1,0:T(8,128)(2,1)S(1)} %shard_map.86.keep_ref), channel_id=1, source_target_pairs={{0,4},{1,5},{2,6},{3,7},{4,0},{5,1},{6,2},{7,3},{8,12},{9,13},{10,... | collective-permute-start | bytes 460808 | tf_op jit(solution)/shard_map/ppermute | solution.py:72
  90.3 5.4 %collective-permute-start.23 = (bf16[2,40,960]{2,1,0:T(8,128)(2,1)S(1)}, bf16[2,40,960]{2,1,0:T(8,128)(2,1)S(1)}, u32[]{:S(2)}, u32[]{:S(2)}) collective-permute-start(bf16[2,40,960]{2,1,0:T(8,128)(2,1)S(1)} %shard_map.88.own_ref), channel_id=1, source_target_pairs={{0,2},{1,3},{2,0},{3,1},{4,6},{5,7},{6,4},{7,5},{8,10},{9,11},{10,... | collective-permute-start | bytes 460808 | tf_op jit(solution)/shard_map/ppermute | solution.py:72
  91.9 3.7 %collective-permute-start.24 = (bf16[2,40,960]{2,1,0:T(8,128)(2,1)S(1)}, bf16[2,40,960]{2,1,0:T(8,128)(2,1)S(1)}, u32[]{:S(2)}, u32[]{:S(2)}) collective-permute-start(bf16[2,40,960]{2,1,0:T(8,128)(2,1)S(1)} %shard_map.88.own_ref), channel_id=1, source_target_pairs={{0,1},{1,0},{2,3},{3,2},{4,5},{5,4},{6,7},{7,6},{8,9},{9,8},{10,11... | collective-permute-start | bytes 460808 | tf_op jit(solution)/shard_map/ppermute | solution.py:72
  95.7 1.4 %collective-permute-start.25 = (bf16[2,40,960]{2,1,0:T(8,128)(2,1)S(1)}, bf16[2,40,960]{2,1,0:T(8,128)(2,1)S(1)}, u32[]{:S(2)}, u32[]{:S(2)}) collective-permute-start(bf16[2,40,960]{2,1,0:T(8,128)(2,1)S(1)} %collective-permute-done.23.next_ref), channel_id=1, source_target_pairs={{0,1},{1,0},{2,3},{3,2},{4,5},{5,4},{6,7},{7,6},{8,9},{9,8},{10,11... | collective-permute-start | bytes 460808 | tf_op jit(solution)/shard_map/ppermute | solution.py:72
  (2 other events, 18.2 us)
